TPU v7x, 256 devices: a whole 4x4x8 slice. The times are simulated.
256 devices in a mesh: tp: 16 (over x, z_lo, core), grp: 16 (over z_hi, y).
Axes of the slice: x: 4, y: 4, z: 8 (z_hi: 4, z_lo: 2; z = z_hi * 2 + z_lo), core: 2. Of those that a mesh axis runs over, the one named last changes fastest.
Arguments:
- queries: bfloat16 [128, 4, 16384], P('grp', None, 'tp')
- new_keys: bfloat16 [128, 4, 1024], P('grp'), may hold values from -6 to 6
- new_values: bfloat16 [128, 4, 1024], P('grp'), may hold values from -6 to 6
- cache_keys: bfloat16 [128, 8, 4096, 128], P('grp', None, 'tp')
- cache_values: bfloat16 [128, 8, 4096, 128], P('grp', None, 'tp'), may hold values from -6 to 6
- lengths: int32 [128], P('grp'), may hold values from 2 to 4092, as said below
- norm_gain: float32 [16384], P('tp'), may hold values from 0.1 to 1.9
- draft_weight: bfloat16 [16384, 16384], P('tp', 'grp'), may hold values from -0.046875 to 0.046875
- next_hidden: bfloat16 [512, 16384], P('tp', 'grp'), may hold values from -6 to 6
Outputs:
- prediction: bfloat16 [512, 16384], P('tp', 'grp')
- weight_grad: bfloat16 [16384, 16384], P('tp', 'grp')
Inputs may be any that keep to these rules, and one draw needn't show every extreme that they name: lengths[r] + 4 <= 4096; some sequence has exactly 4092.
All inputs are finite; a program needn't handle non-finite values.
Results may differ from a plain program's by a relative error of at most 0.024.
Values may be sent and summed in bfloat16 or wider, within the bound.
No kernel may reach another device: no remote copies, remote signals or barrier semaphores. Data moves between devices by JAX's collectives and lax.ppermute only.
A program may use at most 64 MiB of HBM per device.

v0:
```python
import math

import jax
import jax.numpy as jnp
from jax import lax
from jax.sharding import PartitionSpec as P


def per_device(
    queries,
    new_keys,
    new_values,
    cache_keys,
    cache_values,
    lengths,
    norm_gain,
    draft_weight,
    next_hidden,
):
    tp_count = lax.axis_size("tp")
    tp_place = lax.axis_index("tp")
    seqs, steps, _ = queries.shape
    kv_heads, block, head_size = (cache_keys.shape[1], cache_keys.shape[2], cache_keys.shape[3])
    all_queries = lax.all_gather(queries, "tp", axis=2, tiled=True)
    width = all_queries.shape[2]
    q_heads = width // head_size
    groups = q_heads // kv_heads
    heads = all_queries.reshape(seqs, steps, kv_heads, groups, head_size)
    positions = tp_place * block + jnp.arange(block, dtype=jnp.int32)
    slot = positions[None, :] - lengths[:, None]
    onehot = (slot[:, :, None] == jnp.arange(steps, dtype=jnp.int32)[None, None, :]).astype(
        jnp.bfloat16
    )
    written = ((slot >= 0) & (slot < steps))[:, None, :, None]
    put_keys = jnp.einsum(
        "rps,rskd->rkpd",
        onehot,
        new_keys.reshape(seqs, steps, kv_heads, head_size),
        preferred_element_type=jnp.float32,
    ).astype(jnp.bfloat16)
    put_values = jnp.einsum(
        "rps,rskd->rkpd",
        onehot,
        new_values.reshape(seqs, steps, kv_heads, head_size),
        preferred_element_type=jnp.float32,
    ).astype(jnp.bfloat16)
    keys = jnp.where(written, put_keys, cache_keys)
    values = jnp.where(written, put_values, cache_values)
    scores = jnp.einsum("rskgd,rkpd->rskgp", heads, keys, preferred_element_type=jnp.float32) * (
        1.0 / math.sqrt(head_size)
    )
    limit = lengths[:, None] + jnp.arange(steps, dtype=jnp.int32)[None, :] + 1
    valid = (positions[None, None, :] < limit[:, :, None])[:, :, None, None, :]
    masked = jnp.where(valid, scores, jnp.float32(-1e30))
    local_max = jnp.max(masked, axis=-1)
    expo = jnp.where(valid, jnp.exp(masked - local_max[..., None]), jnp.float32(0.0))
    local_total = jnp.sum(expo, axis=-1).reshape(seqs, steps, q_heads)
    local_acc = jnp.einsum(
        "rskgp,rkpd->rskgd", expo.astype(jnp.bfloat16), values, preferred_element_type=jnp.float32
    ).reshape(seqs, steps, q_heads, head_size)
    local_max = local_max.reshape(seqs, steps, q_heads)
    top = lax.pmax(local_max, "tp")
    factor = jnp.exp(local_max - top)
    summed_acc, summed_total = (
        lax.psum_scatter(local_acc * factor[..., None], "tp", scatter_dimension=2, tiled=True),
        lax.psum_scatter(local_total * factor, "tp", scatter_dimension=2, tiled=True),
    )
    context = summed_acc / summed_total[..., None]
    flat = context.reshape(seqs * steps, width // tp_count)
    squares = lax.psum(jnp.sum(flat * flat, axis=1), "tp")
    scale = lax.rsqrt(squares / width + 1e-05)
    rows = (flat * scale[:, None] * norm_gain[None, :]).astype(jnp.bfloat16)
    all_rows = lax.all_gather(rows, "grp", axis=0, tiled=True)
    row_count = all_rows.shape[0]
    total = lax.psum_scatter(
        jnp.dot(all_rows, draft_weight, preferred_element_type=jnp.float32).astype(jnp.bfloat16),
        "tp",
        scatter_dimension=0,
        tiled=True,
    ).astype(jnp.float32)
    grad_mine = ((total - next_hidden.astype(jnp.float32)) / math.sqrt(row_count)).astype(
        jnp.bfloat16
    )
    grad_out = lax.all_gather(grad_mine, "tp", axis=0, tiled=True)
    prediction = total.astype(jnp.bfloat16)
    weight_grad = lax.dot_general(
        all_rows, grad_out, (((0,), (0,)), ((), ())), preferred_element_type=jnp.float32
    )
    return (prediction, weight_grad.astype(jnp.bfloat16))


def solution(mesh):
    in_specs = (
        P("grp", None, "tp"),
        P("grp", None, None),
        P("grp", None, None),
        P("grp", None, "tp", None),
        P("grp", None, "tp", None),
        P("grp"),
        P("tp"),
        P("tp", "grp"),
        P("tp", "grp"),
    )
    out_specs = (P("tp", "grp"), P("tp", "grp"))
    return jax.shard_map(
        per_device, mesh=mesh, in_specs=in_specs, out_specs=out_specs, check_vma=False
    )
```

profile of v0, /device:TPU:1, one launch (start us, length us, event | category | flops | bytes accessed | tf_op | source)
XLA Modules:
  0.0 385.3 jit_solution(17954328044360350698)
XLA Ops:
  7.2 0.7 all-gather.4.cloned.1.call-update
  8.0 0.7 compare_and_fusion
  8.7 0.7 add_add_fusion
  9.4 0.7 broadcast_subtract_fusion
  10.2 0.1 broadcast_compare_fusion
  10.2 38.8 %all-gather.4.cloned.1.call-done = bf16[8,4,16384]{2,1,0:T(4,128)(2,1)} async-done(((bf16[8,4,1024]{2,1,0:T(4,128)(2,1)}), bf16[8,4,16384]{2,1,0:T(4,128)(2,1)}) %all-gather.4.cloned.1.call-update) | async-done | bytes 1048592 | tf_op jit(solution)/shard_map/all_gather | solution.py:24
  49.0 2.1 reshape.125
  51.2 6.7 %fusion.8 = (f32[8,4,8,16]{3,1,2,0:T(4,128)S(1)}, f32[8,8,256,4,16]{2,4,3,1,0:T(8,128)}) fusion(pred[8,4,256]{2,1,0:T(4,128)(4,1)S(1)} %broadcast_compare_fusion, bf16[8,4,8,16,128]{4,3,2,1,0:T(8,128)(2,1)S(1)} %reshape.125, bf16[8,8,256,128]{3,2,1,0:T(8,128)(2,1)} %param.12, pred[8,256]{1,0:T(8,128)(4,1)S(1)} %compare_and_fusion, ...), kind=kOutput, calls=%fused_computation.12 | convolution fusion | flops 292556800 | bytes 9537536 | tf_op jit(solution)/shard_map/rskgd,rkpd->rskgp/dot_general | solution.py:49
  57.9 3.3 fusion.13
  61.3 0.1 reshape.120
  61.4 0.1 reshape.119
  61.5 50.5 %pmax.7 = f32[8,4,128]{2,0,1:T(8,128)S(1)} all-reduce(f32[8,4,128]{2,0,1:T(8,128)S(1)} %reshape.119), channel_id=1, replica_groups=mesh['tp'=16,'grp'=16] {'tp'}, use_global_device_ids=true, to_apply=%region_1.2 | all-reduce | flops 4096 | bytes 32768 | tf_op jit(solution)/shard_map/pmax | solution.py:62
  112.1 6.7 %fusion.21 = f32[8,4,8,16,128]{4,3,1,2,0:T(8,128)} fusion(f32[8,8,256,4,16]{2,4,3,1,0:T(8,128)} %get-tuple-element.7, f32[8,4,8,16]{3,1,2,0:T(4,128)S(1)} %get-tuple-element.6, pred[8,4,256]{2,1,0:T(4,128)(4,1)S(1)} %broadcast_compare_fusion, bf16[8,8,256,128]{3,2,1,0:T(8,128)(2,1)} %param.13, pred[8,256]{1,0:T(8,128)(4,1)S(1)} %compare_and_fusion, ...), kind=kOutput, calls=%fused_computation.24 | convolution fusion | flops 294658048 | bytes 10586112 | tf_op jit(solution)/shard_map/rskgp,rkpd->rskgd/dot_general | solution.py:58
  118.8 1.9 copy.29
  120.7 1.9 bitcast_multiply_fusion
  122.6 0.0 all-gather.6.cloned.1.call-start
  122.7 0.6 dynamic-slice
  123.9 53.0 %all-reduce = f32[8,4,128]{2,0,1:T(8,128)S(1)} all-reduce(f32[8,4,128]{2,0,1:T(8,128)S(1)} %get-tuple-element.4), channel_id=3, replica_groups=mesh['tp'=16,'grp'=16] {'tp'}, use_global_device_ids=true, to_apply=%region_4.5.clone | all-reduce | flops 4096 | bytes 32768
  176.9 0.1 constant_dynamic-slice_fusion
  177.0 11.8 %reduce-scatter.4.cloned.1.call-done = f32[8,4,8,128]{3,2,1,0:T(8,128)} async-done(((f32[8,4,128,128]{3,2,1,0:T(8,128)}), f32[8,4,8,128]{3,2,1,0:T(8,128)}) %reduce-scatter.4.cloned.1.call-update) | async-done | bytes 131088 | tf_op jit(solution)/shard_map/reduce_scatter | solution.py:65
  188.7 1.1 multiply_reduce_fusion
  189.9 0.1 reduce_sum.22
  189.9 30.6 %psum.7 = f32[32]{0:T(128)S(1)} all-reduce(f32[32]{0:T(128)S(1)} %reduce_sum.22), channel_id=1, replica_groups=mesh['tp'=16,'grp'=16] {'tp'}, use_global_device_ids=true, to_apply=%region_6.7 | all-reduce | flops 32 | bytes 256 | tf_op jit(solution)/shard_map/psum | solution.py:70
  220.5 0.7 fusion.28
  221.2 0.0 reduce-scatter.6.cloned.1.call-start
  221.3 51.6 %all-gather.6.cloned.1.call-done = bf16[512,1024]{1,0:T(8,128)(2,1)} async-done(((bf16[32,1024]{1,0:T(8,128)(2,1)}), bf16[512,1024]{1,0:T(8,128)(2,1)}) %all-gather.6.cloned.1.call-update) | async-done | bytes 1048592 | tf_op jit(solution)/shard_map/all_gather | solution.py:73
  272.9 3.5 convolution_convert_fusion.1
  276.5 0.0 all-gather.8.cloned.1.call-start
  276.5 59.4 %reduce-scatter.6.cloned.1.call-done = bf16[32,1024]{1,0:T(8,128)(2,1)} async-done(((bf16[512,1024]{1,0:T(8,128)(2,1)}), bf16[32,1024]{1,0:T(8,128)(2,1)}) %reduce-scatter.6.cloned.1.call-update) | async-done | bytes 65552 | tf_op jit(solution)/shard_map/reduce_scatter | solution.py:75
  336.0 1.5 multiply_convert_fusion
  337.5 37.4 %all-gather.8.cloned.1.call-done = bf16[512,1024]{1,0:T(8,128)(2,1)} async-done(((bf16[32,1024]{1,0:T(8,128)(2,1)}), bf16[512,1024]{1,0:T(8,128)(2,1)}) %all-gather.8.cloned.1.call-update) | async-done | bytes 1048592 | tf_op jit(solution)/shard_map/all_gather | solution.py:84
  374.9 3.8 convolution_convert_fusion
  (25 shorter events, 0.2 us)
Async XLA Ops:
  7.2 265.7 %copy-start = (bf16[1024,1024]{1,0:T(8,128)(2,1)S(1)}, bf16[1024,1024]{1,0:T(8,128)(2,1)}, u32[]{:S(2)}) copy-start(bf16[1024,1024]{1,0:T(8,128)(2,1)} %param.16) | copy-start | bytes 6291460
  7.2 41.9 %all-gather.4.cloned.1.call-start = ((), (), s32[]{:S(2)}) async-start(), calls=%async_computation.2 | async-start | bytes 1114112 | tf_op jit(solution)/shard_map/all_gather | solution.py:24
  7.9 180.8 %reduce-scatter.4.cloned.1.call-start = ((), (), s32[]{:S(2)}) async-start(), calls=%async_computation.3 | async-start | bytes 2228224 | tf_op jit(solution)/shard_map/reduce_scatter | solution.py:65
  57.9 54.2 %copy-start.4 = (bf16[8,4,1024]{2,1,0:T(4,128)(2,1)S(1)}, bf16[8,4,1024]{2,1,0:T(4,128)(2,1)}, u32[]{:S(2)}) copy-start(bf16[8,4,1024]{2,1,0:T(4,128)(2,1)} %param.11) | copy-start | bytes 196612
  120.6 2.0 copy-start.5
  120.6 99.9 %copy-start.2 = (f32[1024]{0:T(1024)S(1)}, f32[1024]{0:T(1024)}, u32[]{:S(2)}) copy-start(f32[1024]{0:T(1024)} %param.15) | copy-start | bytes 12292
  122.6 150.3 %all-gather.6.cloned.1.call-start = ((), (), s32[]{:S(2)}) async-start(), calls=%async_computation.4 | async-start | bytes 1114112 | tf_op jit(solution)/shard_map/all_gather | solution.py:73
  189.8 146.1 %copy-start.1 = (bf16[32,1024]{1,0:T(8,128)(2,1)S(1)}, bf16[32,1024]{1,0:T(8,128)(2,1)}, u32[]{:S(2)}) copy-start(bf16[32,1024]{1,0:T(8,128)(2,1)} %param.17) | copy-start | bytes 196612
  221.2 114.7 %reduce-scatter.6.cloned.1.call-start = ((), (), s32[]{:S(2)}) async-start(), calls=%async_computation.5 | async-start | bytes 1114112 | tf_op jit(solution)/shard_map/reduce_scatter | solution.py:75
  272.9 102.0 %copy-start.3 = (bf16[512,1024]{1,0:T(8,128)(2,1)S(1)}, bf16[512,1024]{1,0:T(8,128)(2,1)}, u32[]{:S(2)}) copy-start(bf16[512,1024]{1,0:T(8,128)(2,1)} %all-gather.6.cloned.1.call-done) | copy-start | bytes 3145732
  276.5 98.4 %all-gather.8.cloned.1.call-start = ((), (), s32[]{:S(2)}) async-start(), calls=%async_computation.6 | async-start | bytes 1114112 | tf_op jit(solution)/shard_map/all_gather | solution.py:84
Sparse Core Ops, SparseCore 0:
  9.8 39.1 all-gather.3
  122.7 65.9 reduce-scatter.3
  221.4 51.4 all-gather.5
  276.6 59.3 reduce-scatter.5
  338.4 36.4 all-gather.7
where the time goes:
time: 386 us; the launch traced here: 385 us
  waiting for transfers between devices  200 us (52%)
  blocking collectives  134 us (35%)
  matrix products  20.8 us (5%)
  between operations  14.6 us (4%)
  other arithmetic  10.8 us (3%)
  local copies, waits for them, and re-layouts  5.01 us (1%)
    reduce_scatter x1, waiting for transfers between devices, per_device(): lax.psum_scatter(jnp.dot(all_rows, draft_weight, preferred_element_type=j...  59.4 us
    unnamed x1, blocking collectives  53 us
    all_gather x1, waiting for transfers between devices, per_device(): all_rows = lax.all_gather(rows, 'grp', axis=0, tiled=True)  51.6 us
    pmax x1, blocking collectives, per_device(): top = lax.pmax(local_max, 'tp')  50.5 us
    all_gather x1, waiting for transfers between devices, per_device(): all_queries = lax.all_gather(queries, 'tp', axis=2, tiled=True)  38.8 us
    all_gather x1, waiting for transfers between devices, per_device(): grad_out = lax.all_gather(grad_mine, 'tp', axis=0, tiled=True)  37.4 us
    psum x1, blocking collectives, per_device(): squares = lax.psum(jnp.sum(flat * flat, axis=1), 'tp')  30.6 us
    reduce_scatter x1, waiting for transfers between devices, per_device(): lax.psum_scatter(local_acc * factor[..., None], 'tp', scatter_dimension=2...  11.8 us
  transfers between devices with their start and end apart: 5, of which 5 were waited for; matrix products, arithmetic and copies ran while one was open for 1% of the time, Pallas kernels for 0%

commit v1 on v0

v1 whole, which is shorter than its diff:
```python
import math

import jax
import jax.numpy as jnp
from jax import lax
from jax.sharding import PartitionSpec as P


def split_pieces(x):
    a = x.astype(jnp.bfloat16)
    r = x - a.astype(jnp.float32)
    b = r.astype(jnp.bfloat16)
    c = (r - b.astype(jnp.float32)).astype(jnp.bfloat16)
    return a, b, c


def gather(x, axis):
    n = lax.axis_size(axis)
    return lax.all_to_all(jnp.broadcast_to(x[None], (n,) + x.shape), axis, 0, 0)


def per_device(
    queries,
    new_keys,
    new_values,
    cache_keys,
    cache_values,
    lengths,
    norm_gain,
    draft_weight,
    next_hidden,
):
    tp_count = lax.axis_size("tp")
    tp_place = lax.axis_index("tp")
    seqs, steps, feats = queries.shape
    kv_heads, block, head_size = (cache_keys.shape[1], cache_keys.shape[2], cache_keys.shape[3])
    mine = feats // head_size
    width = feats * tp_count
    q_heads = width // head_size
    groups = q_heads // kv_heads
    share = tp_count // kv_heads
    packed = queries.reshape(seqs, steps, mine, head_size).transpose(0, 2, 1, 3)
    heads = gather(packed, "tp").reshape(kv_heads, share, seqs, mine * steps, head_size)
    positions = tp_place * block + jnp.arange(block, dtype=jnp.int32)
    slot = positions[None, :] - lengths[:, None]
    onehot = (slot[:, :, None] == jnp.arange(steps, dtype=jnp.int32)[None, None, :]).astype(
        jnp.bfloat16
    )
    written = ((slot >= 0) & (slot < steps))[:, None, :, None]
    put_keys = jnp.einsum(
        "rps,rskd->rkpd",
        onehot,
        new_keys.reshape(seqs, steps, kv_heads, head_size),
        preferred_element_type=jnp.float32,
    ).astype(jnp.bfloat16)
    put_values = jnp.einsum(
        "rps,rskd->rkpd",
        onehot,
        new_values.reshape(seqs, steps, kv_heads, head_size),
        preferred_element_type=jnp.float32,
    ).astype(jnp.bfloat16)
    keys = jnp.where(written, put_keys, cache_keys)
    values = jnp.where(written, put_values, cache_values)
    scores = jnp.einsum("karqd,rkpd->rkaqp", heads, keys, preferred_element_type=jnp.float32) * (
        1.0 / math.sqrt(head_size)
    )
    step_of = jnp.arange(mine * steps, dtype=jnp.int32) % steps
    limit = lengths[:, None] + step_of[None, :] + 1
    valid = (positions[None, None, :] < limit[:, :, None])[:, None, None]
    masked = jnp.where(valid, scores, jnp.float32(-1e30))
    top = jnp.max(masked, axis=-1)
    expo = jnp.where(valid, jnp.exp(masked - top[..., None]), jnp.float32(0.0))
    total_e = jnp.sum(expo, axis=-1)
    some = total_e > 0
    acc = jnp.einsum(
        "rkaqp,rkpd->karqd", expo.astype(jnp.bfloat16), values, preferred_element_type=jnp.float32
    )
    safe = jnp.where(some, total_e, 1.0)
    lse = jnp.where(some, top + jnp.log(safe), jnp.float32(-1e30))
    outs = (acc * (1.0 / safe).transpose(1, 2, 0, 3)[..., None]).astype(jnp.bfloat16)
    outs = outs.reshape(tp_count, seqs * mine * steps, head_size)
    lse = lse.transpose(1, 2, 0, 3).reshape(tp_count, seqs * mine * steps)
    pieces = jnp.stack(split_pieces(lse), axis=1).reshape(tp_count, -1, head_size)
    extra = -pieces.shape[1] % 16
    pieces = jnp.pad(pieces, ((0, 0), (0, extra), (0, 0)))
    got = lax.all_to_all(jnp.concatenate([outs, pieces], axis=1), "tp", 0, 0)
    n_rows = seqs * mine * steps
    got_out = got[:, :n_rows].astype(jnp.float32)
    n_piece = 3 * n_rows // head_size
    got_lse = (
        got[:, n_rows : n_rows + n_piece].astype(jnp.float32).reshape(tp_count, 3, n_rows)
    )
    got_lse = got_lse[:, 0] + got_lse[:, 1] + got_lse[:, 2]
    factor = jnp.exp(got_lse - jnp.max(got_lse, axis=0, keepdims=True))
    context = jnp.sum(got_out * factor[..., None], axis=0) / jnp.sum(factor, axis=0)[:, None]
    flat = (
        context.reshape(seqs, mine, steps, head_size)
        .transpose(0, 2, 1, 3)
        .reshape(seqs * steps, feats)
    )
    raw = (flat * norm_gain[None, :]).astype(jnp.bfloat16)
    all_raw = gather(raw, "grp").reshape(-1, feats)
    row_count = all_raw.shape[0]
    own = row_count // tp_count
    plain = all_raw.astype(jnp.float32) * (1.0 / norm_gain)[None, :]
    squares = jnp.sum(plain * plain, axis=1).reshape(tp_count, own)
    sq = jnp.stack(split_pieces(squares), axis=-1)
    sq = jnp.pad(sq, ((0, 0), (0, 0), (0, 128 - 3)))
    partial = jnp.dot(all_raw, draft_weight, preferred_element_type=jnp.float32).astype(
        jnp.bfloat16
    )
    cols = partial.shape[1]
    payload = jnp.concatenate([partial.reshape(tp_count, own, cols), sq], axis=2)
    parts = lax.all_to_all(payload, "tp", 0, 0).astype(jnp.float32)
    summed = jnp.sum(parts, axis=0)
    meansq = jnp.sum(summed[:, cols : cols + 3], axis=1) / width
    scale = lax.rsqrt(meansq + 1e-05)[:, None]
    total = summed[:, :cols] * scale
    grad_mine = (
        (total - next_hidden.astype(jnp.float32)) * (scale / math.sqrt(row_count))
    ).astype(jnp.bfloat16)
    grad_out = gather(grad_mine, "tp").reshape(row_count, cols)
    prediction = total.astype(jnp.bfloat16)
    weight_grad = lax.dot_general(
        all_raw, grad_out, (((0,), (0,)), ((), ())), preferred_element_type=jnp.float32
    )
    return (prediction, weight_grad.astype(jnp.bfloat16))


def solution(mesh):
    in_specs = (
        P("grp", None, "tp"),
        P("grp", None, None),
        P("grp", None, None),
        P("grp", None, "tp", None),
        P("grp", None, "tp", None),
        P("grp"),
        P("tp"),
        P("tp", "grp"),
        P("tp", "grp"),
    )
    out_specs = (P("tp", "grp"), P("tp", "grp"))
    return jax.shard_map(
        per_device, mesh=mesh, in_specs=in_specs, out_specs=out_specs, check_vma=False
    )
```

time: 386 us -> 151 us (0.39)
  waiting for transfers between devices: 200 us -> 38.3 us
  blocking collectives: 134 us -> 61.4 us
  starting transfers between devices: 0.2 us -> 17.2 us
  between operations: 14.6 us -> 0.91 us
    all_gather x3 -> x0, waiting for transfers between devices: 128 us -> none  [the longest x1 51.6 us: per_device(): all_rows = lax.all_gather(rows, 'grp', axis=0, tiled=True)]
    reduce_scatter x2 -> x0, waiting for transfers between devices: 71.2 us -> none  [the longest x1 59.4 us: per_device(): lax.psum_scatter(jnp.dot(all_rows, draft_weight, preferred_element_type=j...]
    all_to_all x0 -> x3, blocking collectives: none -> 61.4 us  [the longest x1 22.5 us: per_device(): parts = lax.all_to_all(payload, 'tp', 0, 0).astype(jnp.float32)]
    unnamed x1 -> x0, blocking collectives: 53 us -> none
    pmax x1 -> x0, blocking collectives: 50.5 us -> none  [per_device(): top = lax.pmax(local_max, 'tp')]
    all_to_all x0 -> x2, waiting for transfers between devices: none -> 38.3 us  [gather(): return lax.all_to_all(jnp.broadcast_to(x[None], (n,) + x.shape), axis, 0, 0)]
    psum x1 -> x0, blocking collectives: 30.6 us -> none  [per_device(): squares = lax.psum(jnp.sum(flat * flat, axis=1), 'tp')]
    all_to_all x0 -> x2, starting transfers between devices: none -> 17.2 us  [gather(): return lax.all_to_all(jnp.broadcast_to(x[None], (n,) + x.shape), axis, 0, 0)]
  transfers between devices with their start and end apart: 5 -> 2, of which waited for: 5 -> 2; matrix products, arithmetic and copies ran while one was open for 1% -> 3% of each run, Pallas kernels for 0% -> 0%
where the time goes in v1:
time: 151 us
  blocking collectives  61.4 us (41%)
  waiting for transfers between devices  38.3 us (25%)
  matrix products  20.4 us (14%)
  starting transfers between devices  17.2 us (11%)
  other arithmetic  7.05 us (5%)
  local copies, waits for them, and re-layouts  5.69 us (4%)
    all_to_all x2, waiting for transfers between devices, gather(): return lax.all_to_all(jnp.broadcast_to(x[None], (n,) + x.shape), axis, 0, 0)  38.3 us
    all_to_all x1, blocking collectives, per_device(): parts = lax.all_to_all(payload, 'tp', 0, 0).astype(jnp.float32)  22.5 us
    all_to_all x1, blocking collectives, per_device(): got = lax.all_to_all(jnp.concatenate([outs, pieces], axis=1), 'tp', 0, 0)  20.2 us
    all_to_all x1, blocking collectives, gather(): return lax.all_to_all(jnp.broadcast_to(x[None], (n,) + x.shape), axis, 0, 0)  18.6 us
    all_to_all x2, starting transfers between devices, gather(): return lax.all_to_all(jnp.broadcast_to(x[None], (n,) + x.shape), axis, 0, 0)  17.2 us
    dot_general x1, matrix products, per_device(): jnp.einsum('karqd,rkpd->rkaqp', heads, keys, preferred_element_type=jnp.f...  7.86 us
    dot_general x1, matrix products, per_device(): jnp.einsum('rps,rskd->rkpd', onehot, new_values.reshape(seqs, steps, kv_h...  4.89 us
    convert_element_type x1, other arithmetic, per_device(): expo.astype(jnp.bfloat16)  4.1 us
  transfers between devices with their start and end apart: 2, of which 2 were waited for; matrix products, arithmetic and copies ran while one was open for 3% of the time, Pallas kernels for 0%

profile of v1, /device:TPU:1, one launch (start us, length us, event | category | flops | bytes accessed | tf_op | source)
XLA Modules:
  0.0 150.9 jit_solution(8176936728696700088)
XLA Ops:
  0.7 2.4 %broadcast_in_dim.43 = bf16[16,8,8,4,128]{4,3,2,1,0:T(4,128)(2,1)} broadcast(bf16[8,8,4,128]{3,2,1,0:T(4,128)(2,1)} %bitcast.112), dimensions={1,2,3,4} | broadcast | bytes 1114112 | tf_op jit(solution)/shard_map/broadcast_in_dim | solution.py:19
  3.1 7.2 %all-to-all-start = ((bf16[16,8,8,4,128]{4,3,2,1,0:T(4,128)(2,1)}), bf16[16,8,8,4,128]{4,3,2,1,0:T(4,128)(2,1)S(1)}, u32[]{:S(2)}, u32[]{:S(2)}) async-start(bf16[16,8,8,4,128]{4,3,2,1,0:T(4,128)(2,1)} %broadcast_in_dim.43), calls=%async_computation | async-start | bytes 2097152 | tf_op jit(solution)/shard_map/all_to_all | solution.py:19
  10.3 0.1 compare_and_fusion
  10.5 0.1 broadcast_compare_fusion
  10.6 4.9 %fusion.4 = bf16[8,8,256,128,1]{3,2,1,0,4:T(8,128)(2,1)} fusion(bf16[8,8,256,128]{3,2,1,0:T(8,128)(2,1)} %param.13, pred[8,256]{1,0:T(8,128)(4,1)S(1)} %compare_and_fusion, bf16[8,4,1024]{2,1,0:T(4,128)(2,1)S(1)} %copy-done.1, s32[8,256]{1,0:T(8,128)S(1)} %broadcast_subtract_fusion), kind=kOutput, calls=%fused_computation.8 | convolution fusion | flops 20979712 | bytes 8464384 | tf_op jit(solution)/shard_map/rps,rskd->rkpd/dot_general | solution.py:56
  15.5 10.6 %all-to-all-done = bf16[16,8,8,4,128]{4,3,2,1,0:T(4,128)(2,1)S(1)} async-done(((bf16[16,8,8,4,128]{4,3,2,1,0:T(4,128)(2,1)}), bf16[16,8,8,4,128]{4,3,2,1,0:T(4,128)(2,1)S(1)}, u32[]{:S(2)}, u32[]{:S(2)}) %all-to-all-start) | async-done | bytes 1048608 | tf_op jit(solution)/shard_map/all_to_all | solution.py:19
  26.1 1.4 copy.37
  27.5 7.9 %fusion.7 = (f32[8,8,2,32]{3,2,1,0:T(2,128)S(1)}, f32[8,8,256,2,32]{2,4,3,1,0:T(8,128)}) fusion(pred[8,32,256]{2,1,0:T(8,128)(4,1)S(1)} %broadcast_compare_fusion, bf16[8,2,8,32,128]{4,3,1,0,2:T(8,128)(2,1)} %bitcast.108, bf16[8,8,256,128]{3,2,1,0:T(8,128)(2,1)} %param.12, pred[8,256]{1,0:T(8,128)(4,1)S(1)} %compare_and_fusion, ...), kind=kOutput, calls=%fused_computation.12 | convolution fusion | flops 292556800 | bytes 9594880 | tf_op jit(solution)/shard_map/karqd,rkpd->rkaqp/dot_general | solution.py:64
  35.3 4.1 %fusion.11 = (bf16[8,8,2,32,256]{4,3,2,1,0:T(8,128)(2,1)}, f32[8,8,2,32]{3,2,1,0:T(2,128)S(1)}) fusion(f32[8,8,256,2,32]{2,4,3,1,0:T(8,128)} %get-tuple-element.20, f32[8,8,2,32]{3,2,1,0:T(2,128)S(1)} %get-tuple-element.19, pred[8,32,256]{2,1,0:T(8,128)(4,1)S(1)} %broadcast_compare_fusion), kind=kLoop, calls=%fused_computation.15 | loop fusion | flops 6287360 | bytes 6389760 | tf_op jit(solution)/shard_map/convert_element_type | solution.py:76
  39.5 0.1 fusion.27
  39.6 0.1 reshape.306
  39.8 3.7 %fusion.14 = bf16[8,2,8,32,128]{4,3,1,2,0:T(8,128)(2,1)S(1)} fusion(bf16[8,8,2,32,256]{4,3,2,1,0:T(8,128)(2,1)} %get-tuple-element.6, bf16[8,8,256,128,1]{3,2,1,0,4:T(8,128)(2,1)} %fusion.4, f32[8,2,8,32]{3,1,0,2:T(2,128)S(1)} %get-tuple-element.10), kind=kOutput, calls=%fused_computation.22 | convolution fusion | flops 269484032 | bytes 7356416 | tf_op jit(solution)/shard_map/rkaqp,rkpd->karqd/dot_general | solution.py:75
  43.5 0.1 copy.41
  43.6 0.1 fusion.21
  43.7 20.2 %all_to_all.25 = bf16[16,272,128]{2,1,0:T(8,128)(2,1)S(1)} all-to-all(bf16[16,272,128]{2,1,0:T(8,128)(2,1)S(1)} %fusion.21), channel_id=1, replica_groups=mesh['tp'=16,'grp'=16] {'tp'}, dimensions={0} | all-to-all | bytes 2228224 | tf_op jit(solution)/shard_map/all_to_all | solution.py:86
  64.0 0.1 div.38
  64.1 0.7 multiply_reduce_fusion.1
  64.9 0.1 divide_bitcast_fusion
  65.1 1.1 broadcast_in_dim.47
  66.2 10.0 %all-to-all-start.2 = ((bf16[16,32,1024]{2,1,0:T(8,128)(2,1)}), bf16[16,32,1024]{2,1,0:T(8,128)(2,1)S(1)}, u32[]{:S(2)}, u32[]{:S(2)}) async-start(bf16[16,32,1024]{2,1,0:T(8,128)(2,1)} %broadcast_in_dim.47), calls=%async_computation.2 | async-start | bytes 2097152 | tf_op jit(solution)/shard_map/all_to_all | solution.py:19
  76.2 27.8 %all-to-all-done.2 = bf16[16,32,1024]{2,1,0:T(8,128)(2,1)S(1)} async-done(((bf16[16,32,1024]{2,1,0:T(8,128)(2,1)}), bf16[16,32,1024]{2,1,0:T(8,128)(2,1)S(1)}, u32[]{:S(2)}, u32[]{:S(2)}) %all-to-all-start.2) | async-done | bytes 1048608 | tf_op jit(solution)/shard_map/all_to_all | solution.py:19
  104.0 0.3 multiply_reduce_fusion
  104.4 0.2 copy.52
  104.6 1.2 convolution_convert_fusion
  105.8 0.1 fusion.20
  106.0 22.5 %all_to_all.26 = bf16[16,32,1152]{2,1,0:T(8,128)(2,1)S(1)} all-to-all(bf16[16,32,1152]{2,1,0:T(8,128)(2,1)S(1)} %fusion.20), channel_id=1, replica_groups=mesh['tp'=16,'grp'=16] {'tp'}, dimensions={0} | all-to-all | bytes 2359296 | tf_op jit(solution)/shard_map/all_to_all | solution.py:114
  128.5 0.2 convert_reduce_fusion
  128.7 0.1 slice_reduce_fusion
  128.8 0.7 multiply_convert_fusion
  129.5 0.1 broadcast_in_dim.78
  129.7 18.6 %all_to_all.27 = bf16[16,32,1024]{2,1,0:T(8,128)(2,1)S(1)} all-to-all(bf16[16,32,1024]{2,1,0:T(8,128)(2,1)S(1)} %broadcast_in_dim.78), channel_id=1, replica_groups=mesh['tp'=16,'grp'=16] {'tp'}, dimensions={0} | all-to-all | bytes 2097152 | tf_op jit(solution)/shard_map/all_to_all | solution.py:19
  148.3 2.6 %bitcast_convert_fusion = bf16[1024,1024]{1,0:T(8,128)(2,1)} fusion(bf16[16,32,1024]{2,1,0:T(8,128)(2,1)S(1)} %all-to-all-done.2, bf16[16,32,1024]{2,1,0:T(8,128)(2,1)S(1)} %all_to_all.27), kind=kOutput, calls=%fused_computation.2 | convolution fusion | flops 1074790400 | bytes 4194304 | tf_op jit(solution)/shard_map/dot_general | solution.py:124
  (32 shorter events, 0.5 us)
Async XLA Ops:
  0.6 104.0 %copy-start = (bf16[1024,1024]{1,0:T(8,128)(2,1)S(1)}, bf16[1024,1024]{1,0:T(8,128)(2,1)}, u32[]{:S(2)}) copy-start(bf16[1024,1024]{1,0:T(8,128)(2,1)} %param.16) | copy-start | bytes 6291460
  0.6 9.6 %copy-start.4 = (s32[8]{0:T(128)S(1)}, s32[8]{0:T(128)}, u32[]{:S(2)}) copy-start(s32[8]{0:T(128)} %param.14) | copy-start | bytes 100
  0.7 9.9 %copy-start.1 = (bf16[8,4,1024]{2,1,0:T(4,128)(2,1)S(1)}, bf16[8,4,1024]{2,1,0:T(4,128)(2,1)}, u32[]{:S(2)}) copy-start(bf16[8,4,1024]{2,1,0:T(4,128)(2,1)} %param.11) | copy-start | bytes 196612
  3.1 23.0 %all-to-all-start = ((bf16[16,8,8,4,128]{4,3,2,1,0:T(4,128)(2,1)}), bf16[16,8,8,4,128]{4,3,2,1,0:T(4,128)(2,1)S(1)}, u32[]{:S(2)}, u32[]{:S(2)}) async-start(bf16[16,8,8,4,128]{4,3,2,1,0:T(4,128)(2,1)} %broadcast_in_dim.43), calls=%async_computation | async-start | bytes 2097152 | tf_op jit(solution)/shard_map/all_to_all | solution.py:19
  10.6 16.9 %copy-start.5 = (bf16[8,4,1024]{2,1,0:T(4,128)(2,1)S(1)}, bf16[8,4,1024]{2,1,0:T(4,128)(2,1)}, u32[]{:S(2)}) copy-start(bf16[8,4,1024]{2,1,0:T(4,128)(2,1)} %param.10) | copy-start | bytes 196612
  43.7 21.3 %copy-start.3 = (f32[1024]{0:T(1024)S(1)}, f32[1024]{0:T(1024)}, u32[]{:S(2)}) copy-start(f32[1024]{0:T(1024)} %param.15) | copy-start | bytes 12292
  66.2 37.8 %all-to-all-start.2 = ((bf16[16,32,1024]{2,1,0:T(8,128)(2,1)}), bf16[16,32,1024]{2,1,0:T(8,128)(2,1)S(1)}, u32[]{:S(2)}, u32[]{:S(2)}) async-start(bf16[16,32,1024]{2,1,0:T(8,128)(2,1)} %broadcast_in_dim.47), calls=%async_computation.2 | async-start | bytes 2097152 | tf_op jit(solution)/shard_map/all_to_all | solution.py:19
  106.0 22.9 %copy-start.2 = (bf16[32,1024]{1,0:T(8,128)(2,1)S(1)}, bf16[32,1024]{1,0:T(8,128)(2,1)}, u32[]{:S(2)}) copy-start(bf16[32,1024]{1,0:T(8,128)(2,1)} %param.17) | copy-start | bytes 196612

commit v2 on v0

v2 whole, which is shorter than its diff:
```python
import functools
import math

import jax
import jax.numpy as jnp
from jax import lax
from jax.experimental import pallas as pl
from jax.experimental.pallas import tpu as pltpu
from jax.sharding import Mesh
from jax.sharding import PartitionSpec as P

TP = ("ch", "c")
TILE = 16


def split_pieces(x):
    a = lax.reduce_precision(x, 8, 7)
    b = lax.reduce_precision(x - a, 8, 7)
    return a, b, x - a - b


def gather(x, axis):
    n = lax.axis_size(axis)
    return lax.all_to_all(jnp.broadcast_to(x[None], (n,) + x.shape), axis, 0, 0)


def swap(x):
    return lax.ppermute(x, "c", [(0, 1), (1, 0)])


def attend_kernel(steps, meta, q_ref, ko, vo, ks, vs, new_ref, out_ref, lse_ref):
    i = pl.program_id(0)
    half = pl.num_programs(0)
    kv_heads, block, head_size = ko.shape[1:]
    q_rows = q_ref.shape[1] * q_ref.shape[3]
    length = meta[3 + meta[0] * half + i]
    scale = 1.0 / math.sqrt(head_size)

    for kref, vref, base in ((ko, vo, meta[1]), (ks, vs, meta[2])):
        for j in range(steps):
            place = length + j - base

            @pl.when((place >= 0) & (place < block))
            def _(kref=kref, vref=vref, place=place, j=j):
                start = pl.multiple_of((place // TILE) * TILE, TILE)
                hit = lax.broadcasted_iota(jnp.int32, (TILE, head_size), 0) == place - start
                for k in range(kv_heads):
                    for which, ref in ((0, kref), (1, vref)):
                        slab = ref[0, k, pl.ds(start, TILE), :].astype(jnp.float32)
                        fresh = new_ref[0, which, k, j : j + 1, :]
                        ref[0, k, pl.ds(start, TILE), :] = jnp.where(hit, fresh, slab).astype(
                            jnp.bfloat16
                        )

    row = lax.broadcasted_iota(jnp.int32, (q_rows, block), 0)
    lane = lax.broadcasted_iota(jnp.int32, (q_rows, block), 1)
    limit = length + lax.rem(row, steps) + 1
    valid_o = lane + meta[1] < limit
    valid_s = lane + meta[2] < limit
    column = lax.broadcasted_iota(jnp.int32, (q_rows, 128), 1) == i
    nt = (((1,), (1,)), ((), ()))

    @pl.when(i == 0)
    def _():
        lse_ref[...] = jnp.zeros_like(lse_ref)

    for k in range(kv_heads):
        q = q_ref[k, :, 0].reshape(q_rows, head_size)
        so = lax.dot_general(q, ko[0, k], nt, preferred_element_type=jnp.float32)
        ss = lax.dot_general(q, ks[0, k], nt, preferred_element_type=jnp.float32)
        so = jnp.where(valid_o, so * scale, -1e30)
        ss = jnp.where(valid_s, ss * scale, -1e30)
        top = jnp.max(jnp.maximum(so, ss), axis=1, keepdims=True)
        po = jnp.exp(so - top)
        ps = jnp.exp(ss - top)
        total = jnp.sum(po + ps, axis=1, keepdims=True)
        acc = jnp.dot(po.astype(jnp.bfloat16), vo[0, k], preferred_element_type=jnp.float32)
        acc += jnp.dot(ps.astype(jnp.bfloat16), vs[0, k], preferred_element_type=jnp.float32)
        out_ref[k, pl.ds(pl.multiple_of(i * q_rows, q_rows), q_rows), :] = (acc / total).astype(
            jnp.bfloat16
        )
        lse = jnp.where(top > -1e29, top + jnp.log(total), -1e30)
        lse_ref[k, :q_rows, :] = jnp.where(column, lse, lse_ref[k, :q_rows, :])

    @pl.when(i == half - 1)
    def _():
        for k in range(kv_heads):
            x = lse_ref[k].T[:half]
            a = x.astype(jnp.bfloat16).astype(jnp.float32)
            b = (x - a).astype(jnp.bfloat16).astype(jnp.float32)
            c = x - a - b
            rows = jnp.concatenate([a, b, c, jnp.zeros((TILE - 3 * half, 128), jnp.float32)], 0)
            out_ref[k, half * q_rows :, :] = rows.astype(jnp.bfloat16)


def attend(steps, meta, heads, own_k, own_v, sib_k, sib_v, fresh):
    kv_heads, share, half, rows, head_size = heads.shape
    block = own_k.shape[2]
    q_rows = share * rows
    out_rows = half * q_rows + TILE
    own = pl.BlockSpec((1, kv_heads, block, head_size), lambda i, m: (m[0] * half + i, 0, 0, 0))
    sib = pl.BlockSpec((1, kv_heads, block, head_size), lambda i, m: (i, 0, 0, 0))
    return pl.pallas_call(
        functools.partial(attend_kernel, steps),
        grid_spec=pltpu.PrefetchScalarGridSpec(
            num_scalar_prefetch=1,
            grid=(half,),
            in_specs=[
                pl.BlockSpec(
                    (kv_heads, share, 1, rows, head_size), lambda i, m: (0, 0, i, 0, 0)
                ),
                own,
                own,
                sib,
                sib,
                pl.BlockSpec(
                    (1, 2, kv_heads, steps, head_size), lambda i, m: (m[0] * half + i, 0, 0, 0, 0)
                ),
            ],
            out_specs=pl.BlockSpec((kv_heads, out_rows, head_size), lambda i, m: (0, 0, 0)),
            scratch_shapes=[pltpu.VMEM((kv_heads, 128, 128), jnp.float32)],
        ),
        out_shape=jax.ShapeDtypeStruct((kv_heads, out_rows, head_size), jnp.bfloat16),
        compiler_params=pltpu.CompilerParams(
            dimension_semantics=("arbitrary",), vmem_limit_bytes=32 * 1024 * 1024
        ),
        cost_estimate=pl.CostEstimate(
            flops=half * kv_heads * q_rows * 2 * block * head_size * 4,
            bytes_accessed=half * kv_heads * block * head_size * 8,
            transcendentals=half * kv_heads * q_rows * 2 * block,
        ),
        name="attend",
    )(meta, heads, own_k, own_v, sib_k, sib_v, fresh)


def per_device(
    queries,
    new_keys,
    new_values,
    cache_keys,
    cache_values,
    lengths,
    norm_gain,
    draft_weight,
    next_hidden,
):
    chips, cores = lax.axis_size("ch"), lax.axis_size("c")
    chip, core = lax.axis_index("ch"), lax.axis_index("c")
    zh, ny = lax.axis_size("zh"), lax.axis_size("y")
    seqs, steps, feats = queries.shape
    kv_heads, block, head_size = (cache_keys.shape[1], cache_keys.shape[2], cache_keys.shape[3])
    mine = feats // head_size
    width = feats * chips * cores
    half = seqs // cores
    hrows = half * steps
    cols = draft_weight.shape[1]
    other = 1 - core

    packed = queries.reshape(cores, half, steps, mine, head_size).transpose(0, 1, 3, 2, 4)
    packed = packed.reshape(cores, half, mine * steps, head_size)
    spread = jnp.broadcast_to(packed[None], (chips,) + packed.shape)
    spread = spread.reshape((chips * cores,) + packed.shape[1:])

    sib_k = swap(lax.dynamic_slice_in_dim(cache_keys, other * half, half, 0))
    sib_v = swap(lax.dynamic_slice_in_dim(cache_values, other * half, half, 0))
    sib_w = swap(draft_weight)
    sib_gain = swap(norm_gain)
    sib_hidden = swap(lax.dynamic_slice_in_dim(next_hidden, other * hrows, hrows, 0))
    own_hidden = lax.dynamic_slice_in_dim(next_hidden, core * hrows, hrows, 0)

    heads = lax.all_to_all(spread, TP, 0, 0).reshape(
        kv_heads, cores, half, mine * steps, head_size
    )
    place = (chip * cores + core) * block
    sib_place = (chip * cores + other) * block
    meta = jnp.concatenate([jnp.stack([core, place, sib_place]).astype(jnp.int32), lengths])
    fresh = jnp.stack([new_keys, new_values], axis=1).reshape(
        seqs, 2, steps, kv_heads, head_size
    )
    fresh = fresh.transpose(0, 1, 3, 2, 4).astype(jnp.float32)
    sent = attend(steps, meta, heads, cache_keys, cache_values, sib_k, sib_v, fresh)

    got = lax.all_to_all(sent, "ch", 0, 0)
    q_rows = cores * mine * steps
    outs = got[:, : half * q_rows].astype(jnp.float32).reshape(chips, half, q_rows, head_size)
    lse = got[:, half * q_rows : half * q_rows + 3 * half, :q_rows].astype(jnp.float32)
    lse = jnp.sum(lse.reshape(chips, 3, half, q_rows), axis=1)
    factor = jnp.exp(lse - jnp.max(lse, axis=0, keepdims=True))
    context = jnp.sum(outs * factor[..., None], axis=0) / jnp.sum(factor, axis=0)[..., None]
    context = context.reshape(half, cores, mine, steps, head_size).transpose(1, 0, 3, 2, 4)
    context = context.reshape(cores, hrows, feats)
    flat_own = lax.dynamic_index_in_dim(context, core, 0, keepdims=False)
    flat_sib = lax.dynamic_index_in_dim(context, other, 0, keepdims=False)
    raw = jnp.stack([flat_own * norm_gain[None, :], flat_sib * sib_gain[None, :]])
    raw = raw.astype(jnp.bfloat16)

    by_zh = gather(raw, "zh")
    by_y = gather(by_zh, "y")
    by_y = by_y.transpose(2, 1, 0, 3, 4).reshape(2, zh * ny * hrows, feats)
    own_raw, sib_raw = by_y[0], by_y[1]
    row_half = zh * ny * hrows
    row_count = row_half * cores

    def squares(x, gain):
        plain = x.astype(jnp.float32) * (1.0 / gain)[None, :]
        return jnp.sum(plain * plain, axis=1)

    sq = squares(own_raw, norm_gain) + squares(sib_raw, sib_gain)
    sq = jnp.stack(split_pieces(sq), axis=-1).astype(jnp.bfloat16)
    sq = jnp.pad(sq, ((0, 0), (0, 128 - 3))).reshape(chips, cores * hrows, 128)
    partial = jnp.dot(own_raw, draft_weight, preferred_element_type=jnp.float32)
    partial += jnp.dot(sib_raw, sib_w, preferred_element_type=jnp.float32)
    partial = partial.astype(jnp.bfloat16).reshape(chips, cores * hrows, cols)
    oth_raw = swap(sib_raw)
    parts = lax.all_to_all(jnp.concatenate([partial, sq], axis=2), "ch", 0, 0)
    summed = jnp.sum(parts.astype(jnp.float32), axis=0)
    meansq = jnp.sum(summed[:, cols : cols + 3], axis=1) / width
    scale = lax.rsqrt(meansq + 1e-05)[:, None]
    total = summed[:, :cols] * scale

    flip = core == 1
    hid0 = jnp.where(flip, sib_hidden, own_hidden)
    hid1 = jnp.where(flip, own_hidden, sib_hidden)
    hidden = jnp.concatenate([hid0, hid1]).astype(jnp.float32)
    grad_mine = ((total - hidden) * (scale / math.sqrt(row_count))).astype(jnp.bfloat16)
    grad_half = gather(grad_mine, "ch").reshape(row_half, cols)
    grad_other = swap(grad_half)

    pred = total.astype(jnp.bfloat16).reshape(cores, hrows, cols)
    keep = jnp.where(flip, pred[1], pred[0])
    came = swap(jnp.where(flip, pred[0], pred[1]))
    prediction = jnp.concatenate([jnp.where(flip, came, keep), jnp.where(flip, keep, came)])

    tn = (((0,), (0,)), ((), ()))
    weight_grad = lax.dot_general(own_raw, grad_half, tn, preferred_element_type=jnp.float32)
    weight_grad += lax.dot_general(oth_raw, grad_other, tn, preferred_element_type=jnp.float32)
    return (prediction, weight_grad.astype(jnp.bfloat16))


def solution(mesh):
    tp, grp = mesh.devices.shape
    fine = Mesh(mesh.devices.reshape(tp // 2, 2, 4, grp // 4), ("ch", "c", "zh", "y"))
    g = ("zh", "y")
    in_specs = (
        P(g, None, TP),
        P(g, None, None),
        P(g, None, None),
        P(g, None, TP, None),
        P(g, None, TP, None),
        P(g),
        P(TP),
        P(TP, g),
        P(TP, g),
    )
    out_specs = (P(TP, g), P(TP, g))
    return jax.shard_map(
        per_device, mesh=fine, in_specs=in_specs, out_specs=out_specs, check_vma=False
    )
```

time: 386 us -> 128 us (0.33)
  waiting for transfers between devices: 200 us -> 37.7 us
  blocking collectives: 134 us -> 0 us
  starting transfers between devices: 0.2 us -> 53 us
  between operations: 14.6 us -> 0.92 us
  matrix products: 20.8 us -> 7.42 us
  Pallas kernels: 0 us -> 11.5 us
  local copies, waits for them, and re-layouts: 5.01 us -> 13.5 us
  other arithmetic: 10.8 us -> 2.94 us
    all_gather x3 -> x0, waiting for transfers between devices: 128 us -> none  [the longest x1 51.6 us: per_device(): all_rows = lax.all_gather(rows, 'grp', axis=0, tiled=True)]
    reduce_scatter x2 -> x0, waiting for transfers between devices: 71.2 us -> none  [the longest x1 59.4 us: per_device(): lax.psum_scatter(jnp.dot(all_rows, draft_weight, preferred_element_type=j...]
    unnamed x1 -> x0, blocking collectives: 53 us -> none
    pmax x1 -> x0, blocking collectives: 50.5 us -> none  [per_device(): top = lax.pmax(local_max, 'tp')]
    all_to_all x0 -> x6, waiting for transfers between devices: none -> 36.7 us  [the longest x3 17.6 us: gather(): return lax.all_to_all(jnp.broadcast_to(x[None], (n,) + x.shape), axis, 0, 0)]
    psum x1 -> x0, blocking collectives: 30.6 us -> none  [per_device(): squares = lax.psum(jnp.sum(flat * flat, axis=1), 'tp')]
    all_to_all x0 -> x6, starting transfers between devices: none -> 27 us  [the longest x3 15.5 us: gather(): return lax.all_to_all(jnp.broadcast_to(x[None], (n,) + x.shape), axis, 0, 0)]
    ppermute x0 -> x8, starting transfers between devices: none -> 26 us  [swap(): return lax.ppermute(x, 'c', [(0, 1), (1, 0)])]
  transfers between devices with their start and end apart: 5 -> 14, of which waited for: 5 -> 8; matrix products, arithmetic and copies ran while one was open for 1% -> 7% of each run, Pallas kernels for 0% -> 0%
where the time goes in v2:
time: 128 us; the launch traced here: 127 us
  starting transfers between devices  53 us (41%)
  waiting for transfers between devices  37.7 us (29%)
  local copies, waits for them, and re-layouts  13.5 us (11%)
  Pallas kernels  11.5 us (9%)
  matrix products  7.42 us (6%)
  other arithmetic  2.94 us (2%)
    ppermute x8, starting transfers between devices, swap(): return lax.ppermute(x, 'c', [(0, 1), (1, 0)])  26 us
    all_to_all x3, waiting for transfers between devices, gather(): return lax.all_to_all(jnp.broadcast_to(x[None], (n,) + x.shape), axis, 0, 0)  17.6 us
    all_to_all x3, starting transfers between devices, gather(): return lax.all_to_all(jnp.broadcast_to(x[None], (n,) + x.shape), axis, 0, 0)  15.5 us
    pallas_call x1, Pallas kernels, attend(): pl.pallas_call(functools.partial(attend_kernel, steps), grid_spec=pltpu.P...  11.5 us
    all_to_all x1, waiting for transfers between devices, per_device(): lax.all_to_all(spread, TP, 0, 0)  9.62 us
    all_to_all x1, waiting for transfers between devices, per_device(): got = lax.all_to_all(sent, 'ch', 0, 0)  7.85 us
    unnamed x19, local copies, waits for them, and re-layouts  4.55 us
    all_to_all x1, starting transfers between devices, per_device(): lax.all_to_all(spread, TP, 0, 0)  4.41 us
  transfers between devices with their start and end apart: 14, of which 8 were waited for; matrix products, arithmetic and copies ran while one was open for 7% of the time, Pallas kernels for 0%

profile of v2, /device:TPU:1, one launch (start us, length us, event | category | flops | bytes accessed | tf_op | source)
XLA Modules:
  0.0 127.0 jit_solution(2778087617932647846)
XLA Ops:
  0.6 3.3 %constant_dynamic-slice_fusion.1 = bf16[4,8,256,128]{3,2,1,0:T(8,128)(2,1)} fusion(bf16[8,8,256,128]{3,2,1,0:T(8,128)(2,1)} %vo.1, s32[]{:T(128)S(6)} %select_n.46), kind=kLoop, calls=%fused_computation.32 | loop fusion | bytes 4194308 | tf_op jit(solution)/shard_map/dynamic_slice | solution.py:165
  3.9 3.3 %collective-permute-start.1 = (bf16[4,8,256,128]{3,2,1,0:T(8,128)(2,1)}, bf16[4,8,256,128]{3,2,1,0:T(8,128)(2,1)S(1)}, u32[]{:S(2)}, u32[]{:S(2)}) collective-permute-start(bf16[4,8,256,128]{3,2,1,0:T(8,128)(2,1)} %constant_dynamic-slice_fusion.1), channel_id=1, source_target_pairs={{0,16},{16,0},{1,17},{17,1},{2,18},{18,2},{3,19},{19,3},{4,20},{20... | collective-permute-start | bytes 6291464 | tf_op jit(solution)/shard_map/ppermute | solution.py:28
  7.3 1.5 %constant_dynamic-slice_fusion.2 = bf16[4,8,256,128]{3,2,1,0:T(8,128)(2,1)} fusion(bf16[8,8,256,128]{3,2,1,0:T(8,128)(2,1)S(1)} %copy-done, s32[]{:T(128)S(6)} %select_n.46), kind=kLoop, calls=%fused_computation.33 | loop fusion | bytes 4194308 | tf_op jit(solution)/shard_map/dynamic_slice | solution.py:164
  8.8 0.9 broadcast_in_dim.11
  9.7 4.4 %all-to-all-start = ((bf16[16,4,32,128]{3,2,1,0:T(8,128)(2,1)}), bf16[16,4,32,128]{3,2,1,0:T(8,128)(2,1)S(1)}, u32[]{:S(2)}, u32[]{:S(2)}) async-start(bf16[16,4,32,128]{3,2,1,0:T(8,128)(2,1)} %bitcast.6), calls=%async_computation | async-start | bytes 1048576 | tf_op jit(solution)/shard_map/all_to_all | solution.py:171
  14.2 9.6 %all-to-all-done = bf16[16,4,32,128]{3,2,1,0:T(8,128)(2,1)S(1)} async-done(((bf16[16,4,32,128]{3,2,1,0:T(8,128)(2,1)}), bf16[16,4,32,128]{3,2,1,0:T(8,128)(2,1)S(1)}, u32[]{:S(2)}, u32[]{:S(2)}) %all-to-all-start) | async-done | bytes 524320 | tf_op jit(solution)/shard_map/all_to_all | solution.py:171
  23.9 2.2 %copy-done.1 = bf16[8,8,256,128]{3,2,1,0:T(8,128)(2,1)S(1)} copy-done((bf16[8,8,256,128]{3,2,1,0:T(8,128)(2,1)S(1)}, bf16[8,8,256,128]{3,2,1,0:T(8,128)(2,1)}, u32[]{:S(2)}) %copy-start.1) | copy-done | bytes 4194328
  26.1 2.2 %copy-done.2 = bf16[8,8,256,128]{3,2,1,0:T(8,128)(2,1)S(1)} copy-done((bf16[8,8,256,128]{3,2,1,0:T(8,128)(2,1)S(1)}, bf16[8,8,256,128]{3,2,1,0:T(8,128)(2,1)}, u32[]{:S(2)}) %copy-start.2) | copy-done | bytes 4194328
  28.3 11.5 %attend.1 = bf16[8,272,128]{2,1,0:T(8,128)(2,1)} custom-call(s32[11]{0:T(128)S(1)} %pad_add_fusion.meta, bf16[8,2,4,32,128]{4,3,2,1,0:T(8,128)(2,1)S(1)} %bitcast.36, bf16[8,8,256,128]{3,2,1,0:T(8,128)(2,1)S(1)} %copy-done.1, bf16[8,8,256,128]{3,2,1,0:T(8,128)(2,1)S(1)} %copy-done.2, bf16[4,8,256,128]{3,2,1,0:T(8,128)(2,1)} %collective-permute-done.ks, ...), custom_call_target="tpu_custom_call" | custom-call | flops 536870912 | bytes 8388608 | tf_op jit(solution)/shard_map/attend/pallas_call | solution.py:103
  39.7 3.5 %all-to-all-start.1 = ((bf16[8,272,128]{2,1,0:T(8,128)(2,1)}), bf16[8,272,128]{2,1,0:T(8,128)(2,1)S(1)}, u32[]{:S(2)}, u32[]{:S(2)}) async-start(bf16[8,272,128]{2,1,0:T(8,128)(2,1)} %attend.1), calls=%async_computation.1 | async-start | bytes 1114112 | tf_op jit(solution)/shard_map/all_to_all | solution.py:183
  43.3 1.3 %collective-permute-start.2 = (f32[1024]{0:T(1024)S(1)}, f32[1024]{0:T(1024)S(1)}, u32[]{:S(2)}, u32[]{:S(2)}) collective-permute-start(f32[1024]{0:T(1024)S(1)} %copy-done.7), channel_id=1, source_target_pairs={{0,16},{16,0},{1,17},{17,1},{2,18},{18,2},{3,19},{19,3},{4,20},{20... | collective-permute-start | bytes 12296 | tf_op jit(solution)/shard_map/ppermute | solution.py:28
  44.6 7.8 %all-to-all-done.1 = bf16[8,272,128]{2,1,0:T(8,128)(2,1)S(1)} async-done(((bf16[8,272,128]{2,1,0:T(8,128)(2,1)}), bf16[8,272,128]{2,1,0:T(8,128)(2,1)S(1)}, u32[]{:S(2)}, u32[]{:S(2)}) %all-to-all-start.1) | async-done | bytes 557088 | tf_op jit(solution)/shard_map/all_to_all | solution.py:183
  54.2 7.3 %all-to-all-start.2 = ((bf16[4,2,16,1024]{3,2,1,0:T(8,128)(2,1)}), bf16[4,2,16,1024]{3,2,1,0:T(8,128)(2,1)S(1)}, u32[]{:S(2)}, u32[]{:S(2)}) async-start(bf16[4,2,16,1024]{3,2,1,0:T(8,128)(2,1)} %broadcast_in_dim.12), calls=%async_computation.2 | async-start | bytes 524288 | tf_op jit(solution)/shard_map/all_to_all | solution.py:24
  61.4 2.4 %collective-permute-start.3 = (bf16[1024,1024]{1,0:T(8,128)(2,1)}, bf16[1024,1024]{1,0:T(8,128)(2,1)}, u32[]{:S(2)}, u32[]{:S(2)}) collective-permute-start(bf16[1024,1024]{1,0:T(8,128)(2,1)} %param.16), channel_id=1, source_target_pairs={{0,16},{16,0},{1,17},{17,1},{2,18},{18,2},{3,19},{19,3},{4,20},{20... | collective-permute-start | bytes 6291464 | tf_op jit(solution)/shard_map/ppermute | solution.py:28
  63.9 5.6 %all-to-all-done.2 = bf16[4,2,16,1024]{3,2,1,0:T(8,128)(2,1)S(1)} async-done(((bf16[4,2,16,1024]{3,2,1,0:T(8,128)(2,1)}), bf16[4,2,16,1024]{3,2,1,0:T(8,128)(2,1)S(1)}, u32[]{:S(2)}, u32[]{:S(2)}) %all-to-all-start.2) | async-done | bytes 262176 | tf_op jit(solution)/shard_map/all_to_all | solution.py:24
  69.5 1.1 broadcast_in_dim.13
  70.6 4.5 %all-to-all-start.3 = ((bf16[4,4,2,16,1024]{4,3,1,2,0:T(8,128)(2,1)}), bf16[4,4,2,16,1024]{4,3,1,2,0:T(8,128)(2,1)S(1)}, u32[]{:S(2)}, u32[]{:S(2)}) async-start(bf16[4,4,2,16,1024]{4,3,1,2,0:T(8,128)(2,1)} %broadcast_in_dim.13), calls=%async_computation.3 | async-start | bytes 2097152 | tf_op jit(solution)/shard_map/all_to_all | solution.py:24
  75.2 10.8 %all-to-all-done.3 = bf16[4,4,2,16,1024]{4,3,1,2,0:T(8,128)(2,1)S(1)} async-done(((bf16[4,4,2,16,1024]{4,3,1,2,0:T(8,128)(2,1)}), bf16[4,4,2,16,1024]{4,3,1,2,0:T(8,128)(2,1)S(1)}, u32[]{:S(2)}, u32[]{:S(2)}) %all-to-all-start.3) | async-done | bytes 1048608 | tf_op jit(solution)/shard_map/all_to_all | solution.py:24
  86.8 2.3 %fusion.4 = f32[256,1024]{1,0:T(8,128)S(1)} fusion(bf16[256,1024]{1,0:T(8,128)(2,1)S(1)} %bitcast.39, bf16[1024,1024]{1,0:T(8,128)(2,1)} %param.16), kind=kOutput, calls=%fused_computation.43 | convolution fusion | flops 536870912 | bytes 3670016 | tf_op jit(solution)/shard_map/dot_general | solution.py:211
  89.2 2.3 %fusion = bf16[256,1024]{1,0:T(8,128)(2,1)S(1)} fusion(f32[256,1024]{1,0:T(8,128)S(1)} %fusion.4, bf16[256,1024]{1,0:T(8,128)(2,1)S(1)} %bitcast.44, bf16[1024,1024]{1,0:T(8,128)(2,1)} %collective-permute-done.3), kind=kOutput, calls=%fused_computation.2 | convolution fusion | flops 537395200 | bytes 4194304 | tf_op jit(solution)/shard_map/dot_general | solution.py:212
  91.5 0.9 pad_maximum_fusion
  92.3 3.5 %all-to-all-start.4 = ((bf16[8,32,1152]{2,1,0:T(8,128)(2,1)}), bf16[8,32,1152]{2,1,0:T(8,128)(2,1)S(1)}, u32[]{:S(2)}, u32[]{:S(2)}) async-start(bf16[8,32,1152]{2,1,0:T(8,128)(2,1)} %pad_maximum_fusion), calls=%async_computation.4 | async-start | bytes 1179648 | tf_op jit(solution)/shard_map/all_to_all | solution.py:215
  95.9 5.3 %collective-permute-start.5 = (bf16[16,1024]{1,0:T(8,128)(2,1)S(1)}, bf16[16,1024]{1,0:T(8,128)(2,1)S(1)}, u32[]{:S(2)}, u32[]{:S(2)}) collective-permute-start(bf16[16,1024]{1,0:T(8,128)(2,1)S(1)} %constant_dynamic-slice_fusion), channel_id=1, source_target_pairs={{0,16},{16,0},{1,17},{17,1},{2,18},{18,2},{3,19},{19,3},{4,20},{20... | collective-permute-start | bytes 98312 | tf_op jit(solution)/shard_map/ppermute | solution.py:28
  101.2 0.9 collective-permute-done.5
  102.1 1.6 %all-to-all-done.4 = bf16[8,32,1152]{2,1,0:T(8,128)(2,1)S(1)} async-done(((bf16[8,32,1152]{2,1,0:T(8,128)(2,1)}), bf16[8,32,1152]{2,1,0:T(8,128)(2,1)S(1)}, u32[]{:S(2)}, u32[]{:S(2)}) %all-to-all-start.4) | async-done | bytes 589856 | tf_op jit(solution)/shard_map/all_to_all | solution.py:215
  104.0 0.9 broadcast_in_dim.14
  104.9 3.7 %all-to-all-start.5 = ((bf16[8,32,1024]{2,1,0:T(8,128)(2,1)}), bf16[8,32,1024]{2,1,0:T(8,128)(2,1)S(1)}, u32[]{:S(2)}, u32[]{:S(2)}) async-start(bf16[8,32,1024]{2,1,0:T(8,128)(2,1)} %broadcast_in_dim.14), calls=%async_computation.5 | async-start | bytes 1048576 | tf_op jit(solution)/shard_map/all_to_all | solution.py:24
  108.6 6.2 %collective-permute-start.4 = (bf16[16,1024]{1,0:T(8,128)(2,1)S(1)}, bf16[16,1024]{1,0:T(8,128)(2,1)S(1)}, u32[]{:S(2)}, u32[]{:S(2)}) collective-permute-start(bf16[16,1024]{1,0:T(8,128)(2,1)S(1)} %broadcast_select_fusion.5), channel_id=1, source_target_pairs={{0,16},{16,0},{1,17},{17,1},{2,18},{18,2},{3,19},{19,3},{4,20},{20... | collective-permute-start | bytes 98312 | tf_op jit(solution)/shard_map/ppermute | solution.py:28
  115.0 1.2 all-to-all-done.5
  116.2 7.2 %collective-permute-start.7 = (bf16[256,1024]{1,0:T(8,128)(2,1)S(1)}, bf16[256,1024]{1,0:T(8,128)(2,1)S(1)}, u32[]{:S(2)}, u32[]{:S(2)}) collective-permute-start(bf16[256,1024]{1,0:T(8,128)(2,1)S(1)} %bitcast.41), channel_id=1, source_target_pairs={{0,16},{16,0},{1,17},{17,1},{2,18},{18,2},{3,19},{19,3},{4,20},{20... | collective-permute-start | bytes 1572872 | tf_op jit(solution)/shard_map/ppermute | solution.py:28
  124.0 0.7 fusion.5
  124.9 2.1 %add_convert_fusion = bf16[1024,1024]{1,0:T(8,128)(2,1)} fusion(f32[1024,1024]{1,0:T(8,128)S(1)} %fusion.5, bf16[256,1024]{1,0:T(8,128)(2,1)S(1)} %collective-permute-done.6, bf16[256,1024]{1,0:T(8,128)(2,1)S(1)} %collective-permute-done.7), kind=kOutput, calls=%fused_computation | convolution fusion | flops 538968064 | bytes 7340032 | tf_op jit(solution)/shard_map/dot_general | solution.py:236
  (65 shorter events, 3.9 us)
Async XLA Ops:
  0.6 6.6 %copy-start = (bf16[8,8,256,128]{3,2,1,0:T(8,128)(2,1)S(1)}, bf16[8,8,256,128]{3,2,1,0:T(8,128)(2,1)}, u32[]{:S(2)}) copy-start(bf16[8,8,256,128]{3,2,1,0:T(8,128)(2,1)} %ko.1) | copy-start | bytes 12582916
  3.9 4.8 %copy-start.3 = (bf16[8,4,1024]{2,1,0:T(4,128)(2,1)S(1)}, bf16[8,4,1024]{2,1,0:T(4,128)(2,1)}, u32[]{:S(2)}) copy-start(bf16[8,4,1024]{2,1,0:T(4,128)(2,1)} %param.9) | copy-start | bytes 196612
  3.9 10.1 %copy-start.8 = (s32[8]{0:T(128)S(1)}, s32[8]{0:T(128)}, u32[]{:S(2)}) copy-start(s32[8]{0:T(128)} %param.14) | copy-start | bytes 100
  3.9 10.2 %copy-start.5 = (bf16[8,4,1024]{2,1,0:T(4,128)(2,1)S(1)}, bf16[8,4,1024]{2,1,0:T(4,128)(2,1)}, u32[]{:S(2)}) copy-start(bf16[8,4,1024]{2,1,0:T(4,128)(2,1)} %param.11) | copy-start | bytes 196612
  3.9 10.2 %copy-start.6 = (bf16[8,4,1024]{2,1,0:T(4,128)(2,1)S(1)}, bf16[8,4,1024]{2,1,0:T(4,128)(2,1)}, u32[]{:S(2)}) copy-start(bf16[8,4,1024]{2,1,0:T(4,128)(2,1)} %param.10) | copy-start | bytes 196612
  3.9 19.9 %collective-permute-start.1 = (bf16[4,8,256,128]{3,2,1,0:T(8,128)(2,1)}, bf16[4,8,256,128]{3,2,1,0:T(8,128)(2,1)S(1)}, u32[]{:S(2)}, u32[]{:S(2)}) collective-permute-start(bf16[4,8,256,128]{3,2,1,0:T(8,128)(2,1)} %constant_dynamic-slice_fusion.1), channel_id=1, source_target_pairs={{0,16},{16,0},{1,17},{17,1},{2,18},{18,2},{3,19},{19,3},{4,20},{20... | collective-permute-start | bytes 6291464 | tf_op jit(solution)/shard_map/ppermute | solution.py:28
  8.7 15.1 %collective-permute-start = (bf16[4,8,256,128]{3,2,1,0:T(8,128)(2,1)}, bf16[4,8,256,128]{3,2,1,0:T(8,128)(2,1)}, u32[]{:S(2)}, u32[]{:S(2)}) collective-permute-start(bf16[4,8,256,128]{3,2,1,0:T(8,128)(2,1)} %constant_dynamic-slice_fusion.2), channel_id=1, source_target_pairs={{0,16},{16,0},{1,17},{17,1},{2,18},{18,2},{3,19},{19,3},{4,20},{20... | collective-permute-start | bytes 6291464 | tf_op jit(solution)/shard_map/ppermute | solution.py:28
  9.7 14.2 %all-to-all-start = ((bf16[16,4,32,128]{3,2,1,0:T(8,128)(2,1)}), bf16[16,4,32,128]{3,2,1,0:T(8,128)(2,1)S(1)}, u32[]{:S(2)}, u32[]{:S(2)}) async-start(bf16[16,4,32,128]{3,2,1,0:T(8,128)(2,1)} %bitcast.6), calls=%async_computation | async-start | bytes 1048576 | tf_op jit(solution)/shard_map/all_to_all | solution.py:171
  23.9 2.2 %copy-start.1 = (bf16[8,8,256,128]{3,2,1,0:T(8,128)(2,1)S(1)}, bf16[8,8,256,128]{3,2,1,0:T(8,128)(2,1)}, u32[]{:S(2)}) copy-start(bf16[8,8,256,128]{3,2,1,0:T(8,128)(2,1)} %ko.1) | copy-start | bytes 12582916
  26.1 2.2 %copy-start.2 = (bf16[8,8,256,128]{3,2,1,0:T(8,128)(2,1)S(1)}, bf16[8,8,256,128]{3,2,1,0:T(8,128)(2,1)}, u32[]{:S(2)}) copy-start(bf16[8,8,256,128]{3,2,1,0:T(8,128)(2,1)} %vo.1) | copy-start | bytes 12582916
  28.3 15.0 %copy-start.7 = (f32[1024]{0:T(1024)S(1)}, f32[1024]{0:T(1024)}, u32[]{:S(2)}) copy-start(f32[1024]{0:T(1024)} %param.15) | copy-start | bytes 12292
  39.7 12.7 %all-to-all-start.1 = ((bf16[8,272,128]{2,1,0:T(8,128)(2,1)}), bf16[8,272,128]{2,1,0:T(8,128)(2,1)S(1)}, u32[]{:S(2)}, u32[]{:S(2)}) async-start(bf16[8,272,128]{2,1,0:T(8,128)(2,1)} %attend.1), calls=%async_computation.1 | async-start | bytes 1114112 | tf_op jit(solution)/shard_map/all_to_all | solution.py:183
  43.3 10.1 %collective-permute-start.2 = (f32[1024]{0:T(1024)S(1)}, f32[1024]{0:T(1024)S(1)}, u32[]{:S(2)}, u32[]{:S(2)}) collective-permute-start(f32[1024]{0:T(1024)S(1)} %copy-done.7), channel_id=1, source_target_pairs={{0,16},{16,0},{1,17},{17,1},{2,18},{18,2},{3,19},{19,3},{4,20},{20... | collective-permute-start | bytes 12296 | tf_op jit(solution)/shard_map/ppermute | solution.py:28
  54.2 15.3 %all-to-all-start.2 = ((bf16[4,2,16,1024]{3,2,1,0:T(8,128)(2,1)}), bf16[4,2,16,1024]{3,2,1,0:T(8,128)(2,1)S(1)}, u32[]{:S(2)}, u32[]{:S(2)}) async-start(bf16[4,2,16,1024]{3,2,1,0:T(8,128)(2,1)} %broadcast_in_dim.12), calls=%async_computation.2 | async-start | bytes 524288 | tf_op jit(solution)/shard_map/all_to_all | solution.py:24
  61.4 27.7 %collective-permute-start.3 = (bf16[1024,1024]{1,0:T(8,128)(2,1)}, bf16[1024,1024]{1,0:T(8,128)(2,1)}, u32[]{:S(2)}, u32[]{:S(2)}) collective-permute-start(bf16[1024,1024]{1,0:T(8,128)(2,1)} %param.16), channel_id=1, source_target_pairs={{0,16},{16,0},{1,17},{17,1},{2,18},{18,2},{3,19},{19,3},{4,20},{20... | collective-permute-start | bytes 6291464 | tf_op jit(solution)/shard_map/ppermute | solution.py:28
  70.6 15.4 %all-to-all-start.3 = ((bf16[4,4,2,16,1024]{4,3,1,2,0:T(8,128)(2,1)}), bf16[4,4,2,16,1024]{4,3,1,2,0:T(8,128)(2,1)S(1)}, u32[]{:S(2)}, u32[]{:S(2)}) async-start(bf16[4,4,2,16,1024]{4,3,1,2,0:T(8,128)(2,1)} %broadcast_in_dim.13), calls=%async_computation.3 | async-start | bytes 2097152 | tf_op jit(solution)/shard_map/all_to_all | solution.py:24
  91.5 4.4 %copy-start.4 = (bf16[32,1024]{1,0:T(8,128)(2,1)S(1)}, bf16[32,1024]{1,0:T(8,128)(2,1)}, u32[]{:S(2)}) copy-start(bf16[32,1024]{1,0:T(8,128)(2,1)} %param.17) | copy-start | bytes 196612
  92.3 11.4 %all-to-all-start.4 = ((bf16[8,32,1152]{2,1,0:T(8,128)(2,1)}), bf16[8,32,1152]{2,1,0:T(8,128)(2,1)S(1)}, u32[]{:S(2)}, u32[]{:S(2)}) async-start(bf16[8,32,1152]{2,1,0:T(8,128)(2,1)} %pad_maximum_fusion), calls=%async_computation.4 | async-start | bytes 1179648 | tf_op jit(solution)/shard_map/all_to_all | solution.py:215
  95.9 6.2 %collective-permute-start.5 = (bf16[16,1024]{1,0:T(8,128)(2,1)S(1)}, bf16[16,1024]{1,0:T(8,128)(2,1)S(1)}, u32[]{:S(2)}, u32[]{:S(2)}) collective-permute-start(bf16[16,1024]{1,0:T(8,128)(2,1)S(1)} %constant_dynamic-slice_fusion), channel_id=1, source_target_pairs={{0,16},{16,0},{1,17},{17,1},{2,18},{18,2},{3,19},{19,3},{4,20},{20... | collective-permute-start | bytes 98312 | tf_op jit(solution)/shard_map/ppermute | solution.py:28
  104.9 11.3 %all-to-all-start.5 = ((bf16[8,32,1024]{2,1,0:T(8,128)(2,1)}), bf16[8,32,1024]{2,1,0:T(8,128)(2,1)S(1)}, u32[]{:S(2)}, u32[]{:S(2)}) async-start(bf16[8,32,1024]{2,1,0:T(8,128)(2,1)} %broadcast_in_dim.14), calls=%async_computation.5 | async-start | bytes 1048576 | tf_op jit(solution)/shard_map/all_to_all | solution.py:24
  108.6 14.8 %collective-permute-start.4 = (bf16[16,1024]{1,0:T(8,128)(2,1)S(1)}, bf16[16,1024]{1,0:T(8,128)(2,1)S(1)}, u32[]{:S(2)}, u32[]{:S(2)}) collective-permute-start(bf16[16,1024]{1,0:T(8,128)(2,1)S(1)} %broadcast_select_fusion.5), channel_id=1, source_target_pairs={{0,16},{16,0},{1,17},{17,1},{2,18},{18,2},{3,19},{19,3},{4,20},{20... | collective-permute-start | bytes 98312 | tf_op jit(solution)/shard_map/ppermute | solution.py:28
  114.9 9.9 %collective-permute-start.6 = (bf16[256,1024]{1,0:T(8,128)(2,1)S(1)}, bf16[256,1024]{1,0:T(8,128)(2,1)S(1)}, u32[]{:S(2)}, u32[]{:S(2)}) collective-permute-start(bf16[256,1024]{1,0:T(8,128)(2,1)S(1)} %bitcast.45), channel_id=1, source_target_pairs={{0,16},{16,0},{1,17},{17,1},{2,18},{18,2},{3,19},{19,3},{4,20},{20... | collective-permute-start | bytes 1572872 | tf_op jit(solution)/shard_map/ppermute | solution.py:28
  116.2 8.8 %collective-permute-start.7 = (bf16[256,1024]{1,0:T(8,128)(2,1)S(1)}, bf16[256,1024]{1,0:T(8,128)(2,1)S(1)}, u32[]{:S(2)}, u32[]{:S(2)}) collective-permute-start(bf16[256,1024]{1,0:T(8,128)(2,1)S(1)} %bitcast.41), channel_id=1, source_target_pairs={{0,16},{16,0},{1,17},{17,1},{2,18},{18,2},{3,19},{19,3},{4,20},{20... | collective-permute-start | bytes 1572872 | tf_op jit(solution)/shard_map/ppermute | solution.py:28

commit v3 on v2

v3 whole, which is shorter than its diff:
```python
import functools
import math

import jax
import jax.numpy as jnp
from jax import lax
from jax.experimental import pallas as pl
from jax.experimental.pallas import tpu as pltpu
from jax.sharding import Mesh
from jax.sharding import PartitionSpec as P

TP = ("ch", "c")
TILE = 16


def gather(x, axis):
    n = lax.axis_size(axis)
    return lax.all_to_all(jnp.broadcast_to(x[None], (n,) + x.shape), axis, 0, 0)


def shift(x, axis, k):
    n = lax.axis_size(axis)
    return lax.ppermute(x, axis, [(j, (j + k) % n) for j in range(n)])


def swap(x):
    return lax.ppermute(x, "c", [(0, 1), (1, 0)])


def attend_kernel(steps, meta, q_ref, ko, vo, ks, vs, new_ref, out_ref, buf, lse_ref, sems):
    half = buf.shape[1]
    kv_heads, block, head_size = buf.shape[2:]
    q_rows = q_ref.shape[1] * q_ref.shape[3]
    scale = math.log2(math.e) / math.sqrt(head_size)
    core = meta[0]

    def copies(i):
        out = []
        for n, ref in enumerate((ko, ks, vo, vs)):
            src = ref.at[core * half + i]
            out.append(pltpu.make_async_copy(src, buf.at[n, i], sems.at[n, i]))
        return out

    for i in range(half):
        for copy in copies(i):
            copy.start()

    row = lax.broadcasted_iota(jnp.int32, (q_rows, block), 0)
    lane = lax.broadcasted_iota(jnp.int32, (q_rows, block), 1)
    step_of = lax.rem(row, steps) + 1
    column = lax.broadcasted_iota(jnp.int32, (q_rows, 128), 1)
    nt = (((1,), (1,)), ((), ()))
    lse_ref[...] = jnp.zeros_like(lse_ref)

    def one(i):
        length = meta[3 + core * half + i]
        c = copies(i)

        def insert(n, base):
            for j in range(steps):
                place = length + j - base

                @pl.when((place >= 0) & (place < block))
                def _(place=place, j=j):
                    start = pl.multiple_of((place // TILE) * TILE, TILE)
                    hit = lax.broadcasted_iota(jnp.int32, (TILE, head_size), 0) == place - start
                    for k in range(kv_heads):
                        slab = buf[n, i, k, pl.ds(start, TILE), :].astype(jnp.float32)
                        fresh = new_ref[core * half + i, n // 2, k, j : j + 1, :]
                        buf[n, i, k, pl.ds(start, TILE), :] = jnp.where(hit, fresh, slab).astype(
                            jnp.bfloat16
                        )

        c[0].wait()
        c[1].wait()
        insert(0, meta[1])
        insert(1, meta[2])
        limit = length + step_of
        valid_o = lane + meta[1] < limit
        valid_s = lane + meta[2] < limit
        qk = []
        for k in range(kv_heads):
            q = q_ref[k, :, i].reshape(q_rows, head_size)
            so = lax.dot_general(q, buf[0, i, k], nt, preferred_element_type=jnp.float32)
            ss = lax.dot_general(q, buf[1, i, k], nt, preferred_element_type=jnp.float32)
            qk.append((so, ss))
        pr = []
        for k in range(kv_heads):
            so, ss = qk[k]
            so = jnp.where(valid_o, so * scale, -1e30)
            ss = jnp.where(valid_s, ss * scale, -1e30)
            top = jnp.max(jnp.maximum(so, ss), axis=1, keepdims=True)
            po = jnp.exp2(so - top)
            ps = jnp.exp2(ss - top)
            total = jnp.sum(po + ps, axis=1, keepdims=True)
            pr.append((top, total, po.astype(jnp.bfloat16), ps.astype(jnp.bfloat16)))
        c[2].wait()
        c[3].wait()
        insert(2, meta[1])
        insert(3, meta[2])
        for k in range(kv_heads):
            top, total, po, ps = pr[k]
            acc = jnp.dot(po, buf[2, i, k], preferred_element_type=jnp.float32)
            acc += jnp.dot(ps, buf[3, i, k], preferred_element_type=jnp.float32)
            out_ref[k, i * q_rows : (i + 1) * q_rows, :] = (acc / total).astype(jnp.bfloat16)
            lse = jnp.where(top > -1e29, top + jnp.log2(total), -1e30)
            lse_ref[k, :q_rows, :] = jnp.where(column == i, lse, lse_ref[k, :q_rows, :])

    for i in range(half):
        one(i)

    for k in range(kv_heads):
        x = lse_ref[k].T[:half]
        a = x.astype(jnp.bfloat16).astype(jnp.float32)
        b = (x - a).astype(jnp.bfloat16).astype(jnp.float32)
        c = x - a - b
        rows = jnp.concatenate([a, b, c, jnp.zeros((TILE - 3 * half, 128), jnp.float32)], 0)
        out_ref[k, half * q_rows :, :] = rows.astype(jnp.bfloat16)


def attend(steps, meta, heads, own_k, own_v, sib_k, sib_v, fresh):
    kv_heads, share, half, rows, head_size = heads.shape
    block = own_k.shape[2]
    q_rows = share * rows
    out_rows = half * q_rows + TILE
    vmem = pl.BlockSpec(memory_space=pltpu.VMEM)
    hbm = pl.BlockSpec(memory_space=pl.ANY)
    return pl.pallas_call(
        functools.partial(attend_kernel, steps),
        in_specs=[pl.BlockSpec(memory_space=pltpu.SMEM), vmem, hbm, hbm, hbm, hbm, vmem],
        out_specs=vmem,
        scratch_shapes=[
            pltpu.VMEM((4, half, kv_heads, block, head_size), jnp.bfloat16),
            pltpu.VMEM((kv_heads, 128, 128), jnp.float32),
            pltpu.SemaphoreType.DMA((4, half)),
        ],
        out_shape=jax.ShapeDtypeStruct((kv_heads, out_rows, head_size), jnp.bfloat16),
        compiler_params=pltpu.CompilerParams(vmem_limit_bytes=60 * 1024 * 1024),
        cost_estimate=pl.CostEstimate(
            flops=half * kv_heads * q_rows * 2 * block * head_size * 4,
            bytes_accessed=half * kv_heads * block * head_size * 8,
            transcendentals=half * kv_heads * q_rows * 2 * block,
        ),
        name="attend",
    )(meta, heads, own_k, own_v, sib_k, sib_v, fresh)


def project_kernel(place, *refs):
    blocks, (g_own, g_sib, w_own, w_sib, out_ref, own_ref, sib_ref) = refs[:-7], refs[-7:]
    hrows = blocks[0].shape[2]
    tile = w_own.shape[1]
    cols = tile * pl.num_programs(0)
    t = pl.program_id(0)

    @pl.when(t == 0)
    def _():
        for n, ref in enumerate(blocks):
            y_back, z_backs = n // 2, ((0, 1, 3), (2,))[n % 2]
            y = lax.rem(place[1] - y_back + 4, 4)
            for at, z_back in enumerate(z_backs):
                z = lax.rem(place[0] - z_back + 4, 4)
                rows = pl.ds(pl.multiple_of((z * 4 + y) * hrows, hrows), hrows)
                own_ref[rows, :] = ref[at, 0]
                sib_ref[rows, :] = ref[at, 1]
        own = own_ref[...].astype(jnp.float32) * (1.0 / g_own[...])
        sib = sib_ref[...].astype(jnp.float32) * (1.0 / g_sib[...])
        sq = jnp.sum(own * own + sib * sib, axis=1, keepdims=True)
        a = sq.astype(jnp.bfloat16).astype(jnp.float32)
        b = (sq - a).astype(jnp.bfloat16).astype(jnp.float32)
        lane = lax.broadcasted_iota(jnp.int32, (sq.shape[0], 128), 1)
        pieces = jnp.where(lane == 0, a, jnp.where(lane == 1, b, sq - a - b))
        out_ref[:, cols:] = jnp.where(lane < 3, pieces, 0.0).astype(jnp.bfloat16)

    acc = jnp.dot(own_ref[...], w_own[...], preferred_element_type=jnp.float32)
    acc += jnp.dot(sib_ref[...], w_sib[...], preferred_element_type=jnp.float32)
    out_ref[:, pl.ds(pl.multiple_of(t * tile, tile), tile)] = acc.astype(jnp.bfloat16)


def project(place, blocks, g_own, g_sib, w_own, w_sib):
    hrows, feats = blocks[0].shape[2:]
    cols = w_own.shape[1]
    rows = 16 * hrows
    tile = 256
    whole = lambda x: pl.BlockSpec(x.shape, lambda t, m, n=len(x.shape): (0,) * n)
    weights = pl.BlockSpec((feats, tile), lambda t, m: (0, t))
    outs = (
        jax.ShapeDtypeStruct((rows, cols + 128), jnp.bfloat16),
        jax.ShapeDtypeStruct((rows, feats), jnp.bfloat16),
        jax.ShapeDtypeStruct((rows, feats), jnp.bfloat16),
    )
    return pl.pallas_call(
        project_kernel,
        grid_spec=pltpu.PrefetchScalarGridSpec(
            num_scalar_prefetch=1,
            grid=(cols // tile,),
            in_specs=[whole(x) for x in blocks] + [whole(g_own), whole(g_sib), weights, weights],
            out_specs=tuple(whole(x) for x in outs),
        ),
        out_shape=outs,
        compiler_params=pltpu.CompilerParams(
            dimension_semantics=("arbitrary",), vmem_limit_bytes=40 * 1024 * 1024
        ),
        cost_estimate=pl.CostEstimate(
            flops=rows * feats * cols * 4, bytes_accessed=feats * cols * 4, transcendentals=0
        ),
        name="project",
    )(place, *blocks, g_own, g_sib, w_own, w_sib)


def per_device(
    queries,
    new_keys,
    new_values,
    cache_keys,
    cache_values,
    lengths,
    norm_gain,
    draft_weight,
    next_hidden,
):
    chips, cores = lax.axis_size("ch"), lax.axis_size("c")
    chip, core = lax.axis_index("ch"), lax.axis_index("c")
    zh, ny = lax.axis_size("zh"), lax.axis_size("y")
    seqs, steps, feats = queries.shape
    kv_heads, block, head_size = (cache_keys.shape[1], cache_keys.shape[2], cache_keys.shape[3])
    mine = feats // head_size
    width = feats * chips * cores
    half = seqs // cores
    hrows = half * steps
    cols = draft_weight.shape[1]
    other = 1 - core

    packed = queries.reshape(cores, half, steps, mine, head_size).transpose(0, 1, 3, 2, 4)
    packed = packed.reshape(cores, half, mine * steps, head_size)
    spread = jnp.broadcast_to(packed[None], (chips,) + packed.shape)
    spread = spread.reshape((chips * cores,) + packed.shape[1:])

    sib_k = swap(cache_keys)
    sib_v = swap(cache_values)
    sib_w = swap(draft_weight)
    sib_gain = swap(norm_gain)
    sib_hidden = swap(lax.dynamic_slice_in_dim(next_hidden, other * hrows, hrows, 0))
    own_hidden = lax.dynamic_slice_in_dim(next_hidden, core * hrows, hrows, 0)

    heads = lax.all_to_all(spread, TP, 0, 0).reshape(
        kv_heads, cores, half, mine * steps, head_size
    )
    place = (chip * cores + core) * block
    sib_place = (chip * cores + other) * block
    meta = jnp.concatenate([jnp.stack([core, place, sib_place]).astype(jnp.int32), lengths])
    fresh = jnp.stack([new_keys, new_values], axis=1).reshape(
        seqs, 2, steps, kv_heads, head_size
    )
    fresh = fresh.transpose(0, 1, 3, 2, 4).astype(jnp.float32)
    sent = attend(steps, meta, heads, cache_keys, cache_values, sib_k, sib_v, fresh)

    got = lax.all_to_all(sent, "ch", 0, 0)
    q_rows = cores * mine * steps
    outs = got[:, : half * q_rows].astype(jnp.float32).reshape(chips, half, q_rows, head_size)
    lse = got[:, half * q_rows : half * q_rows + 3 * half, :q_rows].astype(jnp.float32)
    lse = jnp.sum(lse.reshape(chips, 3, half, q_rows), axis=1)
    factor = jnp.exp2(lse - jnp.max(lse, axis=0, keepdims=True))
    context = jnp.sum(outs * factor[..., None], axis=0) / jnp.sum(factor, axis=0)[..., None]
    context = context.reshape(half, cores, mine, steps, head_size).transpose(1, 0, 3, 2, 4)
    context = context.reshape(cores, hrows, feats)
    flat_own = lax.dynamic_index_in_dim(context, core, 0, keepdims=False)
    flat_sib = lax.dynamic_index_in_dim(context, other, 0, keepdims=False)
    raw = jnp.stack([flat_own * norm_gain[None, :], flat_sib * sib_gain[None, :]])
    raw = raw.astype(jnp.bfloat16)

    near = jnp.stack([raw, shift(raw, "zh", 1), shift(raw, "zh", 3)])
    far = shift(raw, "zh", 2)[None]
    blocks = [near, far]
    for k in (1, 2, 3):
        blocks += [shift(near, "y", k), shift(far, "y", k)]
    row_half = zh * ny * hrows
    row_count = row_half * cores
    where = jnp.stack([lax.axis_index("zh"), lax.axis_index("y")]).astype(jnp.int32)
    partial, own_raw, sib_raw = project(
        where, blocks, norm_gain[None, :], sib_gain[None, :], draft_weight, sib_w
    )
    payload = partial.reshape(chips, cores * hrows, cols + 128)
    oth_raw = swap(sib_raw)
    parts = lax.all_to_all(payload, "ch", 0, 0)
    summed = jnp.sum(parts.astype(jnp.float32), axis=0)
    meansq = jnp.sum(summed[:, cols : cols + 3], axis=1) / width
    scale = lax.rsqrt(meansq + 1e-05)[:, None]
    total = summed[:, :cols] * scale

    flip = core == 1
    hid0 = jnp.where(flip, sib_hidden, own_hidden)
    hid1 = jnp.where(flip, own_hidden, sib_hidden)
    hidden = jnp.concatenate([hid0, hid1]).astype(jnp.float32)
    grad_mine = ((total - hidden) * (scale / math.sqrt(row_count))).astype(jnp.bfloat16)
    grad_half = gather(grad_mine, "ch").reshape(row_half, cols)
    grad_other = swap(grad_half)

    pred = total.astype(jnp.bfloat16).reshape(cores, hrows, cols)
    keep = jnp.where(flip, pred[1], pred[0])
    came = swap(jnp.where(flip, pred[0], pred[1]))
    prediction = jnp.concatenate([jnp.where(flip, came, keep), jnp.where(flip, keep, came)])

    tn = (((0,), (0,)), ((), ()))
    weight_grad = lax.dot_general(own_raw, grad_half, tn, preferred_element_type=jnp.float32)
    weight_grad += lax.dot_general(oth_raw, grad_other, tn, preferred_element_type=jnp.float32)
    return (prediction, weight_grad.astype(jnp.bfloat16))


def solution(mesh):
    tp, grp = mesh.devices.shape
    fine = Mesh(mesh.devices.reshape(tp // 2, 2, 4, grp // 4), ("ch", "c", "zh", "y"))
    g = ("zh", "y")
    in_specs = (
        P(g, None, TP),
        P(g, None, None),
        P(g, None, None),
        P(g, None, TP, None),
        P(g, None, TP, None),
        P(g),
        P(TP),
        P(TP, g),
        P(TP, g),
    )
    out_specs = (P(TP, g), P(TP, g))
    return jax.shard_map(
        per_device, mesh=fine, in_specs=in_specs, out_specs=out_specs, check_vma=False
    )
```

time: 128 us -> 111 us (0.87)
  waiting for transfers between devices: 37.7 us -> 28.7 us
  local copies, waits for them, and re-layouts: 13.5 us -> 5.3 us
  matrix products: 7.42 us -> 2.82 us
  other arithmetic: 2.94 us -> 5.37 us
  Pallas kernels: 11.5 us -> 13.3 us
    ppermute x0 -> x9, starting transfers between devices: none -> 18 us  [shift(): return lax.ppermute(x, axis, [(j, (j + k) % n) for j in range(n)])]
    all_to_all x3 -> x1, waiting for transfers between devices: 17.6 us -> 2.73 us  [gather(): return lax.all_to_all(jnp.broadcast_to(x[None], (n,) + x.shape), axis, 0, 0)]
    all_to_all x3 -> x1, starting transfers between devices: 15.5 us -> 4.46 us  [gather(): return lax.all_to_all(jnp.broadcast_to(x[None], (n,) + x.shape), axis, 0, 0)]
    ppermute x0 -> x9, waiting for transfers between devices: none -> 8.21 us  [shift(): return lax.ppermute(x, axis, [(j, (j + k) % n) for j in range(n)])]
    ppermute x8, starting transfers between devices: 26 us -> 20.1 us  [swap(): return lax.ppermute(x, 'c', [(0, 1), (1, 0)])]
    dynamic_slice x2 -> x0, local copies, waits for them, and re-layouts: 4.74 us -> none  [the longest x1 3.28 us: per_device(): sib_v = swap(lax.dynamic_slice_in_dim(cache_values, other * half, half, 0))]
    dot_general x2 -> x0, matrix products: 4.6 us -> none  [the longest x1 2.3 us: per_device(): partial += jnp.dot(sib_raw, sib_w, preferred_element_type=jnp.float32)]
    unnamed x19 -> x8, local copies, waits for them, and re-layouts: 4.55 us -> 1.63 us
  transfers between devices with their start and end apart: 14 -> 21, of which waited for: 8 -> 8; matrix products, arithmetic and copies ran while one was open for 7% -> 7% of each run, Pallas kernels for 0% -> 0%
where the time goes in v3:
time: 111 us; the launch traced here: 110 us
  starting transfers between devices  54 us (49%)
  waiting for transfers between devices  28.7 us (26%)
  Pallas kernels  13.3 us (12%)
  other arithmetic  5.37 us (5%)
  local copies, waits for them, and re-layouts  5.3 us (5%)
  matrix products  2.82 us (3%)
    ppermute x8, starting transfers between devices, swap(): return lax.ppermute(x, 'c', [(0, 1), (1, 0)])  20.1 us
    ppermute x9, starting transfers between devices, shift(): return lax.ppermute(x, axis, [(j, (j + k) % n) for j in range(n)])  18 us
    ppermute x9, waiting for transfers between devices, shift(): return lax.ppermute(x, axis, [(j, (j + k) % n) for j in range(n)])  8.21 us
    pallas_call x1, Pallas kernels, attend(): pl.pallas_call(functools.partial(attend_kernel, steps), in_specs=[pl.Bloc...  7.7 us
    all_to_all x1, waiting for transfers between devices, per_device(): got = lax.all_to_all(sent, 'ch', 0, 0)  7.66 us
    all_to_all x1, waiting for transfers between devices, per_device(): lax.all_to_all(spread, TP, 0, 0)  6.82 us
    pallas_call x1, Pallas kernels, project(): pl.pallas_call(project_kernel, grid_spec=pltpu.PrefetchScalarGridSpec(num...  5.56 us
    all_to_all x1, starting transfers between devices, gather(): return lax.all_to_all(jnp.broadcast_to(x[None], (n,) + x.shape), axis, 0, 0)  4.46 us
  transfers between devices with their start and end apart: 21, of which 8 were waited for; matrix products, arithmetic and copies ran while one was open for 7% of the time, Pallas kernels for 0%

profile of v3, /device:TPU:1, one launch (start us, length us, event | category | flops | bytes accessed | tf_op | source)
XLA Modules:
  0.0 110.3 jit_solution(1639347303585428020)
XLA Ops:
  0.6 3.3 %collective-permute-start = (bf16[8,8,256,128]{3,2,1,0:T(8,128)(2,1)}, bf16[8,8,256,128]{3,2,1,0:T(8,128)(2,1)}, u32[]{:S(2)}, u32[]{:S(2)}) collective-permute-start(bf16[8,8,256,128]{3,2,1,0:T(8,128)(2,1)} %ko.1), channel_id=1, source_target_pairs={{0,16},{16,0},{1,17},{17,1},{2,18},{18,2},{3,19},{19,3},{4,20},{20... | collective-permute-start | bytes 12582920 | tf_op jit(solution)/shard_map/ppermute | solution.py:27
  4.1 1.7 %broadcast_in_dim.13 = bf16[8,2,4,32,128]{4,3,2,1,0:T(8,128)(2,1)} broadcast(bf16[2,4,32,128]{3,2,1,0:T(8,128)(2,1)} %bitcast.48), dimensions={1,2,3,4} | broadcast | bytes 589824 | tf_op jit(solution)/shard_map/broadcast_in_dim | solution.py:235
  5.8 4.3 %all-to-all-start = ((bf16[16,4,32,128]{3,2,1,0:T(8,128)(2,1)}), bf16[16,4,32,128]{3,2,1,0:T(8,128)(2,1)S(1)}, u32[]{:S(2)}, u32[]{:S(2)}) async-start(bf16[16,4,32,128]{3,2,1,0:T(8,128)(2,1)} %bitcast.8), calls=%async_computation | async-start | bytes 1048576 | tf_op jit(solution)/shard_map/all_to_all | solution.py:245
  10.1 1.3 %pad_add_fusion.1.meta = s32[11]{0:T(128)} fusion(s32[8]{0:T(128)} %param.14, s32[1]{0:T(128)} %bitcast.4, s32[1]{0:T(128)} %bitcast.3, s32[1]{0:T(128)} %bitcast.2), kind=kLoop, calls=%fused_computation.25 | loop fusion | flops 33 | bytes 88 | tf_op jit(solution)/shard_map/concatenate | solution.py:250
  11.4 1.7 %convert_bitcast_fusion.new_ref = f32[8,2,8,4,128]{4,3,2,1,0:T(4,128)} fusion(bf16[8,1,4,8,128]{4,2,3,1,0:T(4,128)(2,1)} %bitcast.49, bf16[8,1,4,8,128]{4,2,3,1,0:T(4,128)(2,1)} %bitcast.50), kind=kLoop, calls=%fused_computation.3 | loop fusion | flops 131072 | bytes 393216 | tf_op jit(solution)/shard_map/convert_element_type | solution.py:254
  13.1 6.8 %all-to-all-done = bf16[16,4,32,128]{3,2,1,0:T(8,128)(2,1)S(1)} async-done(((bf16[16,4,32,128]{3,2,1,0:T(8,128)(2,1)}), bf16[16,4,32,128]{3,2,1,0:T(8,128)(2,1)S(1)}, u32[]{:S(2)}, u32[]{:S(2)}) %all-to-all-start) | async-done | bytes 524320 | tf_op jit(solution)/shard_map/all_to_all | solution.py:245
  19.9 0.8 copy-done.3
  20.8 7.7 %attend.1 = bf16[8,272,128]{2,1,0:T(8,128)(2,1)} custom-call(s32[11]{0:T(128)} %pad_add_fusion.1.meta, bf16[8,2,4,32,128]{4,3,2,1,0:T(8,128)(2,1)} %bitcast.43, bf16[8,8,256,128]{3,2,1,0:T(8,128)(2,1)} %ko.1, bf16[8,8,256,128]{3,2,1,0:T(8,128)(2,1)} %vo.1, bf16[8,8,256,128]{3,2,1,0:T(8,128)(2,1)} %collective-permute-done.ks, ...), custom_call_target="tpu_custom_call" | custom-call | flops 536870912 | bytes 8388608 | tf_op jit(solution)/shard_map/attend/pallas_call | solution.py:128
  28.5 3.5 %all-to-all-start.1 = ((bf16[8,272,128]{2,1,0:T(8,128)(2,1)}), bf16[8,272,128]{2,1,0:T(8,128)(2,1)S(1)}, u32[]{:S(2)}, u32[]{:S(2)}) async-start(bf16[8,272,128]{2,1,0:T(8,128)(2,1)} %attend.1), calls=%async_computation.1 | async-start | bytes 1114112 | tf_op jit(solution)/shard_map/all_to_all | solution.py:257
  32.1 1.4 %collective-permute-start.12 = (bf16[1024,1024]{1,0:T(8,128)(2,1)S(1)}, bf16[1024,1024]{1,0:T(8,128)(2,1)}, u32[]{:S(2)}, u32[]{:S(2)}) collective-permute-start(bf16[1024,1024]{1,0:T(8,128)(2,1)S(1)} %copy-done), channel_id=1, source_target_pairs={{0,16},{16,0},{1,17},{17,1},{2,18},{18,2},{3,19},{19,3},{4,20},{20... | collective-permute-start | bytes 6291464 | tf_op jit(solution)/shard_map/ppermute | solution.py:27
  33.5 7.7 %all-to-all-done.1 = bf16[8,272,128]{2,1,0:T(8,128)(2,1)S(1)} async-done(((bf16[8,272,128]{2,1,0:T(8,128)(2,1)}), bf16[8,272,128]{2,1,0:T(8,128)(2,1)S(1)}, u32[]{:S(2)}, u32[]{:S(2)}) %all-to-all-start.1) | async-done | bytes 557088 | tf_op jit(solution)/shard_map/all_to_all | solution.py:257
  42.2 3.2 %collective-permute-start.3 = (bf16[2,16,1024]{2,1,0:T(8,128)(2,1)S(1)}, bf16[2,16,1024]{2,1,0:T(8,128)(2,1)S(1)}, u32[]{:S(2)}, u32[]{:S(2)}) collective-permute-start(bf16[2,16,1024]{2,1,0:T(8,128)(2,1)S(1)} %pad_maximum_fusion.1), channel_id=1, source_target_pairs={{0,4},{4,8},{8,12},{12,0},{1,5},{5,9},{9,13},{13,1},{2,6},{6,10},{... | collective-permute-start | bytes 196616 | tf_op jit(solution)/shard_map/ppermute | solution.py:23
  45.3 2.4 %collective-permute-start.4 = (bf16[2,16,1024]{2,1,0:T(8,128)(2,1)S(1)}, bf16[2,16,1024]{2,1,0:T(8,128)(2,1)S(1)}, u32[]{:S(2)}, u32[]{:S(2)}) collective-permute-start(bf16[2,16,1024]{2,1,0:T(8,128)(2,1)S(1)} %pad_maximum_fusion.1), channel_id=1, source_target_pairs={{0,12},{4,0},{8,4},{12,8},{1,13},{5,1},{9,5},{13,9},{2,14},{6,2},{... | collective-permute-start | bytes 196616 | tf_op jit(solution)/shard_map/ppermute | solution.py:23
  47.7 4.1 %collective-permute-start.5 = (bf16[2,16,1024]{2,1,0:T(8,128)(2,1)S(1)}, bf16[2,16,1024]{2,1,0:T(8,128)(2,1)S(1)}, u32[]{:S(2)}, u32[]{:S(2)}) collective-permute-start(bf16[2,16,1024]{2,1,0:T(8,128)(2,1)S(1)} %pad_maximum_fusion.1), channel_id=1, source_target_pairs={{0,8},{4,12},{8,0},{12,4},{1,9},{5,13},{9,1},{13,5},{2,10},{6,14},... | collective-permute-start | bytes 196616 | tf_op jit(solution)/shard_map/ppermute | solution.py:23
  51.9 3.1 %collective-permute-start.10 = (bf16[3,2,16,1024]{3,2,1,0:T(8,128)(2,1)S(1)}, bf16[3,2,16,1024]{3,2,1,0:T(8,128)(2,1)S(1)}, u32[]{:S(2)}, u32[]{:S(2)}) collective-permute-start(bf16[3,2,16,1024]{3,2,1,0:T(8,128)(2,1)S(1)} %pad_maximum_fusion.refs_0_), channel_id=1, source_target_pairs={{0,3},{1,0},{2,1},{3,2},{4,7},{5,4},{6,5},{7,6},{8,11},{9,8},{10,9... | collective-permute-start | bytes 589832 | tf_op jit(solution)/shard_map/ppermute | solution.py:23
  55.0 2.0 %collective-permute-start.8 = (bf16[3,2,16,1024]{3,2,1,0:T(8,128)(2,1)S(1)}, bf16[3,2,16,1024]{3,2,1,0:T(8,128)(2,1)S(1)}, u32[]{:S(2)}, u32[]{:S(2)}) collective-permute-start(bf16[3,2,16,1024]{3,2,1,0:T(8,128)(2,1)S(1)} %pad_maximum_fusion.refs_0_), channel_id=1, source_target_pairs={{0,2},{1,3},{2,0},{3,1},{4,6},{5,7},{6,4},{7,5},{8,10},{9,11},{10,... | collective-permute-start | bytes 589832 | tf_op jit(solution)/shard_map/ppermute | solution.py:23
  58.4 4.7 %collective-permute-done.11.refs_7_ = bf16[1,2,16,1024]{3,2,1,0:T(8,128)(2,1)S(1)} collective-permute-done((bf16[1,2,16,1024]{3,2,1,0:T(8,128)(2,1)S(1)}, bf16[1,2,16,1024]{3,2,1,0:T(8,128)(2,1)S(1)}, u32[]{:S(2)}, u32[]{:S(2)}) %collective-permute-start.11) | collective-permute-done | bytes 65568 | tf_op jit(solution)/shard_map/ppermute | solution.py:23
  63.1 1.8 %collective-permute-start.9 = (bf16[1,2,16,1024]{3,2,1,0:T(8,128)(2,1)S(1)}, bf16[1,2,16,1024]{3,2,1,0:T(8,128)(2,1)S(1)}, u32[]{:S(2)}, u32[]{:S(2)}) collective-permute-start(bf16[1,2,16,1024]{3,2,1,0:T(8,128)(2,1)S(1)} %bitcast.37), channel_id=1, source_target_pairs={{0,2},{1,3},{2,0},{3,1},{4,6},{5,7},{6,4},{7,5},{8,10},{9,11},{10,... | collective-permute-start | bytes 196616 | tf_op jit(solution)/shard_map/ppermute | solution.py:23
  65.0 3.5 %collective-permute-done.9.refs_5_ = bf16[1,2,16,1024]{3,2,1,0:T(8,128)(2,1)S(1)} collective-permute-done((bf16[1,2,16,1024]{3,2,1,0:T(8,128)(2,1)S(1)}, bf16[1,2,16,1024]{3,2,1,0:T(8,128)(2,1)S(1)}, u32[]{:S(2)}, u32[]{:S(2)}) %collective-permute-start.9) | collective-permute-done | bytes 65568 | tf_op jit(solution)/shard_map/ppermute | solution.py:23
  68.5 5.6 %project.1 = (bf16[256,1152]{1,0:T(8,128)(2,1)}, bf16[256,1024]{1,0:T(8,128)(2,1)S(1)}, bf16[256,1024]{1,0:T(8,128)(2,1)S(1)}) custom-call(s32[2]{0:T(128)S(1)} %pad_add_fusion.place, bf16[3,2,16,1024]{3,2,1,0:T(8,128)(2,1)S(1)} %pad_maximum_fusion.refs_0_, bf16[1,2,16,1024]{3,2,1,0:T(8,128)(2,1)S(1)} %bitcast.38, ...), custom_call_target="tpu_custom_call" | custom-call | flops 1073741824 | bytes 4194304 | tf_op jit(solution)/shard_map/project/pallas_call | solution.py:191
  74.1 0.8 copy-done.2
  74.8 3.5 %all-to-all-start.2 = ((bf16[8,32,1152]{2,1,0:T(8,128)(2,1)}), bf16[8,32,1152]{2,1,0:T(8,128)(2,1)S(1)}, u32[]{:S(2)}, u32[]{:S(2)}) async-start(bf16[8,32,1152]{2,1,0:T(8,128)(2,1)} %bitcast.23), calls=%async_computation.2 | async-start | bytes 1179648 | tf_op jit(solution)/shard_map/all_to_all | solution.py:284
  79.2 4.5 %collective-permute-start.14 = (bf16[16,1024]{1,0:T(8,128)(2,1)S(1)}, bf16[16,1024]{1,0:T(8,128)(2,1)S(1)}, u32[]{:S(2)}, u32[]{:S(2)}) collective-permute-start(bf16[16,1024]{1,0:T(8,128)(2,1)S(1)} %constant_dynamic-slice_fusion), channel_id=1, source_target_pairs={{0,16},{16,0},{1,17},{17,1},{2,18},{18,2},{3,19},{19,3},{4,20},{20... | collective-permute-start | bytes 98312 | tf_op jit(solution)/shard_map/ppermute | solution.py:27
  83.7 0.9 collective-permute-done.14
  85.3 0.9 all-to-all-done.2
  86.5 0.9 broadcast_in_dim.33
  87.4 4.5 %all-to-all-start.3 = ((bf16[8,32,1024]{2,1,0:T(8,128)(2,1)}), bf16[8,32,1024]{2,1,0:T(8,128)(2,1)S(1)}, u32[]{:S(2)}, u32[]{:S(2)}) async-start(bf16[8,32,1024]{2,1,0:T(8,128)(2,1)} %broadcast_in_dim.33), calls=%async_computation.3 | async-start | bytes 1048576 | tf_op jit(solution)/shard_map/all_to_all | solution.py:18
  91.8 4.8 %collective-permute-start.15 = (bf16[256,1024]{1,0:T(8,128)(2,1)}, bf16[256,1024]{1,0:T(8,128)(2,1)S(1)}, u32[]{:S(2)}, u32[]{:S(2)}) collective-permute-start(bf16[256,1024]{1,0:T(8,128)(2,1)} %copy-done.2), channel_id=1, source_target_pairs={{0,16},{16,0},{1,17},{17,1},{2,18},{18,2},{3,19},{19,3},{4,20},{20... | collective-permute-start | bytes 1572872 | tf_op jit(solution)/shard_map/ppermute | solution.py:27
  96.6 2.7 %all-to-all-done.3 = bf16[8,32,1024]{2,1,0:T(8,128)(2,1)S(1)} async-done(((bf16[8,32,1024]{2,1,0:T(8,128)(2,1)}), bf16[8,32,1024]{2,1,0:T(8,128)(2,1)S(1)}, u32[]{:S(2)}, u32[]{:S(2)}) %all-to-all-start.3) | async-done | bytes 524320 | tf_op jit(solution)/shard_map/all_to_all | solution.py:18
  99.4 5.8 %collective-permute-start.16 = (bf16[256,1024]{1,0:T(8,128)(2,1)S(1)}, bf16[256,1024]{1,0:T(8,128)(2,1)S(1)}, u32[]{:S(2)}, u32[]{:S(2)}) collective-permute-start(bf16[256,1024]{1,0:T(8,128)(2,1)S(1)} %bitcast.41), channel_id=1, source_target_pairs={{0,16},{16,0},{1,17},{17,1},{2,18},{18,2},{3,19},{19,3},{4,20},{20... | collective-permute-start | bytes 1572872 | tf_op jit(solution)/shard_map/ppermute | solution.py:27
  105.3 1.5 %collective-permute-done.13 = bf16[16,1024]{1,0:T(8,128)(2,1)S(1)} collective-permute-done((bf16[16,1024]{1,0:T(8,128)(2,1)S(1)}, bf16[16,1024]{1,0:T(8,128)(2,1)S(1)}, u32[]{:S(2)}, u32[]{:S(2)}) %collective-permute-start.13) | collective-permute-done | bytes 32800 | tf_op jit(solution)/shard_map/ppermute | solution.py:27
  108.2 2.1 %add_convert_fusion = bf16[1024,1024]{1,0:T(8,128)(2,1)} fusion(f32[1024,1024]{1,0:T(8,128)S(1)} %fusion.1, bf16[256,1024]{1,0:T(8,128)(2,1)S(1)} %get-tuple-element.6, bf16[256,1024]{1,0:T(8,128)(2,1)S(1)} %bitcast.42), kind=kOutput, calls=%fused_computation | convolution fusion | flops 538968064 | bytes 7340032 | tf_op jit(solution)/shard_map/dot_general | solution.py:304
  (53 shorter events, 6.0 us)
Async XLA Ops:
  0.6 19.3 %collective-permute-start = (bf16[8,8,256,128]{3,2,1,0:T(8,128)(2,1)}, bf16[8,8,256,128]{3,2,1,0:T(8,128)(2,1)}, u32[]{:S(2)}, u32[]{:S(2)}) collective-permute-start(bf16[8,8,256,128]{3,2,1,0:T(8,128)(2,1)} %ko.1), channel_id=1, source_target_pairs={{0,16},{16,0},{1,17},{17,1},{2,18},{18,2},{3,19},{19,3},{4,20},{20... | collective-permute-start | bytes 12582920 | tf_op jit(solution)/shard_map/ppermute | solution.py:27
  4.0 16.0 %collective-permute-start.1 = (bf16[8,8,256,128]{3,2,1,0:T(8,128)(2,1)}, bf16[8,8,256,128]{3,2,1,0:T(8,128)(2,1)}, u32[]{:S(2)}, u32[]{:S(2)}) collective-permute-start(bf16[8,8,256,128]{3,2,1,0:T(8,128)(2,1)} %vo.1), channel_id=1, source_target_pairs={{0,16},{16,0},{1,17},{17,1},{2,18},{18,2},{3,19},{19,3},{4,20},{20... | collective-permute-start | bytes 12582920 | tf_op jit(solution)/shard_map/ppermute | solution.py:27
  5.8 14.1 %all-to-all-start = ((bf16[16,4,32,128]{3,2,1,0:T(8,128)(2,1)}), bf16[16,4,32,128]{3,2,1,0:T(8,128)(2,1)S(1)}, u32[]{:S(2)}, u32[]{:S(2)}) async-start(bf16[16,4,32,128]{3,2,1,0:T(8,128)(2,1)} %bitcast.8), calls=%async_computation | async-start | bytes 1048576 | tf_op jit(solution)/shard_map/all_to_all | solution.py:245
  19.9 0.8 copy-start.3
  20.8 11.3 %copy-start = (bf16[1024,1024]{1,0:T(8,128)(2,1)S(1)}, bf16[1024,1024]{1,0:T(8,128)(2,1)}, u32[]{:S(2)}) copy-start(bf16[1024,1024]{1,0:T(8,128)(2,1)} %refs_10_.1) | copy-start | bytes 6291460
  20.8 12.6 %copy-start.1 = (f32[1024]{0:T(1024)S(1)}, f32[1024]{0:T(1024)}, u32[]{:S(2)}) copy-start(f32[1024]{0:T(1024)} %param.15) | copy-start | bytes 12292
  28.5 12.7 %all-to-all-start.1 = ((bf16[8,272,128]{2,1,0:T(8,128)(2,1)}), bf16[8,272,128]{2,1,0:T(8,128)(2,1)S(1)}, u32[]{:S(2)}, u32[]{:S(2)}) async-start(bf16[8,272,128]{2,1,0:T(8,128)(2,1)} %attend.1), calls=%async_computation.1 | async-start | bytes 1114112 | tf_op jit(solution)/shard_map/all_to_all | solution.py:257
  32.1 25.6 %collective-permute-start.12 = (bf16[1024,1024]{1,0:T(8,128)(2,1)S(1)}, bf16[1024,1024]{1,0:T(8,128)(2,1)}, u32[]{:S(2)}, u32[]{:S(2)}) collective-permute-start(bf16[1024,1024]{1,0:T(8,128)(2,1)S(1)} %copy-done), channel_id=1, source_target_pairs={{0,16},{16,0},{1,17},{17,1},{2,18},{18,2},{3,19},{19,3},{4,20},{20... | collective-permute-start | bytes 6291464 | tf_op jit(solution)/shard_map/ppermute | solution.py:27
  33.4 8.7 %collective-permute-start.2 = (f32[1024]{0:T(1024)S(1)}, f32[1024]{0:T(1024)S(1)}, u32[]{:S(2)}, u32[]{:S(2)}) collective-permute-start(f32[1024]{0:T(1024)S(1)} %copy-done.1), channel_id=1, source_target_pairs={{0,16},{16,0},{1,17},{17,1},{2,18},{18,2},{3,19},{19,3},{4,20},{20... | collective-permute-start | bytes 12296 | tf_op jit(solution)/shard_map/ppermute | solution.py:27
  42.2 9.7 %collective-permute-start.3 = (bf16[2,16,1024]{2,1,0:T(8,128)(2,1)S(1)}, bf16[2,16,1024]{2,1,0:T(8,128)(2,1)S(1)}, u32[]{:S(2)}, u32[]{:S(2)}) collective-permute-start(bf16[2,16,1024]{2,1,0:T(8,128)(2,1)S(1)} %pad_maximum_fusion.1), channel_id=1, source_target_pairs={{0,4},{4,8},{8,12},{12,0},{1,5},{5,9},{9,13},{13,1},{2,6},{6,10},{... | collective-permute-start | bytes 196616 | tf_op jit(solution)/shard_map/ppermute | solution.py:23
  45.3 6.5 %collective-permute-start.4 = (bf16[2,16,1024]{2,1,0:T(8,128)(2,1)S(1)}, bf16[2,16,1024]{2,1,0:T(8,128)(2,1)S(1)}, u32[]{:S(2)}, u32[]{:S(2)}) collective-permute-start(bf16[2,16,1024]{2,1,0:T(8,128)(2,1)S(1)} %pad_maximum_fusion.1), channel_id=1, source_target_pairs={{0,12},{4,0},{8,4},{12,8},{1,13},{5,1},{9,5},{13,9},{2,14},{6,2},{... | collective-permute-start | bytes 196616 | tf_op jit(solution)/shard_map/ppermute | solution.py:23
  47.7 9.2 %collective-permute-start.5 = (bf16[2,16,1024]{2,1,0:T(8,128)(2,1)S(1)}, bf16[2,16,1024]{2,1,0:T(8,128)(2,1)S(1)}, u32[]{:S(2)}, u32[]{:S(2)}) collective-permute-start(bf16[2,16,1024]{2,1,0:T(8,128)(2,1)S(1)} %pad_maximum_fusion.1), channel_id=1, source_target_pairs={{0,8},{4,12},{8,0},{12,4},{1,9},{5,13},{9,1},{13,5},{2,10},{6,14},... | collective-permute-start | bytes 196616 | tf_op jit(solution)/shard_map/ppermute | solution.py:23
  51.9 16.6 %collective-permute-start.10 = (bf16[3,2,16,1024]{3,2,1,0:T(8,128)(2,1)S(1)}, bf16[3,2,16,1024]{3,2,1,0:T(8,128)(2,1)S(1)}, u32[]{:S(2)}, u32[]{:S(2)}) collective-permute-start(bf16[3,2,16,1024]{3,2,1,0:T(8,128)(2,1)S(1)} %pad_maximum_fusion.refs_0_), channel_id=1, source_target_pairs={{0,3},{1,0},{2,1},{3,2},{4,7},{5,4},{6,5},{7,6},{8,11},{9,8},{10,9... | collective-permute-start | bytes 589832 | tf_op jit(solution)/shard_map/ppermute | solution.py:23
  55.0 13.5 %collective-permute-start.6 = (bf16[3,2,16,1024]{3,2,1,0:T(8,128)(2,1)S(1)}, bf16[3,2,16,1024]{3,2,1,0:T(8,128)(2,1)S(1)}, u32[]{:S(2)}, u32[]{:S(2)}) collective-permute-start(bf16[3,2,16,1024]{3,2,1,0:T(8,128)(2,1)S(1)} %pad_maximum_fusion.refs_0_), channel_id=1, source_target_pairs={{0,1},{1,2},{2,3},{3,0},{4,5},{5,6},{6,7},{7,4},{8,9},{9,10},{10,1... | collective-permute-start | bytes 589832 | tf_op jit(solution)/shard_map/ppermute | solution.py:23
  55.0 13.5 %collective-permute-start.8 = (bf16[3,2,16,1024]{3,2,1,0:T(8,128)(2,1)S(1)}, bf16[3,2,16,1024]{3,2,1,0:T(8,128)(2,1)S(1)}, u32[]{:S(2)}, u32[]{:S(2)}) collective-permute-start(bf16[3,2,16,1024]{3,2,1,0:T(8,128)(2,1)S(1)} %pad_maximum_fusion.refs_0_), channel_id=1, source_target_pairs={{0,2},{1,3},{2,0},{3,1},{4,6},{5,7},{6,4},{7,5},{8,10},{9,11},{10,... | collective-permute-start | bytes 589832 | tf_op jit(solution)/shard_map/ppermute | solution.py:23
  56.9 6.1 %collective-permute-start.11 = (bf16[1,2,16,1024]{3,2,1,0:T(8,128)(2,1)S(1)}, bf16[1,2,16,1024]{3,2,1,0:T(8,128)(2,1)S(1)}, u32[]{:S(2)}, u32[]{:S(2)}) collective-permute-start(bf16[1,2,16,1024]{3,2,1,0:T(8,128)(2,1)S(1)} %bitcast.35), channel_id=1, source_target_pairs={{0,3},{1,0},{2,1},{3,2},{4,7},{5,4},{6,5},{7,6},{8,11},{9,8},{10,9... | collective-permute-start | bytes 196616 | tf_op jit(solution)/shard_map/ppermute | solution.py:23
  57.7 7.3 %collective-permute-start.7 = (bf16[1,2,16,1024]{3,2,1,0:T(8,128)(2,1)S(1)}, bf16[1,2,16,1024]{3,2,1,0:T(8,128)(2,1)S(1)}, u32[]{:S(2)}, u32[]{:S(2)}) collective-permute-start(bf16[1,2,16,1024]{3,2,1,0:T(8,128)(2,1)S(1)} %bitcast.36), channel_id=1, source_target_pairs={{0,1},{1,2},{2,3},{3,0},{4,5},{5,6},{6,7},{7,4},{8,9},{9,10},{10,1... | collective-permute-start | bytes 196616 | tf_op jit(solution)/shard_map/ppermute | solution.py:23
  63.1 5.4 %collective-permute-start.9 = (bf16[1,2,16,1024]{3,2,1,0:T(8,128)(2,1)S(1)}, bf16[1,2,16,1024]{3,2,1,0:T(8,128)(2,1)S(1)}, u32[]{:S(2)}, u32[]{:S(2)}) collective-permute-start(bf16[1,2,16,1024]{3,2,1,0:T(8,128)(2,1)S(1)} %bitcast.37), channel_id=1, source_target_pairs={{0,2},{1,3},{2,0},{3,1},{4,6},{5,7},{6,4},{7,5},{8,10},{9,11},{10,... | collective-permute-start | bytes 196616 | tf_op jit(solution)/shard_map/ppermute | solution.py:23
  74.1 0.8 copy-start.2
  74.8 11.4 %all-to-all-start.2 = ((bf16[8,32,1152]{2,1,0:T(8,128)(2,1)}), bf16[8,32,1152]{2,1,0:T(8,128)(2,1)S(1)}, u32[]{:S(2)}, u32[]{:S(2)}) async-start(bf16[8,32,1152]{2,1,0:T(8,128)(2,1)} %bitcast.23), calls=%async_computation.2 | async-start | bytes 1179648 | tf_op jit(solution)/shard_map/all_to_all | solution.py:284
  79.2 5.4 %collective-permute-start.14 = (bf16[16,1024]{1,0:T(8,128)(2,1)S(1)}, bf16[16,1024]{1,0:T(8,128)(2,1)S(1)}, u32[]{:S(2)}, u32[]{:S(2)}) collective-permute-start(bf16[16,1024]{1,0:T(8,128)(2,1)S(1)} %constant_dynamic-slice_fusion), channel_id=1, source_target_pairs={{0,16},{16,0},{1,17},{17,1},{2,18},{18,2},{3,19},{19,3},{4,20},{20... | collective-permute-start | bytes 98312 | tf_op jit(solution)/shard_map/ppermute | solution.py:27
  87.4 12.0 %all-to-all-start.3 = ((bf16[8,32,1024]{2,1,0:T(8,128)(2,1)}), bf16[8,32,1024]{2,1,0:T(8,128)(2,1)S(1)}, u32[]{:S(2)}, u32[]{:S(2)}) async-start(bf16[8,32,1024]{2,1,0:T(8,128)(2,1)} %broadcast_in_dim.33), calls=%async_computation.3 | async-start | bytes 1048576 | tf_op jit(solution)/shard_map/all_to_all | solution.py:18
  91.8 15.6 %collective-permute-start.15 = (bf16[256,1024]{1,0:T(8,128)(2,1)}, bf16[256,1024]{1,0:T(8,128)(2,1)S(1)}, u32[]{:S(2)}, u32[]{:S(2)}) collective-permute-start(bf16[256,1024]{1,0:T(8,128)(2,1)} %copy-done.2), channel_id=1, source_target_pairs={{0,16},{16,0},{1,17},{17,1},{2,18},{18,2},{3,19},{19,3},{4,20},{20... | collective-permute-start | bytes 1572872 | tf_op jit(solution)/shard_map/ppermute | solution.py:27
  99.4 8.0 %collective-permute-start.16 = (bf16[256,1024]{1,0:T(8,128)(2,1)S(1)}, bf16[256,1024]{1,0:T(8,128)(2,1)S(1)}, u32[]{:S(2)}, u32[]{:S(2)}) collective-permute-start(bf16[256,1024]{1,0:T(8,128)(2,1)S(1)} %bitcast.41), channel_id=1, source_target_pairs={{0,16},{16,0},{1,17},{17,1},{2,18},{18,2},{3,19},{19,3},{4,20},{20... | collective-permute-start | bytes 1572872 | tf_op jit(solution)/shard_map/ppermute | solution.py:27
  105.2 1.6 %collective-permute-start.13 = (bf16[16,1024]{1,0:T(8,128)(2,1)S(1)}, bf16[16,1024]{1,0:T(8,128)(2,1)S(1)}, u32[]{:S(2)}, u32[]{:S(2)}) collective-permute-start(bf16[16,1024]{1,0:T(8,128)(2,1)S(1)} %broadcast_select_fusion.5), channel_id=1, source_target_pairs={{0,16},{16,0},{1,17},{17,1},{2,18},{18,2},{3,19},{19,3},{4,20},{20... | collective-permute-start | bytes 98312 | tf_op jit(solution)/shard_map/ppermute | solution.py:27

commit v4 on v3

--- a/solution.py
+++ b/solution.py
@@ -16,6 +16,14 @@
 def gather(x, axis):
     n = lax.axis_size(axis)
     return lax.all_to_all(jnp.broadcast_to(x[None], (n,) + x.shape), axis, 0, 0)
+
+
+def in_hbm(x):
+    return pltpu.with_memory_space_constraint(x, pltpu.HBM)
+
+
+def in_vmem(x):
+    return pltpu.with_memory_space_constraint(x, pltpu.VMEM)
 
 
 def shift(x, axis, k):
@@ -135,76 +143,82 @@
             pltpu.SemaphoreType.DMA((4, half)),
         ],
         out_shape=jax.ShapeDtypeStruct((kv_heads, out_rows, head_size), jnp.bfloat16),
-        compiler_params=pltpu.CompilerParams(vmem_limit_bytes=60 * 1024 * 1024),
+        compiler_params=pltpu.CompilerParams(vmem_limit_bytes=28 * 1024 * 1024),
         cost_estimate=pl.CostEstimate(
             flops=half * kv_heads * q_rows * 2 * block * head_size * 4,
             bytes_accessed=half * kv_heads * block * head_size * 8,
             transcendentals=half * kv_heads * q_rows * 2 * block,
         ),
         name="attend",
-    )(meta, heads, own_k, own_v, sib_k, sib_v, fresh)
-
-
-def project_kernel(place, *refs):
-    blocks, (g_own, g_sib, w_own, w_sib, out_ref, own_ref, sib_ref) = refs[:-7], refs[-7:]
+    )(meta, heads, *map(in_hbm, (own_k, own_v, sib_k, sib_v)), fresh)
+
+
+def project_kernel(tile, place, *refs):
+    blocks, refs = refs[:-10], refs[-10:]
+    g_own, g_sib, w_own, w_sib, out_ref, own_out, sib_out, own_ref, sib_ref, sems = refs
     hrows = blocks[0].shape[2]
-    tile = w_own.shape[1]
-    cols = tile * pl.num_programs(0)
-    t = pl.program_id(0)
-
-    @pl.when(t == 0)
-    def _():
-        for n, ref in enumerate(blocks):
-            y_back, z_backs = n // 2, ((0, 1, 3), (2,))[n % 2]
-            y = lax.rem(place[1] - y_back + 4, 4)
-            for at, z_back in enumerate(z_backs):
-                z = lax.rem(place[0] - z_back + 4, 4)
-                rows = pl.ds(pl.multiple_of((z * 4 + y) * hrows, hrows), hrows)
-                own_ref[rows, :] = ref[at, 0]
-                sib_ref[rows, :] = ref[at, 1]
-        own = own_ref[...].astype(jnp.float32) * (1.0 / g_own[...])
-        sib = sib_ref[...].astype(jnp.float32) * (1.0 / g_sib[...])
-        sq = jnp.sum(own * own + sib * sib, axis=1, keepdims=True)
-        a = sq.astype(jnp.bfloat16).astype(jnp.float32)
-        b = (sq - a).astype(jnp.bfloat16).astype(jnp.float32)
-        lane = lax.broadcasted_iota(jnp.int32, (sq.shape[0], 128), 1)
-        pieces = jnp.where(lane == 0, a, jnp.where(lane == 1, b, sq - a - b))
-        out_ref[:, cols:] = jnp.where(lane < 3, pieces, 0.0).astype(jnp.bfloat16)
-
-    acc = jnp.dot(own_ref[...], w_own[...], preferred_element_type=jnp.float32)
-    acc += jnp.dot(sib_ref[...], w_sib[...], preferred_element_type=jnp.float32)
-    out_ref[:, pl.ds(pl.multiple_of(t * tile, tile), tile)] = acc.astype(jnp.bfloat16)
+    feats, cols = w_own.shape
+    for n, ref in enumerate(blocks):
+        y_back, z_backs = n // 2, ((0, 1, 3), (2,))[n % 2]
+        y = lax.rem(place[1] - y_back + 4, 4)
+        for at, z_back in enumerate(z_backs):
+            z = lax.rem(place[0] - z_back + 4, 4)
+            rows = pl.ds(pl.multiple_of((z * 4 + y) * hrows, hrows), hrows)
+            own_ref[rows, :] = ref[at, 0]
+            sib_ref[rows, :] = ref[at, 1]
+    copies = [
+        pltpu.make_async_copy(own_ref, own_out, sems.at[0]),
+        pltpu.make_async_copy(sib_ref, sib_out, sems.at[1]),
+    ]
+    for copy in copies:
+        copy.start()
+    own, sib = own_ref[...], sib_ref[...]
+    for t in range(0, cols, tile):
+        acc = jnp.dot(own, w_own[:, t : t + tile], preferred_element_type=jnp.float32)
+        acc += jnp.dot(sib, w_sib[:, t : t + tile], preferred_element_type=jnp.float32)
+        out_ref[:, t : t + tile] = acc.astype(jnp.bfloat16)
+    sq = 0.0
+    for t in range(0, feats, 128):
+        a = own_ref[:, t : t + 128].astype(jnp.float32) * (1.0 / g_own[:, t : t + 128])
+        b = sib_ref[:, t : t + 128].astype(jnp.float32) * (1.0 / g_sib[:, t : t + 128])
+        sq = sq + a * a + b * b
+    sq = jnp.sum(sq, axis=1, keepdims=True)
+    a = sq.astype(jnp.bfloat16).astype(jnp.float32)
+    b = (sq - a).astype(jnp.bfloat16).astype(jnp.float32)
+    lane = lax.broadcasted_iota(jnp.int32, (sq.shape[0], 128), 1)
+    pieces = jnp.where(lane == 0, a, jnp.where(lane == 1, b, sq - a - b))
+    out_ref[:, cols:] = jnp.where(lane < 3, pieces, 0.0).astype(jnp.bfloat16)
+    for copy in copies:
+        copy.wait()
 
 
 def project(place, blocks, g_own, g_sib, w_own, w_sib):
     hrows, feats = blocks[0].shape[2:]
     cols = w_own.shape[1]
     rows = 16 * hrows
-    tile = 256
-    whole = lambda x: pl.BlockSpec(x.shape, lambda t, m, n=len(x.shape): (0,) * n)
-    weights = pl.BlockSpec((feats, tile), lambda t, m: (0, t))
+    vmem = pl.BlockSpec(memory_space=pltpu.VMEM)
+    hbm = pl.BlockSpec(memory_space=pl.ANY)
     outs = (
         jax.ShapeDtypeStruct((rows, cols + 128), jnp.bfloat16),
-        jax.ShapeDtypeStruct((rows, feats), jnp.bfloat16),
-        jax.ShapeDtypeStruct((rows, feats), jnp.bfloat16),
+        pltpu.HBM((rows, feats), jnp.bfloat16),
+        pltpu.HBM((rows, feats), jnp.bfloat16),
     )
     return pl.pallas_call(
-        project_kernel,
-        grid_spec=pltpu.PrefetchScalarGridSpec(
-            num_scalar_prefetch=1,
-            grid=(cols // tile,),
-            in_specs=[whole(x) for x in blocks] + [whole(g_own), whole(g_sib), weights, weights],
-            out_specs=tuple(whole(x) for x in outs),
-        ),
+        functools.partial(project_kernel, 256),
+        in_specs=[pl.BlockSpec(memory_space=pltpu.SMEM)] + [vmem] * (len(blocks) + 4),
+        out_specs=(vmem, hbm, hbm),
+        scratch_shapes=[
+            pltpu.VMEM((rows, feats), jnp.bfloat16),
+            pltpu.VMEM((rows, feats), jnp.bfloat16),
+            pltpu.SemaphoreType.DMA((2,)),
+        ],
         out_shape=outs,
-        compiler_params=pltpu.CompilerParams(
-            dimension_semantics=("arbitrary",), vmem_limit_bytes=40 * 1024 * 1024
-        ),
+        compiler_params=pltpu.CompilerParams(vmem_limit_bytes=24 * 1024 * 1024),
         cost_estimate=pl.CostEstimate(
             flops=rows * feats * cols * 4, bytes_accessed=feats * cols * 4, transcendentals=0
         ),
         name="project",
-    )(place, *blocks, g_own, g_sib, w_own, w_sib)
+    )(place, *map(in_vmem, blocks), g_own, g_sib, in_vmem(w_own), in_vmem(w_sib))
 
 
 def per_device(
@@ -292,17 +306,17 @@
     hid1 = jnp.where(flip, own_hidden, sib_hidden)
     hidden = jnp.concatenate([hid0, hid1]).astype(jnp.float32)
     grad_mine = ((total - hidden) * (scale / math.sqrt(row_count))).astype(jnp.bfloat16)
-    grad_half = gather(grad_mine, "ch").reshape(row_half, cols)
-    grad_other = swap(grad_half)
-
     pred = total.astype(jnp.bfloat16).reshape(cores, hrows, cols)
     keep = jnp.where(flip, pred[1], pred[0])
     came = swap(jnp.where(flip, pred[0], pred[1]))
+    grad_half = gather(grad_mine, "ch").reshape(row_half, cols)
     prediction = jnp.concatenate([jnp.where(flip, came, keep), jnp.where(flip, keep, came)])
+    grad_half, prediction = lax.optimization_barrier((grad_half, prediction))
+    grad_other = swap(grad_half)
 
     tn = (((0,), (0,)), ((), ()))
-    weight_grad = lax.dot_general(own_raw, grad_half, tn, preferred_element_type=jnp.float32)
-    weight_grad += lax.dot_general(oth_raw, grad_other, tn, preferred_element_type=jnp.float32)
+    weight_grad = lax.dot_general(oth_raw, grad_other, tn, preferred_element_type=jnp.float32)
+    weight_grad += lax.dot_general(own_raw, grad_half, tn, preferred_element_type=jnp.float32)
     return (prediction, weight_grad.astype(jnp.bfloat16))
 
 

time: 111 us -> 106 us (0.955)
  local copies, waits for them, and re-layouts: 5.3 us -> 2.94 us
  other arithmetic: 5.37 us -> 3.33 us
  Pallas kernels: 13.3 us -> 11.7 us
    all_to_all x1, waiting for transfers between devices: 2.73 us -> 0.01 us  [gather(): return lax.all_to_all(jnp.broadcast_to(x[None], (n,) + x.shape), axis, 0, 0)]
    ppermute x8, starting transfers between devices: 20.1 us -> 22.7 us  [swap(): return lax.ppermute(x, 'c', [(0, 1), (1, 0)])]
    unnamed x8 -> x10, local copies, waits for them, and re-layouts: 1.63 us -> 0.02 us
    dot_general x1, matrix products: 2.08 us -> 0.74 us  [per_device(): lax.dot_general(own_raw, grad_half, tn, preferred_element_type=jnp.float32)]
    dot_general x1, matrix products: 0.74 us -> 2.08 us  [per_device(): lax.dot_general(oth_raw, grad_other, tn, preferred_element_type=jnp.float32)]
    all_to_all x1, waiting for transfers between devices: 6.82 us -> 8.11 us  [per_device(): lax.all_to_all(spread, TP, 0, 0)]
    all_to_all x1, waiting for transfers between devices: 0.89 us -> 2.03 us  [per_device(): parts = lax.all_to_all(payload, 'ch', 0, 0)]
  transfers between devices with their start and end apart: 21 -> 21, of which waited for: 8 -> 9; matrix products, arithmetic and copies ran while one was open for 7% -> 6% of each run, Pallas kernels for 0% -> 0%
where the time goes in v4:
time: 106 us
  starting transfers between devices  54.8 us (52%)
  waiting for transfers between devices  29.2 us (28%)
  Pallas kernels  11.7 us (11%)
  other arithmetic  3.33 us (3%)
  local copies, waits for them, and re-layouts  2.94 us (3%)
  matrix products  2.82 us (3%)
    ppermute x8, starting transfers between devices, swap(): return lax.ppermute(x, 'c', [(0, 1), (1, 0)])  22.7 us
    ppermute x9, starting transfers between devices, shift(): return lax.ppermute(x, axis, [(j, (j + k) % n) for j in range(n)])  17 us
    ppermute x9, waiting for transfers between devices, shift(): return lax.ppermute(x, axis, [(j, (j + k) % n) for j in range(n)])  8.58 us
    all_to_all x1, waiting for transfers between devices, per_device(): lax.all_to_all(spread, TP, 0, 0)  8.11 us
    all_to_all x1, waiting for transfers between devices, per_device(): got = lax.all_to_all(sent, 'ch', 0, 0)  8.06 us
    pallas_call x1, Pallas kernels, attend(): pl.pallas_call(functools.partial(attend_kernel, steps), in_specs=[pl.Bloc...  7.26 us
    pallas_call x1, Pallas kernels, project(): pl.pallas_call(functools.partial(project_kernel, 256), in_specs=[pl.Block...  4.49 us
    all_to_all x1, starting transfers between devices, per_device(): lax.all_to_all(spread, TP, 0, 0)  4.34 us
  transfers between devices with their start and end apart: 21, of which 9 were waited for; matrix products, arithmetic and copies ran while one was open for 6% of the time, Pallas kernels for 0%

profile of v4, /device:TPU:1, one launch (start us, length us, event | category | flops | bytes accessed | tf_op | source)
XLA Modules:
  0.0 105.7 jit_solution(17833794875843941867)
XLA Ops:
  0.6 3.3 %collective-permute-start = (bf16[8,8,256,128]{3,2,1,0:T(8,128)(2,1)}, bf16[8,8,256,128]{3,2,1,0:T(8,128)(2,1)}, u32[]{:S(2)}, u32[]{:S(2)}) collective-permute-start(bf16[8,8,256,128]{3,2,1,0:T(8,128)(2,1)} %ko.1), channel_id=1, source_target_pairs={{0,16},{16,0},{1,17},{17,1},{2,18},{18,2},{3,19},{19,3},{4,20},{20... | collective-permute-start | bytes 12582920 | tf_op jit(solution)/shard_map/ppermute | solution.py:35
  4.1 1.7 %broadcast_in_dim.13 = bf16[8,2,4,32,128]{4,3,2,1,0:T(8,128)(2,1)} broadcast(bf16[2,4,32,128]{3,2,1,0:T(8,128)(2,1)} %bitcast.48), dimensions={1,2,3,4} | broadcast | bytes 589824 | tf_op jit(solution)/shard_map/broadcast_in_dim | solution.py:249
  5.8 4.3 %all-to-all-start = ((bf16[16,4,32,128]{3,2,1,0:T(8,128)(2,1)}), bf16[16,4,32,128]{3,2,1,0:T(8,128)(2,1)S(1)}, u32[]{:S(2)}, u32[]{:S(2)}) async-start(bf16[16,4,32,128]{3,2,1,0:T(8,128)(2,1)} %bitcast.8), calls=%async_computation | async-start | bytes 1048576 | tf_op jit(solution)/shard_map/all_to_all | solution.py:259
  10.1 0.7 pad_add_fusion.1.meta
  10.9 1.0 convert_bitcast_fusion.new_ref
  11.8 8.1 %all-to-all-done = bf16[16,4,32,128]{3,2,1,0:T(8,128)(2,1)S(1)} async-done(((bf16[16,4,32,128]{3,2,1,0:T(8,128)(2,1)}), bf16[16,4,32,128]{3,2,1,0:T(8,128)(2,1)S(1)}, u32[]{:S(2)}, u32[]{:S(2)}) %all-to-all-start) | async-done | bytes 524320 | tf_op jit(solution)/shard_map/all_to_all | solution.py:259
  20.0 7.3 %attend.1 = bf16[8,272,128]{2,1,0:T(8,128)(2,1)} custom-call(s32[11]{0:T(128)S(1)} %pad_add_fusion.1.meta, bf16[8,2,4,32,128]{4,3,2,1,0:T(8,128)(2,1)S(1)} %bitcast.35, bf16[8,8,256,128]{3,2,1,0:T(8,128)(2,1)} %ko.1, bf16[8,8,256,128]{3,2,1,0:T(8,128)(2,1)} %vo.1, bf16[8,8,256,128]{3,2,1,0:T(8,128)(2,1)} %collective-permute-done.ks, ...), custom_call_target="tpu_custom_call" | custom-call | flops 536870912 | bytes 8388608 | tf_op jit(solution)/shard_map/attend/pallas_call | solution.py:136
  27.2 3.5 %all-to-all-start.1 = ((bf16[8,272,128]{2,1,0:T(8,128)(2,1)}), bf16[8,272,128]{2,1,0:T(8,128)(2,1)S(1)}, u32[]{:S(2)}, u32[]{:S(2)}) async-start(bf16[8,272,128]{2,1,0:T(8,128)(2,1)} %attend.1), calls=%async_computation.1 | async-start | bytes 1114112 | tf_op jit(solution)/shard_map/all_to_all | solution.py:271
  30.8 1.2 %collective-permute-start.12 = (bf16[1024,1024]{1,0:T(8,128)(2,1)S(1)}, bf16[1024,1024]{1,0:T(8,128)(2,1)}, u32[]{:S(2)}, u32[]{:S(2)}) collective-permute-start(bf16[1024,1024]{1,0:T(8,128)(2,1)S(1)} %copy-done), channel_id=1, source_target_pairs={{0,16},{16,0},{1,17},{17,1},{2,18},{18,2},{3,19},{19,3},{4,20},{20... | collective-permute-start | bytes 6291464 | tf_op jit(solution)/shard_map/ppermute | solution.py:35
  32.1 8.1 %all-to-all-done.1 = bf16[8,272,128]{2,1,0:T(8,128)(2,1)S(1)} async-done(((bf16[8,272,128]{2,1,0:T(8,128)(2,1)}), bf16[8,272,128]{2,1,0:T(8,128)(2,1)S(1)}, u32[]{:S(2)}, u32[]{:S(2)}) %all-to-all-start.1) | async-done | bytes 557088 | tf_op jit(solution)/shard_map/all_to_all | solution.py:271
  41.1 2.8 %collective-permute-start.3 = (bf16[2,16,1024]{2,1,0:T(8,128)(2,1)S(1)}, bf16[2,16,1024]{2,1,0:T(8,128)(2,1)S(1)}, u32[]{:S(2)}, u32[]{:S(2)}) collective-permute-start(bf16[2,16,1024]{2,1,0:T(8,128)(2,1)S(1)} %pad_maximum_fusion.1), channel_id=1, source_target_pairs={{0,4},{4,8},{8,12},{12,0},{1,5},{5,9},{9,13},{13,1},{2,6},{6,10},{... | collective-permute-start | bytes 196616 | tf_op jit(solution)/shard_map/ppermute | solution.py:31
  43.9 2.6 %collective-permute-start.4 = (bf16[2,16,1024]{2,1,0:T(8,128)(2,1)S(1)}, bf16[2,16,1024]{2,1,0:T(8,128)(2,1)S(1)}, u32[]{:S(2)}, u32[]{:S(2)}) collective-permute-start(bf16[2,16,1024]{2,1,0:T(8,128)(2,1)S(1)} %pad_maximum_fusion.1), channel_id=1, source_target_pairs={{0,12},{4,0},{8,4},{12,8},{1,13},{5,1},{9,5},{13,9},{2,14},{6,2},{... | collective-permute-start | bytes 196616 | tf_op jit(solution)/shard_map/ppermute | solution.py:31
  46.5 4.0 %collective-permute-start.5 = (bf16[2,16,1024]{2,1,0:T(8,128)(2,1)S(1)}, bf16[2,16,1024]{2,1,0:T(8,128)(2,1)S(1)}, u32[]{:S(2)}, u32[]{:S(2)}) collective-permute-start(bf16[2,16,1024]{2,1,0:T(8,128)(2,1)S(1)} %pad_maximum_fusion.1), channel_id=1, source_target_pairs={{0,8},{4,12},{8,0},{12,4},{1,9},{5,13},{9,1},{13,5},{2,10},{6,14},... | collective-permute-start | bytes 196616 | tf_op jit(solution)/shard_map/ppermute | solution.py:31
  50.5 2.9 %collective-permute-start.10 = (bf16[3,2,16,1024]{3,2,1,0:T(8,128)(2,1)S(1)}, bf16[3,2,16,1024]{3,2,1,0:T(8,128)(2,1)S(1)}, u32[]{:S(2)}, u32[]{:S(2)}) collective-permute-start(bf16[3,2,16,1024]{3,2,1,0:T(8,128)(2,1)S(1)} %pad_maximum_fusion.refs_0_), channel_id=1, source_target_pairs={{0,3},{1,0},{2,1},{3,2},{4,7},{5,4},{6,5},{7,6},{8,11},{9,8},{10,9... | collective-permute-start | bytes 589832 | tf_op jit(solution)/shard_map/ppermute | solution.py:31
  53.4 1.7 %collective-permute-start.8 = (bf16[3,2,16,1024]{3,2,1,0:T(8,128)(2,1)S(1)}, bf16[3,2,16,1024]{3,2,1,0:T(8,128)(2,1)S(1)}, u32[]{:S(2)}, u32[]{:S(2)}) collective-permute-start(bf16[3,2,16,1024]{3,2,1,0:T(8,128)(2,1)S(1)} %pad_maximum_fusion.refs_0_), channel_id=1, source_target_pairs={{0,2},{1,3},{2,0},{3,1},{4,6},{5,7},{6,4},{7,5},{8,10},{9,11},{10,... | collective-permute-start | bytes 589832 | tf_op jit(solution)/shard_map/ppermute | solution.py:31
  55.2 1.0 collective-permute-start.11
  56.8 4.9 %collective-permute-done.11.refs_7_ = bf16[1,2,16,1024]{3,2,1,0:T(8,128)(2,1)S(1)} collective-permute-done((bf16[1,2,16,1024]{3,2,1,0:T(8,128)(2,1)S(1)}, bf16[1,2,16,1024]{3,2,1,0:T(8,128)(2,1)S(1)}, u32[]{:S(2)}, u32[]{:S(2)}) %collective-permute-start.11) | collective-permute-done | bytes 65568 | tf_op jit(solution)/shard_map/ppermute | solution.py:31
  61.7 1.3 %collective-permute-start.9 = (bf16[1,2,16,1024]{3,2,1,0:T(8,128)(2,1)S(1)}, bf16[1,2,16,1024]{3,2,1,0:T(8,128)(2,1)S(1)}, u32[]{:S(2)}, u32[]{:S(2)}) collective-permute-start(bf16[1,2,16,1024]{3,2,1,0:T(8,128)(2,1)S(1)} %bitcast.38), channel_id=1, source_target_pairs={{0,2},{1,3},{2,0},{3,1},{4,6},{5,7},{6,4},{7,5},{8,10},{9,11},{10,... | collective-permute-start | bytes 196616 | tf_op jit(solution)/shard_map/ppermute | solution.py:31
  63.3 3.4 %collective-permute-done.9.refs_5_ = bf16[1,2,16,1024]{3,2,1,0:T(8,128)(2,1)S(1)} collective-permute-done((bf16[1,2,16,1024]{3,2,1,0:T(8,128)(2,1)S(1)}, bf16[1,2,16,1024]{3,2,1,0:T(8,128)(2,1)S(1)}, u32[]{:S(2)}, u32[]{:S(2)}) %collective-permute-start.9) | collective-permute-done | bytes 65568 | tf_op jit(solution)/shard_map/ppermute | solution.py:31
  66.8 4.5 %project.1 = (bf16[256,1152]{1,0:T(8,128)(2,1)}, bf16[256,1024]{1,0:T(8,128)(2,1)}, bf16[256,1024]{1,0:T(8,128)(2,1)}) custom-call(s32[2]{0:T(128)S(1)} %pad_add_fusion.place, bf16[3,2,16,1024]{3,2,1,0:T(8,128)(2,1)S(1)} %pad_maximum_fusion.refs_0_, bf16[1,2,16,1024]{3,2,1,0:T(8,128)(2,1)S(1)} %bitcast.39, ...), custom_call_target="tpu_custom_call" | custom-call | flops 1073741824 | bytes 4194304 | tf_op jit(solution)/shard_map/project/pallas_call | solution.py:206
  71.3 3.7 %all-to-all-start.2 = ((bf16[8,32,1152]{2,1,0:T(8,128)(2,1)}), bf16[8,32,1152]{2,1,0:T(8,128)(2,1)S(1)}, u32[]{:S(2)}, u32[]{:S(2)}) async-start(bf16[8,32,1152]{2,1,0:T(8,128)(2,1)} %bitcast.23), calls=%async_computation.2 | async-start | bytes 1179648 | tf_op jit(solution)/shard_map/all_to_all | solution.py:298
  75.0 4.9 %collective-permute-start.13 = (bf16[16,1024]{1,0:T(8,128)(2,1)S(1)}, bf16[16,1024]{1,0:T(8,128)(2,1)S(1)}, u32[]{:S(2)}, u32[]{:S(2)}) collective-permute-start(bf16[16,1024]{1,0:T(8,128)(2,1)S(1)} %constant_dynamic-slice_fusion), channel_id=1, source_target_pairs={{0,16},{16,0},{1,17},{17,1},{2,18},{18,2},{3,19},{19,3},{4,20},{20... | collective-permute-start | bytes 98312 | tf_op jit(solution)/shard_map/ppermute | solution.py:35
  79.9 0.9 collective-permute-done.13
  80.8 2.0 %all-to-all-done.2 = bf16[8,32,1152]{2,1,0:T(8,128)(2,1)S(1)} async-done(((bf16[8,32,1152]{2,1,0:T(8,128)(2,1)}), bf16[8,32,1152]{2,1,0:T(8,128)(2,1)S(1)}, u32[]{:S(2)}, u32[]{:S(2)}) %all-to-all-start.2) | async-done | bytes 589856 | tf_op jit(solution)/shard_map/all_to_all | solution.py:298
  83.1 0.9 broadcast_in_dim.33
  84.0 3.5 %all-to-all-start.3 = ((bf16[8,32,1024]{2,1,0:T(8,128)(2,1)}), bf16[8,32,1024]{2,1,0:T(8,128)(2,1)S(1)}, u32[]{:S(2)}, u32[]{:S(2)}) async-start(bf16[8,32,1024]{2,1,0:T(8,128)(2,1)} %broadcast_in_dim.33), calls=%async_computation.3 | async-start | bytes 1048576 | tf_op jit(solution)/shard_map/all_to_all | solution.py:18
  87.5 6.0 %collective-permute-start.14 = (bf16[16,1024]{1,0:T(8,128)(2,1)S(1)}, bf16[16,1024]{1,0:T(8,128)(2,1)S(1)}, u32[]{:S(2)}, u32[]{:S(2)}) collective-permute-start(bf16[16,1024]{1,0:T(8,128)(2,1)S(1)} %broadcast_select_fusion.3), channel_id=1, source_target_pairs={{0,16},{16,0},{1,17},{17,1},{2,18},{18,2},{3,19},{19,3},{4,20},{20... | collective-permute-start | bytes 98312 | tf_op jit(solution)/shard_map/ppermute | solution.py:35
  93.6 0.7 collective-permute-done.14
  95.0 7.0 %collective-permute-start.16 = (bf16[256,1024]{1,0:T(8,128)(2,1)S(1)}, bf16[256,1024]{1,0:T(8,128)(2,1)S(1)}, u32[]{:S(2)}, u32[]{:S(2)}) collective-permute-start(bf16[256,1024]{1,0:T(8,128)(2,1)S(1)} %bitcast.42), channel_id=1, source_target_pairs={{0,16},{16,0},{1,17},{17,1},{2,18},{18,2},{3,19},{19,3},{4,20},{20... | collective-permute-start | bytes 1572872 | tf_op jit(solution)/shard_map/ppermute | solution.py:35
  102.1 0.7 fusion.1
  102.8 0.8 collective-permute-done.16
  103.6 2.1 %add_convert_fusion = bf16[1024,1024]{1,0:T(8,128)(2,1)} fusion(f32[1024,1024]{1,0:T(8,128)S(1)} %fusion.1, bf16[256,1024]{1,0:T(8,128)(2,1)S(1)} %collective-permute-done.15, bf16[256,1024]{1,0:T(8,128)(2,1)S(1)} %collective-permute-done.16), kind=kOutput, calls=%fused_computation | convolution fusion | flops 538968064 | bytes 7340032 | tf_op jit(solution)/shard_map/dot_general | solution.py:318
  (55 shorter events, 3.3 us)
Async XLA Ops:
  0.6 19.3 %collective-permute-start = (bf16[8,8,256,128]{3,2,1,0:T(8,128)(2,1)}, bf16[8,8,256,128]{3,2,1,0:T(8,128)(2,1)}, u32[]{:S(2)}, u32[]{:S(2)}) collective-permute-start(bf16[8,8,256,128]{3,2,1,0:T(8,128)(2,1)} %ko.1), channel_id=1, source_target_pairs={{0,16},{16,0},{1,17},{17,1},{2,18},{18,2},{3,19},{19,3},{4,20},{20... | collective-permute-start | bytes 12582920 | tf_op jit(solution)/shard_map/ppermute | solution.py:35
  4.0 16.0 %collective-permute-start.1 = (bf16[8,8,256,128]{3,2,1,0:T(8,128)(2,1)}, bf16[8,8,256,128]{3,2,1,0:T(8,128)(2,1)}, u32[]{:S(2)}, u32[]{:S(2)}) collective-permute-start(bf16[8,8,256,128]{3,2,1,0:T(8,128)(2,1)} %vo.1), channel_id=1, source_target_pairs={{0,16},{16,0},{1,17},{17,1},{2,18},{18,2},{3,19},{19,3},{4,20},{20... | collective-permute-start | bytes 12582920 | tf_op jit(solution)/shard_map/ppermute | solution.py:35
  5.8 14.1 %all-to-all-start = ((bf16[16,4,32,128]{3,2,1,0:T(8,128)(2,1)}), bf16[16,4,32,128]{3,2,1,0:T(8,128)(2,1)S(1)}, u32[]{:S(2)}, u32[]{:S(2)}) async-start(bf16[16,4,32,128]{3,2,1,0:T(8,128)(2,1)} %bitcast.8), calls=%async_computation | async-start | bytes 1048576 | tf_op jit(solution)/shard_map/all_to_all | solution.py:259
  19.9 10.8 %copy-start = (bf16[1024,1024]{1,0:T(8,128)(2,1)S(1)}, bf16[1024,1024]{1,0:T(8,128)(2,1)}, u32[]{:S(2)}) copy-start(bf16[1024,1024]{1,0:T(8,128)(2,1)} %refs_10_.1) | copy-start | bytes 6291460
  19.9 12.0 %copy-start.1 = (f32[1024]{0:T(1024)S(1)}, f32[1024]{0:T(1024)}, u32[]{:S(2)}) copy-start(f32[1024]{0:T(1024)} %param.15) | copy-start | bytes 12292
  27.2 12.9 %all-to-all-start.1 = ((bf16[8,272,128]{2,1,0:T(8,128)(2,1)}), bf16[8,272,128]{2,1,0:T(8,128)(2,1)S(1)}, u32[]{:S(2)}, u32[]{:S(2)}) async-start(bf16[8,272,128]{2,1,0:T(8,128)(2,1)} %attend.1), calls=%async_computation.1 | async-start | bytes 1114112 | tf_op jit(solution)/shard_map/all_to_all | solution.py:271
  30.8 25.3 %collective-permute-start.12 = (bf16[1024,1024]{1,0:T(8,128)(2,1)S(1)}, bf16[1024,1024]{1,0:T(8,128)(2,1)}, u32[]{:S(2)}, u32[]{:S(2)}) collective-permute-start(bf16[1024,1024]{1,0:T(8,128)(2,1)S(1)} %copy-done), channel_id=1, source_target_pairs={{0,16},{16,0},{1,17},{17,1},{2,18},{18,2},{3,19},{19,3},{4,20},{20... | collective-permute-start | bytes 6291464 | tf_op jit(solution)/shard_map/ppermute | solution.py:35
  31.9 9.1 %collective-permute-start.2 = (f32[1024]{0:T(1024)S(1)}, f32[1024]{0:T(1024)S(1)}, u32[]{:S(2)}, u32[]{:S(2)}) collective-permute-start(f32[1024]{0:T(1024)S(1)} %copy-done.1), channel_id=1, source_target_pairs={{0,16},{16,0},{1,17},{17,1},{2,18},{18,2},{3,19},{19,3},{4,20},{20... | collective-permute-start | bytes 12296 | tf_op jit(solution)/shard_map/ppermute | solution.py:35
  40.5 34.5 %copy-start.3 = (bf16[32,1024]{1,0:T(8,128)(2,1)S(1)}, bf16[32,1024]{1,0:T(8,128)(2,1)}, u32[]{:S(2)}) copy-start(bf16[32,1024]{1,0:T(8,128)(2,1)} %param.17) | copy-start | bytes 196612
  41.1 9.4 %collective-permute-start.3 = (bf16[2,16,1024]{2,1,0:T(8,128)(2,1)S(1)}, bf16[2,16,1024]{2,1,0:T(8,128)(2,1)S(1)}, u32[]{:S(2)}, u32[]{:S(2)}) collective-permute-start(bf16[2,16,1024]{2,1,0:T(8,128)(2,1)S(1)} %pad_maximum_fusion.1), channel_id=1, source_target_pairs={{0,4},{4,8},{8,12},{12,0},{1,5},{5,9},{9,13},{13,1},{2,6},{6,10},{... | collective-permute-start | bytes 196616 | tf_op jit(solution)/shard_map/ppermute | solution.py:31
  43.9 6.6 %collective-permute-start.4 = (bf16[2,16,1024]{2,1,0:T(8,128)(2,1)S(1)}, bf16[2,16,1024]{2,1,0:T(8,128)(2,1)S(1)}, u32[]{:S(2)}, u32[]{:S(2)}) collective-permute-start(bf16[2,16,1024]{2,1,0:T(8,128)(2,1)S(1)} %pad_maximum_fusion.1), channel_id=1, source_target_pairs={{0,12},{4,0},{8,4},{12,8},{1,13},{5,1},{9,5},{13,9},{2,14},{6,2},{... | collective-permute-start | bytes 196616 | tf_op jit(solution)/shard_map/ppermute | solution.py:31
  46.5 8.7 %collective-permute-start.5 = (bf16[2,16,1024]{2,1,0:T(8,128)(2,1)S(1)}, bf16[2,16,1024]{2,1,0:T(8,128)(2,1)S(1)}, u32[]{:S(2)}, u32[]{:S(2)}) collective-permute-start(bf16[2,16,1024]{2,1,0:T(8,128)(2,1)S(1)} %pad_maximum_fusion.1), channel_id=1, source_target_pairs={{0,8},{4,12},{8,0},{12,4},{1,9},{5,13},{9,1},{13,5},{2,10},{6,14},... | collective-permute-start | bytes 196616 | tf_op jit(solution)/shard_map/ppermute | solution.py:31
  50.5 16.2 %collective-permute-start.10 = (bf16[3,2,16,1024]{3,2,1,0:T(8,128)(2,1)S(1)}, bf16[3,2,16,1024]{3,2,1,0:T(8,128)(2,1)S(1)}, u32[]{:S(2)}, u32[]{:S(2)}) collective-permute-start(bf16[3,2,16,1024]{3,2,1,0:T(8,128)(2,1)S(1)} %pad_maximum_fusion.refs_0_), channel_id=1, source_target_pairs={{0,3},{1,0},{2,1},{3,2},{4,7},{5,4},{6,5},{7,6},{8,11},{9,8},{10,9... | collective-permute-start | bytes 589832 | tf_op jit(solution)/shard_map/ppermute | solution.py:31
  53.4 13.3 %collective-permute-start.6 = (bf16[3,2,16,1024]{3,2,1,0:T(8,128)(2,1)S(1)}, bf16[3,2,16,1024]{3,2,1,0:T(8,128)(2,1)S(1)}, u32[]{:S(2)}, u32[]{:S(2)}) collective-permute-start(bf16[3,2,16,1024]{3,2,1,0:T(8,128)(2,1)S(1)} %pad_maximum_fusion.refs_0_), channel_id=1, source_target_pairs={{0,1},{1,2},{2,3},{3,0},{4,5},{5,6},{6,7},{7,4},{8,9},{9,10},{10,1... | collective-permute-start | bytes 589832 | tf_op jit(solution)/shard_map/ppermute | solution.py:31
  53.4 13.3 %collective-permute-start.8 = (bf16[3,2,16,1024]{3,2,1,0:T(8,128)(2,1)S(1)}, bf16[3,2,16,1024]{3,2,1,0:T(8,128)(2,1)S(1)}, u32[]{:S(2)}, u32[]{:S(2)}) collective-permute-start(bf16[3,2,16,1024]{3,2,1,0:T(8,128)(2,1)S(1)} %pad_maximum_fusion.refs_0_), channel_id=1, source_target_pairs={{0,2},{1,3},{2,0},{3,1},{4,6},{5,7},{6,4},{7,5},{8,10},{9,11},{10,... | collective-permute-start | bytes 589832 | tf_op jit(solution)/shard_map/ppermute | solution.py:31
  55.2 6.5 %collective-permute-start.11 = (bf16[1,2,16,1024]{3,2,1,0:T(8,128)(2,1)S(1)}, bf16[1,2,16,1024]{3,2,1,0:T(8,128)(2,1)S(1)}, u32[]{:S(2)}, u32[]{:S(2)}) collective-permute-start(bf16[1,2,16,1024]{3,2,1,0:T(8,128)(2,1)S(1)} %bitcast.36), channel_id=1, source_target_pairs={{0,3},{1,0},{2,1},{3,2},{4,7},{5,4},{6,5},{7,6},{8,11},{9,8},{10,9... | collective-permute-start | bytes 196616 | tf_op jit(solution)/shard_map/ppermute | solution.py:31
  56.1 7.2 %collective-permute-start.7 = (bf16[1,2,16,1024]{3,2,1,0:T(8,128)(2,1)S(1)}, bf16[1,2,16,1024]{3,2,1,0:T(8,128)(2,1)S(1)}, u32[]{:S(2)}, u32[]{:S(2)}) collective-permute-start(bf16[1,2,16,1024]{3,2,1,0:T(8,128)(2,1)S(1)} %bitcast.37), channel_id=1, source_target_pairs={{0,1},{1,2},{2,3},{3,0},{4,5},{5,6},{6,7},{7,4},{8,9},{9,10},{10,1... | collective-permute-start | bytes 196616 | tf_op jit(solution)/shard_map/ppermute | solution.py:31
  61.7 5.1 %collective-permute-start.9 = (bf16[1,2,16,1024]{3,2,1,0:T(8,128)(2,1)S(1)}, bf16[1,2,16,1024]{3,2,1,0:T(8,128)(2,1)S(1)}, u32[]{:S(2)}, u32[]{:S(2)}) collective-permute-start(bf16[1,2,16,1024]{3,2,1,0:T(8,128)(2,1)S(1)} %bitcast.38), channel_id=1, source_target_pairs={{0,2},{1,3},{2,0},{3,1},{4,6},{5,7},{6,4},{7,5},{8,10},{9,11},{10,... | collective-permute-start | bytes 196616 | tf_op jit(solution)/shard_map/ppermute | solution.py:31
  71.3 22.3 %copy-start.4 = (bf16[256,1024]{1,0:T(8,128)(2,1)S(1)}, bf16[256,1024]{1,0:T(8,128)(2,1)}, u32[]{:S(2)}) copy-start(bf16[256,1024]{1,0:T(8,128)(2,1)} %get-tuple-element.9) | copy-start | bytes 1572868
  71.3 30.8 %copy-start.2 = (bf16[256,1024]{1,0:T(8,128)(2,1)S(1)}, bf16[256,1024]{1,0:T(8,128)(2,1)}, u32[]{:S(2)}) copy-start(bf16[256,1024]{1,0:T(8,128)(2,1)} %get-tuple-element.11) | copy-start | bytes 1572868
  71.3 11.5 %all-to-all-start.2 = ((bf16[8,32,1152]{2,1,0:T(8,128)(2,1)}), bf16[8,32,1152]{2,1,0:T(8,128)(2,1)S(1)}, u32[]{:S(2)}, u32[]{:S(2)}) async-start(bf16[8,32,1152]{2,1,0:T(8,128)(2,1)} %bitcast.23), calls=%async_computation.2 | async-start | bytes 1179648 | tf_op jit(solution)/shard_map/all_to_all | solution.py:298
  75.0 5.7 %collective-permute-start.13 = (bf16[16,1024]{1,0:T(8,128)(2,1)S(1)}, bf16[16,1024]{1,0:T(8,128)(2,1)S(1)}, u32[]{:S(2)}, u32[]{:S(2)}) collective-permute-start(bf16[16,1024]{1,0:T(8,128)(2,1)S(1)} %constant_dynamic-slice_fusion), channel_id=1, source_target_pairs={{0,16},{16,0},{1,17},{17,1},{2,18},{18,2},{3,19},{19,3},{4,20},{20... | collective-permute-start | bytes 98312 | tf_op jit(solution)/shard_map/ppermute | solution.py:35
  84.0 11.1 %all-to-all-start.3 = ((bf16[8,32,1024]{2,1,0:T(8,128)(2,1)}), bf16[8,32,1024]{2,1,0:T(8,128)(2,1)S(1)}, u32[]{:S(2)}, u32[]{:S(2)}) async-start(bf16[8,32,1024]{2,1,0:T(8,128)(2,1)} %broadcast_in_dim.33), calls=%async_computation.3 | async-start | bytes 1048576 | tf_op jit(solution)/shard_map/all_to_all | solution.py:18
  87.5 6.9 %collective-permute-start.14 = (bf16[16,1024]{1,0:T(8,128)(2,1)S(1)}, bf16[16,1024]{1,0:T(8,128)(2,1)S(1)}, u32[]{:S(2)}, u32[]{:S(2)}) collective-permute-start(bf16[16,1024]{1,0:T(8,128)(2,1)S(1)} %broadcast_select_fusion.3), channel_id=1, source_target_pairs={{0,16},{16,0},{1,17},{17,1},{2,18},{18,2},{3,19},{19,3},{4,20},{20... | collective-permute-start | bytes 98312 | tf_op jit(solution)/shard_map/ppermute | solution.py:35
  93.5 9.3 %collective-permute-start.15 = (bf16[256,1024]{1,0:T(8,128)(2,1)S(1)}, bf16[256,1024]{1,0:T(8,128)(2,1)S(1)}, u32[]{:S(2)}, u32[]{:S(2)}) collective-permute-start(bf16[256,1024]{1,0:T(8,128)(2,1)S(1)} %copy-done.4), channel_id=1, source_target_pairs={{0,16},{16,0},{1,17},{17,1},{2,18},{18,2},{3,19},{19,3},{4,20},{20... | collective-permute-start | bytes 1572872 | tf_op jit(solution)/shard_map/ppermute | solution.py:35
  95.0 8.5 %collective-permute-start.16 = (bf16[256,1024]{1,0:T(8,128)(2,1)S(1)}, bf16[256,1024]{1,0:T(8,128)(2,1)S(1)}, u32[]{:S(2)}, u32[]{:S(2)}) collective-permute-start(bf16[256,1024]{1,0:T(8,128)(2,1)S(1)} %bitcast.42), channel_id=1, source_target_pairs={{0,16},{16,0},{1,17},{17,1},{2,18},{18,2},{3,19},{19,3},{4,20},{20... | collective-permute-start | bytes 1572872 | tf_op jit(solution)/shard_map/ppermute | solution.py:35

commit v5 on v4

--- a/solution.py
+++ b/solution.py
@@ -159,7 +159,7 @@
     hrows = blocks[0].shape[2]
     feats, cols = w_own.shape
     for n, ref in enumerate(blocks):
-        y_back, z_backs = n // 2, ((0, 1, 3), (2,))[n % 2]
+        y_back, z_backs = (0, 1, 3, 2)[n // 2], ((1, 3), (0, 2))[n % 2]
         y = lax.rem(place[1] - y_back + 4, 4)
         for at, z_back in enumerate(z_backs):
             z = lax.rem(place[0] - z_back + 4, 4)
@@ -282,10 +282,10 @@
     raw = jnp.stack([flat_own * norm_gain[None, :], flat_sib * sib_gain[None, :]])
     raw = raw.astype(jnp.bfloat16)
 
-    near = jnp.stack([raw, shift(raw, "zh", 1), shift(raw, "zh", 3)])
-    far = shift(raw, "zh", 2)[None]
+    near = jnp.stack([shift(raw, "zh", 1), shift(raw, "zh", 3)])
+    far = jnp.stack([raw, shift(raw, "zh", 2)])
     blocks = [near, far]
-    for k in (1, 2, 3):
+    for k in (1, 3, 2):
         blocks += [shift(near, "y", k), shift(far, "y", k)]
     row_half = zh * ny * hrows
     row_count = row_half * cores

time: 106 us -> 103 us (0.972)
  starting transfers between devices: 54.8 us -> 50.8 us
    ppermute x8, starting transfers between devices: 22.7 us -> 16.4 us  [swap(): return lax.ppermute(x, 'c', [(0, 1), (1, 0)])]
    ppermute x9, waiting for transfers between devices: 8.58 us -> 5.31 us  [shift(): return lax.ppermute(x, axis, [(j, (j + k) % n) for j in range(n)])]
    all_to_all x1, waiting for transfers between devices: 2.03 us -> 4.4 us  [per_device(): parts = lax.all_to_all(payload, 'ch', 0, 0)]
    all_to_all x1, waiting for transfers between devices: 0.01 us -> 2.12 us  [gather(): return lax.all_to_all(jnp.broadcast_to(x[None], (n,) + x.shape), axis, 0, 0)]
    ppermute x9, starting transfers between devices: 17 us -> 18.8 us  [shift(): return lax.ppermute(x, axis, [(j, (j + k) % n) for j in range(n)])]
  transfers between devices with their start and end apart: 21 -> 21, of which waited for: 9 -> 12; matrix products, arithmetic and copies ran while one was open for 6% -> 6% of each run, Pallas kernels for 0% -> 0%
where the time goes in v5:
time: 103 us; the launch traced here: 102 us
  starting transfers between devices  50.8 us (49%)
  waiting for transfers between devices  30 us (29%)
  Pallas kernels  11.5 us (11%)
  other arithmetic  3.33 us (3%)
  local copies, waits for them, and re-layouts  2.94 us (3%)
  matrix products  2.82 us (3%)
    ppermute x9, starting transfers between devices, shift(): return lax.ppermute(x, axis, [(j, (j + k) % n) for j in range(n)])  18.8 us
    ppermute x8, starting transfers between devices, swap(): return lax.ppermute(x, 'c', [(0, 1), (1, 0)])  16.4 us
    all_to_all x1, waiting for transfers between devices, per_device(): lax.all_to_all(spread, TP, 0, 0)  8.11 us
    all_to_all x1, waiting for transfers between devices, per_device(): got = lax.all_to_all(sent, 'ch', 0, 0)  7.66 us
    pallas_call x1, Pallas kernels, attend(): pl.pallas_call(functools.partial(attend_kernel, steps), in_specs=[pl.Bloc...  7.05 us
    ppermute x9, waiting for transfers between devices, shift(): return lax.ppermute(x, axis, [(j, (j + k) % n) for j in range(n)])  5.31 us
    pallas_call x1, Pallas kernels, project(): pl.pallas_call(functools.partial(project_kernel, 256), in_specs=[pl.Block...  4.47 us
    all_to_all x1, waiting for transfers between devices, per_device(): parts = lax.all_to_all(payload, 'ch', 0, 0)  4.4 us
  transfers between devices with their start and end apart: 21, of which 12 were waited for; matrix products, arithmetic and copies ran while one was open for 6% of the time, Pallas kernels for 0%

profile of v5, /device:TPU:1, one launch (start us, length us, event | category | flops | bytes accessed | tf_op | source)
XLA Modules:
  0.0 102.3 jit_solution(15654992863038766583)
XLA Ops:
  0.6 3.3 %collective-permute-start = (bf16[8,8,256,128]{3,2,1,0:T(8,128)(2,1)}, bf16[8,8,256,128]{3,2,1,0:T(8,128)(2,1)}, u32[]{:S(2)}, u32[]{:S(2)}) collective-permute-start(bf16[8,8,256,128]{3,2,1,0:T(8,128)(2,1)} %ko.1), channel_id=1, source_target_pairs={{0,16},{16,0},{1,17},{17,1},{2,18},{18,2},{3,19},{19,3},{4,20},{20... | collective-permute-start | bytes 12582920 | tf_op jit(solution)/shard_map/ppermute | solution.py:35
  4.1 1.7 %broadcast_in_dim.11 = bf16[8,2,4,32,128]{4,3,2,1,0:T(8,128)(2,1)} broadcast(bf16[2,4,32,128]{3,2,1,0:T(8,128)(2,1)} %bitcast.44), dimensions={1,2,3,4} | broadcast | bytes 589824 | tf_op jit(solution)/shard_map/broadcast_in_dim | solution.py:249
  5.8 4.3 %all-to-all-start = ((bf16[16,4,32,128]{3,2,1,0:T(8,128)(2,1)}), bf16[16,4,32,128]{3,2,1,0:T(8,128)(2,1)S(1)}, u32[]{:S(2)}, u32[]{:S(2)}) async-start(bf16[16,4,32,128]{3,2,1,0:T(8,128)(2,1)} %bitcast.8), calls=%async_computation | async-start | bytes 1048576 | tf_op jit(solution)/shard_map/all_to_all | solution.py:259
  10.9 1.0 convert_bitcast_fusion.new_ref
  11.8 8.1 %all-to-all-done = bf16[16,4,32,128]{3,2,1,0:T(8,128)(2,1)S(1)} async-done(((bf16[16,4,32,128]{3,2,1,0:T(8,128)(2,1)}), bf16[16,4,32,128]{3,2,1,0:T(8,128)(2,1)S(1)}, u32[]{:S(2)}, u32[]{:S(2)}) %all-to-all-start) | async-done | bytes 524320 | tf_op jit(solution)/shard_map/all_to_all | solution.py:259
  20.0 7.1 %attend.1 = bf16[8,272,128]{2,1,0:T(8,128)(2,1)} custom-call(s32[11]{0:T(128)S(1)} %pad_add_fusion.1.meta, bf16[8,2,4,32,128]{4,3,2,1,0:T(8,128)(2,1)S(1)} %bitcast.35, bf16[8,8,256,128]{3,2,1,0:T(8,128)(2,1)} %ko.1, bf16[8,8,256,128]{3,2,1,0:T(8,128)(2,1)} %vo.1, bf16[8,8,256,128]{3,2,1,0:T(8,128)(2,1)} %collective-permute-done.ks, ...), custom_call_target="tpu_custom_call" | custom-call | flops 536870912 | bytes 8388608 | tf_op jit(solution)/shard_map/attend/pallas_call | solution.py:136
  27.0 3.5 %all-to-all-start.1 = ((bf16[8,272,128]{2,1,0:T(8,128)(2,1)}), bf16[8,272,128]{2,1,0:T(8,128)(2,1)S(1)}, u32[]{:S(2)}, u32[]{:S(2)}) async-start(bf16[8,272,128]{2,1,0:T(8,128)(2,1)} %attend.1), calls=%async_computation.1 | async-start | bytes 1114112 | tf_op jit(solution)/shard_map/all_to_all | solution.py:271
  30.6 1.4 %collective-permute-start.12 = (bf16[1024,1024]{1,0:T(8,128)(2,1)S(1)}, bf16[1024,1024]{1,0:T(8,128)(2,1)}, u32[]{:S(2)}, u32[]{:S(2)}) collective-permute-start(bf16[1024,1024]{1,0:T(8,128)(2,1)S(1)} %copy-done), channel_id=1, source_target_pairs={{0,16},{16,0},{1,17},{17,1},{2,18},{18,2},{3,19},{19,3},{4,20},{20... | collective-permute-start | bytes 6291464 | tf_op jit(solution)/shard_map/ppermute | solution.py:35
  32.0 7.7 %all-to-all-done.1 = bf16[8,272,128]{2,1,0:T(8,128)(2,1)S(1)} async-done(((bf16[8,272,128]{2,1,0:T(8,128)(2,1)}), bf16[8,272,128]{2,1,0:T(8,128)(2,1)S(1)}, u32[]{:S(2)}, u32[]{:S(2)}) %all-to-all-start.1) | async-done | bytes 557088 | tf_op jit(solution)/shard_map/all_to_all | solution.py:271
  40.7 6.2 %collective-permute-start.5 = (bf16[2,16,1024]{2,1,0:T(8,128)(2,1)S(1)}, bf16[2,16,1024]{2,1,0:T(8,128)(2,1)S(1)}, u32[]{:S(2)}, u32[]{:S(2)}) collective-permute-start(bf16[2,16,1024]{2,1,0:T(8,128)(2,1)S(1)} %pad_maximum_fusion.2), channel_id=1, source_target_pairs={{0,8},{4,12},{8,0},{12,4},{1,9},{5,13},{9,1},{13,5},{2,10},{6,14},... | collective-permute-start | bytes 196616 | tf_op jit(solution)/shard_map/ppermute | solution.py:31
  46.9 1.5 %collective-permute-start.3 = (bf16[2,16,1024]{2,1,0:T(8,128)(2,1)S(1)}, bf16[2,16,1024]{2,1,0:T(8,128)(2,1)S(1)}, u32[]{:S(2)}, u32[]{:S(2)}) collective-permute-start(bf16[2,16,1024]{2,1,0:T(8,128)(2,1)S(1)} %pad_maximum_fusion.2), channel_id=1, source_target_pairs={{0,4},{4,8},{8,12},{12,0},{1,5},{5,9},{9,13},{13,1},{2,6},{6,10},{... | collective-permute-start | bytes 196616 | tf_op jit(solution)/shard_map/ppermute | solution.py:31
  48.4 2.1 %collective-permute-start.4 = (bf16[2,16,1024]{2,1,0:T(8,128)(2,1)S(1)}, bf16[2,16,1024]{2,1,0:T(8,128)(2,1)S(1)}, u32[]{:S(2)}, u32[]{:S(2)}) collective-permute-start(bf16[2,16,1024]{2,1,0:T(8,128)(2,1)S(1)} %pad_maximum_fusion.2), channel_id=1, source_target_pairs={{0,12},{4,0},{8,4},{12,8},{1,13},{5,1},{9,5},{13,9},{2,14},{6,2},{... | collective-permute-start | bytes 196616 | tf_op jit(solution)/shard_map/ppermute | solution.py:31
  50.5 2.9 %collective-permute-start.11 = (bf16[2,2,16,1024]{3,2,1,0:T(8,128)(2,1)S(1)}, bf16[2,2,16,1024]{3,2,1,0:T(8,128)(2,1)S(1)}, u32[]{:S(2)}, u32[]{:S(2)}) collective-permute-start(bf16[2,2,16,1024]{3,2,1,0:T(8,128)(2,1)S(1)} %pad_maximum_fusion.1.refs_1_), channel_id=1, source_target_pairs={{0,2},{1,3},{2,0},{3,1},{4,6},{5,7},{6,4},{7,5},{8,10},{9,11},{10,... | collective-permute-start | bytes 393224 | tf_op jit(solution)/shard_map/ppermute | solution.py:31
  53.8 2.3 %collective-permute-start.9 = (bf16[2,2,16,1024]{3,2,1,0:T(8,128)(2,1)S(1)}, bf16[2,2,16,1024]{3,2,1,0:T(8,128)(2,1)S(1)}, u32[]{:S(2)}, u32[]{:S(2)}) collective-permute-start(bf16[2,2,16,1024]{3,2,1,0:T(8,128)(2,1)S(1)} %pad_maximum_fusion.1.refs_1_), channel_id=1, source_target_pairs={{0,3},{1,0},{2,1},{3,2},{4,7},{5,4},{6,5},{7,6},{8,11},{9,8},{10,9... | collective-permute-start | bytes 393224 | tf_op jit(solution)/shard_map/ppermute | solution.py:31
  56.1 0.8 collective-permute-start.10
  57.1 2.5 %collective-permute-start.8 = (bf16[2,2,16,1024]{3,2,1,0:T(8,128)(2,1)S(1)}, bf16[2,2,16,1024]{3,2,1,0:T(8,128)(2,1)S(1)}, u32[]{:S(2)}, u32[]{:S(2)}) collective-permute-start(bf16[2,2,16,1024]{3,2,1,0:T(8,128)(2,1)S(1)} %pad_maximum_fusion.refs_0_), channel_id=1, source_target_pairs={{0,3},{1,0},{2,1},{3,2},{4,7},{5,4},{6,5},{7,6},{8,11},{9,8},{10,9... | collective-permute-start | bytes 393224 | tf_op jit(solution)/shard_map/ppermute | solution.py:31
  59.9 1.0 collective-permute-done.9.refs_5_
  60.8 2.1 %collective-permute-done.10.refs_6_ = bf16[2,2,16,1024]{3,2,1,0:T(8,128)(2,1)S(1)} collective-permute-done((bf16[2,2,16,1024]{3,2,1,0:T(8,128)(2,1)S(1)}, bf16[2,2,16,1024]{3,2,1,0:T(8,128)(2,1)S(1)}, u32[]{:S(2)}, u32[]{:S(2)}) %collective-permute-start.10) | collective-permute-done | bytes 131104 | tf_op jit(solution)/shard_map/ppermute | solution.py:31
  62.9 1.8 %collective-permute-done.6.refs_2_ = bf16[2,2,16,1024]{3,2,1,0:T(8,128)(2,1)S(1)} collective-permute-done((bf16[2,2,16,1024]{3,2,1,0:T(8,128)(2,1)S(1)}, bf16[2,2,16,1024]{3,2,1,0:T(8,128)(2,1)S(1)}, u32[]{:S(2)}, u32[]{:S(2)}) %collective-permute-start.6) | collective-permute-done | bytes 131104 | tf_op jit(solution)/shard_map/ppermute | solution.py:31
  65.0 4.5 %project.1 = (bf16[256,1152]{1,0:T(8,128)(2,1)}, bf16[256,1024]{1,0:T(8,128)(2,1)}, bf16[256,1024]{1,0:T(8,128)(2,1)}) custom-call(s32[2]{0:T(128)S(1)} %pad_add_fusion.place, bf16[2,2,16,1024]{3,2,1,0:T(8,128)(2,1)S(1)} %pad_maximum_fusion.refs_0_, bf16[2,2,16,1024]{3,2,1,0:T(8,128)(2,1)S(1)} %pad_maximum_fusion.1.refs_1_, ...), custom_call_target="tpu_custom_call" | custom-call | flops 1073741824 | bytes 4194304 | tf_op jit(solution)/shard_map/project/pallas_call | solution.py:206
  69.5 4.2 %all-to-all-start.2 = ((bf16[8,32,1152]{2,1,0:T(8,128)(2,1)}), bf16[8,32,1152]{2,1,0:T(8,128)(2,1)S(1)}, u32[]{:S(2)}, u32[]{:S(2)}) async-start(bf16[8,32,1152]{2,1,0:T(8,128)(2,1)} %bitcast.23), calls=%async_computation.2 | async-start | bytes 1179648 | tf_op jit(solution)/shard_map/all_to_all | solution.py:298
  73.7 2.7 %collective-permute-start.13 = (bf16[16,1024]{1,0:T(8,128)(2,1)S(1)}, bf16[16,1024]{1,0:T(8,128)(2,1)S(1)}, u32[]{:S(2)}, u32[]{:S(2)}) collective-permute-start(bf16[16,1024]{1,0:T(8,128)(2,1)S(1)} %constant_dynamic-slice_fusion), channel_id=1, source_target_pairs={{0,16},{16,0},{1,17},{17,1},{2,18},{18,2},{3,19},{19,3},{4,20},{20... | collective-permute-start | bytes 98312 | tf_op jit(solution)/shard_map/ppermute | solution.py:35
  76.3 0.9 collective-permute-done.13
  77.2 4.4 %all-to-all-done.2 = bf16[8,32,1152]{2,1,0:T(8,128)(2,1)S(1)} async-done(((bf16[8,32,1152]{2,1,0:T(8,128)(2,1)}), bf16[8,32,1152]{2,1,0:T(8,128)(2,1)S(1)}, u32[]{:S(2)}, u32[]{:S(2)}) %all-to-all-start.2) | async-done | bytes 589856 | tf_op jit(solution)/shard_map/all_to_all | solution.py:298
  81.9 0.9 broadcast_in_dim.14
  82.8 3.5 %all-to-all-start.3 = ((bf16[8,32,1024]{2,1,0:T(8,128)(2,1)}), bf16[8,32,1024]{2,1,0:T(8,128)(2,1)S(1)}, u32[]{:S(2)}, u32[]{:S(2)}) async-start(bf16[8,32,1024]{2,1,0:T(8,128)(2,1)} %broadcast_in_dim.14), calls=%async_computation.3 | async-start | bytes 1048576 | tf_op jit(solution)/shard_map/all_to_all | solution.py:18
  86.3 3.8 %collective-permute-start.14 = (bf16[16,1024]{1,0:T(8,128)(2,1)S(1)}, bf16[16,1024]{1,0:T(8,128)(2,1)S(1)}, u32[]{:S(2)}, u32[]{:S(2)}) collective-permute-start(bf16[16,1024]{1,0:T(8,128)(2,1)S(1)} %broadcast_select_fusion.3), channel_id=1, source_target_pairs={{0,16},{16,0},{1,17},{17,1},{2,18},{18,2},{3,19},{19,3},{4,20},{20... | collective-permute-start | bytes 98312 | tf_op jit(solution)/shard_map/ppermute | solution.py:35
  90.3 0.7 collective-permute-done.14
  91.7 2.1 %all-to-all-done.3 = bf16[8,32,1024]{2,1,0:T(8,128)(2,1)S(1)} async-done(((bf16[8,32,1024]{2,1,0:T(8,128)(2,1)}), bf16[8,32,1024]{2,1,0:T(8,128)(2,1)S(1)}, u32[]{:S(2)}, u32[]{:S(2)}) %all-to-all-start.3) | async-done | bytes 524320 | tf_op jit(solution)/shard_map/all_to_all | solution.py:18
  93.8 4.9 %collective-permute-start.16 = (bf16[256,1024]{1,0:T(8,128)(2,1)S(1)}, bf16[256,1024]{1,0:T(8,128)(2,1)S(1)}, u32[]{:S(2)}, u32[]{:S(2)}) collective-permute-start(bf16[256,1024]{1,0:T(8,128)(2,1)S(1)} %bitcast.38), channel_id=1, source_target_pairs={{0,16},{16,0},{1,17},{17,1},{2,18},{18,2},{3,19},{19,3},{4,20},{20... | collective-permute-start | bytes 1572872 | tf_op jit(solution)/shard_map/ppermute | solution.py:35
  99.4 0.8 collective-permute-done.16
  100.2 2.1 %add_convert_fusion = bf16[1024,1024]{1,0:T(8,128)(2,1)} fusion(f32[1024,1024]{1,0:T(8,128)S(1)} %fusion.1, bf16[256,1024]{1,0:T(8,128)(2,1)S(1)} %collective-permute-done.15, bf16[256,1024]{1,0:T(8,128)(2,1)S(1)} %collective-permute-done.16), kind=kOutput, calls=%fused_computation | convolution fusion | flops 538968064 | bytes 7340032 | tf_op jit(solution)/shard_map/dot_general | solution.py:318
  (56 shorter events, 4.8 us)
Async XLA Ops:
  0.6 19.3 %collective-permute-start = (bf16[8,8,256,128]{3,2,1,0:T(8,128)(2,1)}, bf16[8,8,256,128]{3,2,1,0:T(8,128)(2,1)}, u32[]{:S(2)}, u32[]{:S(2)}) collective-permute-start(bf16[8,8,256,128]{3,2,1,0:T(8,128)(2,1)} %ko.1), channel_id=1, source_target_pairs={{0,16},{16,0},{1,17},{17,1},{2,18},{18,2},{3,19},{19,3},{4,20},{20... | collective-permute-start | bytes 12582920 | tf_op jit(solution)/shard_map/ppermute | solution.py:35
  4.0 16.0 %collective-permute-start.1 = (bf16[8,8,256,128]{3,2,1,0:T(8,128)(2,1)}, bf16[8,8,256,128]{3,2,1,0:T(8,128)(2,1)}, u32[]{:S(2)}, u32[]{:S(2)}) collective-permute-start(bf16[8,8,256,128]{3,2,1,0:T(8,128)(2,1)} %vo.1), channel_id=1, source_target_pairs={{0,16},{16,0},{1,17},{17,1},{2,18},{18,2},{3,19},{19,3},{4,20},{20... | collective-permute-start | bytes 12582920 | tf_op jit(solution)/shard_map/ppermute | solution.py:35
  5.8 14.1 %all-to-all-start = ((bf16[16,4,32,128]{3,2,1,0:T(8,128)(2,1)}), bf16[16,4,32,128]{3,2,1,0:T(8,128)(2,1)S(1)}, u32[]{:S(2)}, u32[]{:S(2)}) async-start(bf16[16,4,32,128]{3,2,1,0:T(8,128)(2,1)} %bitcast.8), calls=%async_computation | async-start | bytes 1048576 | tf_op jit(solution)/shard_map/all_to_all | solution.py:259
  19.9 10.6 %copy-start = (bf16[1024,1024]{1,0:T(8,128)(2,1)S(1)}, bf16[1024,1024]{1,0:T(8,128)(2,1)}, u32[]{:S(2)}) copy-start(bf16[1024,1024]{1,0:T(8,128)(2,1)} %refs_10_.1) | copy-start | bytes 6291460
  19.9 12.0 %copy-start.1 = (f32[1024]{0:T(1024)S(1)}, f32[1024]{0:T(1024)}, u32[]{:S(2)}) copy-start(f32[1024]{0:T(1024)} %param.15) | copy-start | bytes 12292
  27.0 12.7 %all-to-all-start.1 = ((bf16[8,272,128]{2,1,0:T(8,128)(2,1)}), bf16[8,272,128]{2,1,0:T(8,128)(2,1)S(1)}, u32[]{:S(2)}, u32[]{:S(2)}) async-start(bf16[8,272,128]{2,1,0:T(8,128)(2,1)} %attend.1), calls=%async_computation.1 | async-start | bytes 1114112 | tf_op jit(solution)/shard_map/all_to_all | solution.py:271
  30.6 26.3 %collective-permute-start.12 = (bf16[1024,1024]{1,0:T(8,128)(2,1)S(1)}, bf16[1024,1024]{1,0:T(8,128)(2,1)}, u32[]{:S(2)}, u32[]{:S(2)}) collective-permute-start(bf16[1024,1024]{1,0:T(8,128)(2,1)S(1)} %copy-done), channel_id=1, source_target_pairs={{0,16},{16,0},{1,17},{17,1},{2,18},{18,2},{3,19},{19,3},{4,20},{20... | collective-permute-start | bytes 6291464 | tf_op jit(solution)/shard_map/ppermute | solution.py:35
  31.9 8.7 %collective-permute-start.2 = (f32[1024]{0:T(1024)S(1)}, f32[1024]{0:T(1024)S(1)}, u32[]{:S(2)}, u32[]{:S(2)}) collective-permute-start(f32[1024]{0:T(1024)S(1)} %copy-done.1), channel_id=1, source_target_pairs={{0,16},{16,0},{1,17},{17,1},{2,18},{18,2},{3,19},{19,3},{4,20},{20... | collective-permute-start | bytes 12296 | tf_op jit(solution)/shard_map/ppermute | solution.py:35
  40.4 33.2 %copy-start.3 = (bf16[32,1024]{1,0:T(8,128)(2,1)S(1)}, bf16[32,1024]{1,0:T(8,128)(2,1)}, u32[]{:S(2)}) copy-start(bf16[32,1024]{1,0:T(8,128)(2,1)} %param.17) | copy-start | bytes 196612
  40.7 9.8 %collective-permute-start.5 = (bf16[2,16,1024]{2,1,0:T(8,128)(2,1)S(1)}, bf16[2,16,1024]{2,1,0:T(8,128)(2,1)S(1)}, u32[]{:S(2)}, u32[]{:S(2)}) collective-permute-start(bf16[2,16,1024]{2,1,0:T(8,128)(2,1)S(1)} %pad_maximum_fusion.2), channel_id=1, source_target_pairs={{0,8},{4,12},{8,0},{12,4},{1,9},{5,13},{9,1},{13,5},{2,10},{6,14},... | collective-permute-start | bytes 196616 | tf_op jit(solution)/shard_map/ppermute | solution.py:31
  46.9 6.9 %collective-permute-start.3 = (bf16[2,16,1024]{2,1,0:T(8,128)(2,1)S(1)}, bf16[2,16,1024]{2,1,0:T(8,128)(2,1)S(1)}, u32[]{:S(2)}, u32[]{:S(2)}) collective-permute-start(bf16[2,16,1024]{2,1,0:T(8,128)(2,1)S(1)} %pad_maximum_fusion.2), channel_id=1, source_target_pairs={{0,4},{4,8},{8,12},{12,0},{1,5},{5,9},{9,13},{13,1},{2,6},{6,10},{... | collective-permute-start | bytes 196616 | tf_op jit(solution)/shard_map/ppermute | solution.py:31
  48.4 7.6 %collective-permute-start.4 = (bf16[2,16,1024]{2,1,0:T(8,128)(2,1)S(1)}, bf16[2,16,1024]{2,1,0:T(8,128)(2,1)S(1)}, u32[]{:S(2)}, u32[]{:S(2)}) collective-permute-start(bf16[2,16,1024]{2,1,0:T(8,128)(2,1)S(1)} %pad_maximum_fusion.2), channel_id=1, source_target_pairs={{0,12},{4,0},{8,4},{12,8},{1,13},{5,1},{9,5},{13,9},{2,14},{6,2},{... | collective-permute-start | bytes 196616 | tf_op jit(solution)/shard_map/ppermute | solution.py:31
  50.5 6.5 %collective-permute-start.11 = (bf16[2,2,16,1024]{3,2,1,0:T(8,128)(2,1)S(1)}, bf16[2,2,16,1024]{3,2,1,0:T(8,128)(2,1)S(1)}, u32[]{:S(2)}, u32[]{:S(2)}) collective-permute-start(bf16[2,2,16,1024]{3,2,1,0:T(8,128)(2,1)S(1)} %pad_maximum_fusion.1.refs_1_), channel_id=1, source_target_pairs={{0,2},{1,3},{2,0},{3,1},{4,6},{5,7},{6,4},{7,5},{8,10},{9,11},{10,... | collective-permute-start | bytes 393224 | tf_op jit(solution)/shard_map/ppermute | solution.py:31
  53.4 6.4 %collective-permute-start.7 = (bf16[2,2,16,1024]{3,2,1,0:T(8,128)(2,1)S(1)}, bf16[2,2,16,1024]{3,2,1,0:T(8,128)(2,1)S(1)}, u32[]{:S(2)}, u32[]{:S(2)}) collective-permute-start(bf16[2,2,16,1024]{3,2,1,0:T(8,128)(2,1)S(1)} %pad_maximum_fusion.1.refs_1_), channel_id=1, source_target_pairs={{0,1},{1,2},{2,3},{3,0},{4,5},{5,6},{6,7},{7,4},{8,9},{9,10},{10,1... | collective-permute-start | bytes 393224 | tf_op jit(solution)/shard_map/ppermute | solution.py:31
  53.8 7.0 %collective-permute-start.9 = (bf16[2,2,16,1024]{3,2,1,0:T(8,128)(2,1)S(1)}, bf16[2,2,16,1024]{3,2,1,0:T(8,128)(2,1)S(1)}, u32[]{:S(2)}, u32[]{:S(2)}) collective-permute-start(bf16[2,2,16,1024]{3,2,1,0:T(8,128)(2,1)S(1)} %pad_maximum_fusion.1.refs_1_), channel_id=1, source_target_pairs={{0,3},{1,0},{2,1},{3,2},{4,7},{5,4},{6,5},{7,6},{8,11},{9,8},{10,9... | collective-permute-start | bytes 393224 | tf_op jit(solution)/shard_map/ppermute | solution.py:31
  56.1 6.8 %collective-permute-start.10 = (bf16[2,2,16,1024]{3,2,1,0:T(8,128)(2,1)S(1)}, bf16[2,2,16,1024]{3,2,1,0:T(8,128)(2,1)S(1)}, u32[]{:S(2)}, u32[]{:S(2)}) collective-permute-start(bf16[2,2,16,1024]{3,2,1,0:T(8,128)(2,1)S(1)} %pad_maximum_fusion.refs_0_), channel_id=1, source_target_pairs={{0,2},{1,3},{2,0},{3,1},{4,6},{5,7},{6,4},{7,5},{8,10},{9,11},{10,... | collective-permute-start | bytes 393224 | tf_op jit(solution)/shard_map/ppermute | solution.py:31
  56.9 7.8 %collective-permute-start.6 = (bf16[2,2,16,1024]{3,2,1,0:T(8,128)(2,1)S(1)}, bf16[2,2,16,1024]{3,2,1,0:T(8,128)(2,1)S(1)}, u32[]{:S(2)}, u32[]{:S(2)}) collective-permute-start(bf16[2,2,16,1024]{3,2,1,0:T(8,128)(2,1)S(1)} %pad_maximum_fusion.refs_0_), channel_id=1, source_target_pairs={{0,1},{1,2},{2,3},{3,0},{4,5},{5,6},{6,7},{7,4},{8,9},{9,10},{10,1... | collective-permute-start | bytes 393224 | tf_op jit(solution)/shard_map/ppermute | solution.py:31
  57.1 7.9 %collective-permute-start.8 = (bf16[2,2,16,1024]{3,2,1,0:T(8,128)(2,1)S(1)}, bf16[2,2,16,1024]{3,2,1,0:T(8,128)(2,1)S(1)}, u32[]{:S(2)}, u32[]{:S(2)}) collective-permute-start(bf16[2,2,16,1024]{3,2,1,0:T(8,128)(2,1)S(1)} %pad_maximum_fusion.refs_0_), channel_id=1, source_target_pairs={{0,3},{1,0},{2,1},{3,2},{4,7},{5,4},{6,5},{7,6},{8,11},{9,8},{10,9... | collective-permute-start | bytes 393224 | tf_op jit(solution)/shard_map/ppermute | solution.py:31
  69.5 20.7 %copy-start.4 = (bf16[256,1024]{1,0:T(8,128)(2,1)S(1)}, bf16[256,1024]{1,0:T(8,128)(2,1)}, u32[]{:S(2)}) copy-start(bf16[256,1024]{1,0:T(8,128)(2,1)} %get-tuple-element.9) | copy-start | bytes 1572868
  69.5 29.2 %copy-start.2 = (bf16[256,1024]{1,0:T(8,128)(2,1)S(1)}, bf16[256,1024]{1,0:T(8,128)(2,1)}, u32[]{:S(2)}) copy-start(bf16[256,1024]{1,0:T(8,128)(2,1)} %get-tuple-element.11) | copy-start | bytes 1572868
  69.5 12.2 %all-to-all-start.2 = ((bf16[8,32,1152]{2,1,0:T(8,128)(2,1)}), bf16[8,32,1152]{2,1,0:T(8,128)(2,1)S(1)}, u32[]{:S(2)}, u32[]{:S(2)}) async-start(bf16[8,32,1152]{2,1,0:T(8,128)(2,1)} %bitcast.23), calls=%async_computation.2 | async-start | bytes 1179648 | tf_op jit(solution)/shard_map/all_to_all | solution.py:298
  73.7 3.6 %collective-permute-start.13 = (bf16[16,1024]{1,0:T(8,128)(2,1)S(1)}, bf16[16,1024]{1,0:T(8,128)(2,1)S(1)}, u32[]{:S(2)}, u32[]{:S(2)}) collective-permute-start(bf16[16,1024]{1,0:T(8,128)(2,1)S(1)} %constant_dynamic-slice_fusion), channel_id=1, source_target_pairs={{0,16},{16,0},{1,17},{17,1},{2,18},{18,2},{3,19},{19,3},{4,20},{20... | collective-permute-start | bytes 98312 | tf_op jit(solution)/shard_map/ppermute | solution.py:35
  82.8 11.0 %all-to-all-start.3 = ((bf16[8,32,1024]{2,1,0:T(8,128)(2,1)}), bf16[8,32,1024]{2,1,0:T(8,128)(2,1)S(1)}, u32[]{:S(2)}, u32[]{:S(2)}) async-start(bf16[8,32,1024]{2,1,0:T(8,128)(2,1)} %broadcast_in_dim.14), calls=%async_computation.3 | async-start | bytes 1048576 | tf_op jit(solution)/shard_map/all_to_all | solution.py:18
  86.3 4.7 %collective-permute-start.14 = (bf16[16,1024]{1,0:T(8,128)(2,1)S(1)}, bf16[16,1024]{1,0:T(8,128)(2,1)S(1)}, u32[]{:S(2)}, u32[]{:S(2)}) collective-permute-start(bf16[16,1024]{1,0:T(8,128)(2,1)S(1)} %broadcast_select_fusion.3), channel_id=1, source_target_pairs={{0,16},{16,0},{1,17},{17,1},{2,18},{18,2},{3,19},{19,3},{4,20},{20... | collective-permute-start | bytes 98312 | tf_op jit(solution)/shard_map/ppermute | solution.py:35
  90.1 9.3 %collective-permute-start.15 = (bf16[256,1024]{1,0:T(8,128)(2,1)S(1)}, bf16[256,1024]{1,0:T(8,128)(2,1)S(1)}, u32[]{:S(2)}, u32[]{:S(2)}) collective-permute-start(bf16[256,1024]{1,0:T(8,128)(2,1)S(1)} %copy-done.4), channel_id=1, source_target_pairs={{0,16},{16,0},{1,17},{17,1},{2,18},{18,2},{3,19},{19,3},{4,20},{20... | collective-permute-start | bytes 1572872 | tf_op jit(solution)/shard_map/ppermute | solution.py:35
  93.8 6.4 %collective-permute-start.16 = (bf16[256,1024]{1,0:T(8,128)(2,1)S(1)}, bf16[256,1024]{1,0:T(8,128)(2,1)S(1)}, u32[]{:S(2)}, u32[]{:S(2)}) collective-permute-start(bf16[256,1024]{1,0:T(8,128)(2,1)S(1)} %bitcast.38), channel_id=1, source_target_pairs={{0,16},{16,0},{1,17},{17,1},{2,18},{18,2},{3,19},{19,3},{4,20},{20... | collective-permute-start | bytes 1572872 | tf_op jit(solution)/shard_map/ppermute | solution.py:35

commit v6 on v5

--- a/solution.py
+++ b/solution.py
@@ -35,7 +35,9 @@
     return lax.ppermute(x, "c", [(0, 1), (1, 0)])
 
 
-def attend_kernel(steps, meta, q_ref, ko, vo, ks, vs, new_ref, out_ref, buf, lse_ref, sems):
+def attend_kernel(
+    steps, meta, q_ref, ko, vo, ks, vs, new_ref, sent, buf, out_ref, lse_ref, sems, out_sems
+):
     half = buf.shape[1]
     kv_heads, block, head_size = buf.shape[2:]
     q_rows = q_ref.shape[1] * q_ref.shape[3]
@@ -114,8 +116,13 @@
             lse = jnp.where(top > -1e29, top + jnp.log2(total), -1e30)
             lse_ref[k, :q_rows, :] = jnp.where(column == i, lse, lse_ref[k, :q_rows, :])
 
+    def send(i):
+        rows = pl.ds(i * q_rows, q_rows if i < half else TILE)
+        return pltpu.make_async_copy(out_ref.at[:, rows], sent.at[:, rows], out_sems.at[i])
+
     for i in range(half):
         one(i)
+        send(i).start()
 
     for k in range(kv_heads):
         x = lse_ref[k].T[:half]
@@ -124,6 +131,9 @@
         c = x - a - b
         rows = jnp.concatenate([a, b, c, jnp.zeros((TILE - 3 * half, 128), jnp.float32)], 0)
         out_ref[k, half * q_rows :, :] = rows.astype(jnp.bfloat16)
+    send(half).start()
+    for i in range(half + 1):
+        send(i).wait()
 
 
 def attend(steps, meta, heads, own_k, own_v, sib_k, sib_v, fresh):
@@ -136,13 +146,15 @@
     return pl.pallas_call(
         functools.partial(attend_kernel, steps),
         in_specs=[pl.BlockSpec(memory_space=pltpu.SMEM), vmem, hbm, hbm, hbm, hbm, vmem],
-        out_specs=vmem,
+        out_specs=pl.BlockSpec(memory_space=pl.ANY),
         scratch_shapes=[
             pltpu.VMEM((4, half, kv_heads, block, head_size), jnp.bfloat16),
+            pltpu.VMEM((kv_heads, out_rows, head_size), jnp.bfloat16),
             pltpu.VMEM((kv_heads, 128, 128), jnp.float32),
             pltpu.SemaphoreType.DMA((4, half)),
+            pltpu.SemaphoreType.DMA((half + 1,)),
         ],
-        out_shape=jax.ShapeDtypeStruct((kv_heads, out_rows, head_size), jnp.bfloat16),
+        out_shape=pltpu.HBM((kv_heads, out_rows, head_size), jnp.bfloat16),
         compiler_params=pltpu.CompilerParams(vmem_limit_bytes=28 * 1024 * 1024),
         cost_estimate=pl.CostEstimate(
             flops=half * kv_heads * q_rows * 2 * block * head_size * 4,
@@ -154,8 +166,9 @@
 
 
 def project_kernel(tile, place, *refs):
-    blocks, refs = refs[:-10], refs[-10:]
-    g_own, g_sib, w_own, w_sib, out_ref, own_out, sib_out, own_ref, sib_ref, sems = refs
+    blocks, refs = refs[:-11], refs[-11:]
+    g_own, g_sib, w_own, w_sib, sent, own_out, sib_out = refs[:7]
+    own_ref, sib_ref, out_ref, sems = refs[7:]
     hrows = blocks[0].shape[2]
     feats, cols = w_own.shape
     for n, ref in enumerate(blocks):
@@ -172,11 +185,19 @@
     ]
     for copy in copies:
         copy.start()
+    def send(n, start, size):
+        cut = pl.ds(start, size)
+        copy = pltpu.make_async_copy(out_ref.at[:, cut], sent.at[:, cut], sems.at[n])
+        copy.start()
+        copies.append(copy)
+
     own, sib = own_ref[...], sib_ref[...]
     for t in range(0, cols, tile):
         acc = jnp.dot(own, w_own[:, t : t + tile], preferred_element_type=jnp.float32)
         acc += jnp.dot(sib, w_sib[:, t : t + tile], preferred_element_type=jnp.float32)
         out_ref[:, t : t + tile] = acc.astype(jnp.bfloat16)
+        if t + tile < cols:
+            send(2 + t // tile, t, tile)
     sq = 0.0
     for t in range(0, feats, 128):
         a = own_ref[:, t : t + 128].astype(jnp.float32) * (1.0 / g_own[:, t : t + 128])
@@ -188,6 +209,8 @@
     lane = lax.broadcasted_iota(jnp.int32, (sq.shape[0], 128), 1)
     pieces = jnp.where(lane == 0, a, jnp.where(lane == 1, b, sq - a - b))
     out_ref[:, cols:] = jnp.where(lane < 3, pieces, 0.0).astype(jnp.bfloat16)
+    last = cols - tile
+    send(2 + last // tile, last, tile + 128)
     for copy in copies:
         copy.wait()
 
@@ -199,18 +222,19 @@
     vmem = pl.BlockSpec(memory_space=pltpu.VMEM)
     hbm = pl.BlockSpec(memory_space=pl.ANY)
     outs = (
-        jax.ShapeDtypeStruct((rows, cols + 128), jnp.bfloat16),
+        pltpu.HBM((rows, cols + 128), jnp.bfloat16),
         pltpu.HBM((rows, feats), jnp.bfloat16),
         pltpu.HBM((rows, feats), jnp.bfloat16),
     )
     return pl.pallas_call(
         functools.partial(project_kernel, 256),
         in_specs=[pl.BlockSpec(memory_space=pltpu.SMEM)] + [vmem] * (len(blocks) + 4),
-        out_specs=(vmem, hbm, hbm),
+        out_specs=(hbm, hbm, hbm),
         scratch_shapes=[
             pltpu.VMEM((rows, feats), jnp.bfloat16),
             pltpu.VMEM((rows, feats), jnp.bfloat16),
-            pltpu.SemaphoreType.DMA((2,)),
+            pltpu.VMEM((rows, cols + 128), jnp.bfloat16),
+            pltpu.SemaphoreType.DMA((2 + cols // 256,)),
         ],
         out_shape=outs,
         compiler_params=pltpu.CompilerParams(vmem_limit_bytes=24 * 1024 * 1024),

time: 103 us -> 102 us (level)
  transfers between devices with their start and end apart: 21 -> 21, of which waited for: 12 -> 11; matrix products, arithmetic and copies ran while one was open for 6% -> 6% of each run, Pallas kernels for 0% -> 0%
where the time goes in v6:
time: 102 us; the launch traced here: 101 us
  starting transfers between devices  51.3 us (50%)
  waiting for transfers between devices  29.4 us (29%)
  Pallas kernels  10.7 us (10%)
  other arithmetic  3.33 us (3%)
  local copies, waits for them, and re-layouts  2.94 us (3%)
  matrix products  2.82 us (3%)
    ppermute x9, starting transfers between devices, shift(): return lax.ppermute(x, axis, [(j, (j + k) % n) for j in range(n)])  18.4 us
    ppermute x8, starting transfers between devices, swap(): return lax.ppermute(x, 'c', [(0, 1), (1, 0)])  16.9 us
    all_to_all x1, waiting for transfers between devices, per_device(): lax.all_to_all(spread, TP, 0, 0)  8.11 us
    all_to_all x1, waiting for transfers between devices, per_device(): got = lax.all_to_all(sent, 'ch', 0, 0)  7.88 us
    pallas_call x1, Pallas kernels, attend(): pl.pallas_call(functools.partial(attend_kernel, steps), in_specs=[pl.Bloc...  6.96 us
    ppermute x9, waiting for transfers between devices, shift(): return lax.ppermute(x, axis, [(j, (j + k) % n) for j in range(n)])  4.86 us
    all_to_all x1, starting transfers between devices, per_device(): parts = lax.all_to_all(payload, 'ch', 0, 0)  4.67 us
    all_to_all x1, starting transfers between devices, per_device(): lax.all_to_all(spread, TP, 0, 0)  4.34 us
  transfers between devices with their start and end apart: 21, of which 11 were waited for; matrix products, arithmetic and copies ran while one was open for 6% of the time, Pallas kernels for 0%

profile of v6, /device:TPU:1, one launch (start us, length us, event | category | flops | bytes accessed | tf_op | source)
XLA Modules:
  0.0 101.4 jit_solution(9005177812230111805)
XLA Ops:
  0.6 3.3 %collective-permute-start = (bf16[8,8,256,128]{3,2,1,0:T(8,128)(2,1)}, bf16[8,8,256,128]{3,2,1,0:T(8,128)(2,1)}, u32[]{:S(2)}, u32[]{:S(2)}) collective-permute-start(bf16[8,8,256,128]{3,2,1,0:T(8,128)(2,1)} %ko.1), channel_id=1, source_target_pairs={{0,16},{16,0},{1,17},{17,1},{2,18},{18,2},{3,19},{19,3},{4,20},{20... | collective-permute-start | bytes 12582920 | tf_op jit(solution)/shard_map/ppermute | solution.py:35
  4.1 1.7 %broadcast_in_dim.11 = bf16[8,2,4,32,128]{4,3,2,1,0:T(8,128)(2,1)} broadcast(bf16[2,4,32,128]{3,2,1,0:T(8,128)(2,1)} %bitcast.45), dimensions={1,2,3,4} | broadcast | bytes 589824 | tf_op jit(solution)/shard_map/broadcast_in_dim | solution.py:273
  5.8 4.3 %all-to-all-start = ((bf16[16,4,32,128]{3,2,1,0:T(8,128)(2,1)}), bf16[16,4,32,128]{3,2,1,0:T(8,128)(2,1)S(1)}, u32[]{:S(2)}, u32[]{:S(2)}) async-start(bf16[16,4,32,128]{3,2,1,0:T(8,128)(2,1)} %bitcast.8), calls=%async_computation | async-start | bytes 1048576 | tf_op jit(solution)/shard_map/all_to_all | solution.py:283
  10.9 1.0 convert_bitcast_fusion.new_ref
  11.8 8.1 %all-to-all-done = bf16[16,4,32,128]{3,2,1,0:T(8,128)(2,1)S(1)} async-done(((bf16[16,4,32,128]{3,2,1,0:T(8,128)(2,1)}), bf16[16,4,32,128]{3,2,1,0:T(8,128)(2,1)S(1)}, u32[]{:S(2)}, u32[]{:S(2)}) %all-to-all-start) | async-done | bytes 524320 | tf_op jit(solution)/shard_map/all_to_all | solution.py:283
  20.0 7.0 %attend.1 = bf16[8,272,128]{2,1,0:T(8,128)(2,1)} custom-call(s32[11]{0:T(128)S(1)} %pad_add_fusion.1.meta, bf16[8,2,4,32,128]{4,3,2,1,0:T(8,128)(2,1)S(1)} %bitcast.35, bf16[8,8,256,128]{3,2,1,0:T(8,128)(2,1)} %ko.1, bf16[8,8,256,128]{3,2,1,0:T(8,128)(2,1)} %vo.1, bf16[8,8,256,128]{3,2,1,0:T(8,128)(2,1)} %collective-permute-done.ks, ...), custom_call_target="tpu_custom_call" | custom-call | flops 536870912 | bytes 8388608 | tf_op jit(solution)/shard_map/attend/pallas_call | solution.py:146
  26.9 3.5 %all-to-all-start.1 = ((bf16[8,272,128]{2,1,0:T(8,128)(2,1)}), bf16[8,272,128]{2,1,0:T(8,128)(2,1)S(1)}, u32[]{:S(2)}, u32[]{:S(2)}) async-start(bf16[8,272,128]{2,1,0:T(8,128)(2,1)} %attend.1), calls=%async_computation.1 | async-start | bytes 1114112 | tf_op jit(solution)/shard_map/all_to_all | solution.py:295
  30.5 1.3 %collective-permute-start.12 = (bf16[1024,1024]{1,0:T(8,128)(2,1)S(1)}, bf16[1024,1024]{1,0:T(8,128)(2,1)}, u32[]{:S(2)}, u32[]{:S(2)}) collective-permute-start(bf16[1024,1024]{1,0:T(8,128)(2,1)S(1)} %copy-done), channel_id=1, source_target_pairs={{0,16},{16,0},{1,17},{17,1},{2,18},{18,2},{3,19},{19,3},{4,20},{20... | collective-permute-start | bytes 6291464 | tf_op jit(solution)/shard_map/ppermute | solution.py:35
  31.9 7.9 %all-to-all-done.1 = bf16[8,272,128]{2,1,0:T(8,128)(2,1)S(1)} async-done(((bf16[8,272,128]{2,1,0:T(8,128)(2,1)}), bf16[8,272,128]{2,1,0:T(8,128)(2,1)S(1)}, u32[]{:S(2)}, u32[]{:S(2)}) %all-to-all-start.1) | async-done | bytes 557088 | tf_op jit(solution)/shard_map/all_to_all | solution.py:295
  40.7 6.0 %collective-permute-start.5 = (bf16[2,16,1024]{2,1,0:T(8,128)(2,1)S(1)}, bf16[2,16,1024]{2,1,0:T(8,128)(2,1)S(1)}, u32[]{:S(2)}, u32[]{:S(2)}) collective-permute-start(bf16[2,16,1024]{2,1,0:T(8,128)(2,1)S(1)} %pad_maximum_fusion.2), channel_id=1, source_target_pairs={{0,8},{4,12},{8,0},{12,4},{1,9},{5,13},{9,1},{13,5},{2,10},{6,14},... | collective-permute-start | bytes 196616 | tf_op jit(solution)/shard_map/ppermute | solution.py:31
  46.7 1.6 %collective-permute-start.3 = (bf16[2,16,1024]{2,1,0:T(8,128)(2,1)S(1)}, bf16[2,16,1024]{2,1,0:T(8,128)(2,1)S(1)}, u32[]{:S(2)}, u32[]{:S(2)}) collective-permute-start(bf16[2,16,1024]{2,1,0:T(8,128)(2,1)S(1)} %pad_maximum_fusion.2), channel_id=1, source_target_pairs={{0,4},{4,8},{8,12},{12,0},{1,5},{5,9},{9,13},{13,1},{2,6},{6,10},{... | collective-permute-start | bytes 196616 | tf_op jit(solution)/shard_map/ppermute | solution.py:31
  48.3 2.0 %collective-permute-start.4 = (bf16[2,16,1024]{2,1,0:T(8,128)(2,1)S(1)}, bf16[2,16,1024]{2,1,0:T(8,128)(2,1)S(1)}, u32[]{:S(2)}, u32[]{:S(2)}) collective-permute-start(bf16[2,16,1024]{2,1,0:T(8,128)(2,1)S(1)} %pad_maximum_fusion.2), channel_id=1, source_target_pairs={{0,12},{4,0},{8,4},{12,8},{1,13},{5,1},{9,5},{13,9},{2,14},{6,2},{... | collective-permute-start | bytes 196616 | tf_op jit(solution)/shard_map/ppermute | solution.py:31
  50.3 2.9 %collective-permute-start.11 = (bf16[2,2,16,1024]{3,2,1,0:T(8,128)(2,1)S(1)}, bf16[2,2,16,1024]{3,2,1,0:T(8,128)(2,1)S(1)}, u32[]{:S(2)}, u32[]{:S(2)}) collective-permute-start(bf16[2,2,16,1024]{3,2,1,0:T(8,128)(2,1)S(1)} %pad_maximum_fusion.1.refs_1_), channel_id=1, source_target_pairs={{0,2},{1,3},{2,0},{3,1},{4,6},{5,7},{6,4},{7,5},{8,10},{9,11},{10,... | collective-permute-start | bytes 393224 | tf_op jit(solution)/shard_map/ppermute | solution.py:31
  53.7 2.2 %collective-permute-start.9 = (bf16[2,2,16,1024]{3,2,1,0:T(8,128)(2,1)S(1)}, bf16[2,2,16,1024]{3,2,1,0:T(8,128)(2,1)S(1)}, u32[]{:S(2)}, u32[]{:S(2)}) collective-permute-start(bf16[2,2,16,1024]{3,2,1,0:T(8,128)(2,1)S(1)} %pad_maximum_fusion.1.refs_1_), channel_id=1, source_target_pairs={{0,3},{1,0},{2,1},{3,2},{4,7},{5,4},{6,5},{7,6},{8,11},{9,8},{10,9... | collective-permute-start | bytes 393224 | tf_op jit(solution)/shard_map/ppermute | solution.py:31
  57.2 2.0 %collective-permute-start.8 = (bf16[2,2,16,1024]{3,2,1,0:T(8,128)(2,1)S(1)}, bf16[2,2,16,1024]{3,2,1,0:T(8,128)(2,1)S(1)}, u32[]{:S(2)}, u32[]{:S(2)}) collective-permute-start(bf16[2,2,16,1024]{3,2,1,0:T(8,128)(2,1)S(1)} %pad_maximum_fusion.refs_0_), channel_id=1, source_target_pairs={{0,3},{1,0},{2,1},{3,2},{4,7},{5,4},{6,5},{7,6},{8,11},{9,8},{10,9... | collective-permute-start | bytes 393224 | tf_op jit(solution)/shard_map/ppermute | solution.py:31
  59.6 1.0 collective-permute-done.9.refs_5_
  60.6 1.8 %collective-permute-done.10.refs_6_ = bf16[2,2,16,1024]{3,2,1,0:T(8,128)(2,1)S(1)} collective-permute-done((bf16[2,2,16,1024]{3,2,1,0:T(8,128)(2,1)S(1)}, bf16[2,2,16,1024]{3,2,1,0:T(8,128)(2,1)S(1)}, u32[]{:S(2)}, u32[]{:S(2)}) %collective-permute-start.10) | collective-permute-done | bytes 131104 | tf_op jit(solution)/shard_map/ppermute | solution.py:31
  62.4 1.7 %collective-permute-done.6.refs_2_ = bf16[2,2,16,1024]{3,2,1,0:T(8,128)(2,1)S(1)} collective-permute-done((bf16[2,2,16,1024]{3,2,1,0:T(8,128)(2,1)S(1)}, bf16[2,2,16,1024]{3,2,1,0:T(8,128)(2,1)S(1)}, u32[]{:S(2)}, u32[]{:S(2)}) %collective-permute-start.6) | collective-permute-done | bytes 131104 | tf_op jit(solution)/shard_map/ppermute | solution.py:31
  64.1 3.8 %project.1 = (bf16[256,1152]{1,0:T(8,128)(2,1)}, bf16[256,1024]{1,0:T(8,128)(2,1)}, bf16[256,1024]{1,0:T(8,128)(2,1)}) custom-call(s32[2]{0:T(128)S(1)} %pad_add_fusion.place, bf16[2,2,16,1024]{3,2,1,0:T(8,128)(2,1)S(1)} %pad_maximum_fusion.refs_0_, bf16[2,2,16,1024]{3,2,1,0:T(8,128)(2,1)S(1)} %pad_maximum_fusion.1.refs_1_, ...), custom_call_target="tpu_custom_call" | custom-call | flops 1073741824 | bytes 4194304 | tf_op jit(solution)/shard_map/project/pallas_call | solution.py:229
  67.9 4.7 %all-to-all-start.2 = ((bf16[8,32,1152]{2,1,0:T(8,128)(2,1)}), bf16[8,32,1152]{2,1,0:T(8,128)(2,1)S(1)}, u32[]{:S(2)}, u32[]{:S(2)}) async-start(bf16[8,32,1152]{2,1,0:T(8,128)(2,1)} %bitcast.40), calls=%async_computation.2 | async-start | bytes 1179648 | tf_op jit(solution)/shard_map/all_to_all | solution.py:322
  72.6 2.9 %collective-permute-start.13 = (bf16[16,1024]{1,0:T(8,128)(2,1)S(1)}, bf16[16,1024]{1,0:T(8,128)(2,1)S(1)}, u32[]{:S(2)}, u32[]{:S(2)}) collective-permute-start(bf16[16,1024]{1,0:T(8,128)(2,1)S(1)} %constant_dynamic-slice_fusion), channel_id=1, source_target_pairs={{0,16},{16,0},{1,17},{17,1},{2,18},{18,2},{3,19},{19,3},{4,20},{20... | collective-permute-start | bytes 98312 | tf_op jit(solution)/shard_map/ppermute | solution.py:35
  75.5 0.9 collective-permute-done.13
  76.4 4.2 %all-to-all-done.2 = bf16[8,32,1152]{2,1,0:T(8,128)(2,1)S(1)} async-done(((bf16[8,32,1152]{2,1,0:T(8,128)(2,1)}), bf16[8,32,1152]{2,1,0:T(8,128)(2,1)S(1)}, u32[]{:S(2)}, u32[]{:S(2)}) %all-to-all-start.2) | async-done | bytes 589856 | tf_op jit(solution)/shard_map/all_to_all | solution.py:322
  80.9 0.9 broadcast_in_dim.14
  81.8 3.5 %all-to-all-start.3 = ((bf16[8,32,1024]{2,1,0:T(8,128)(2,1)}), bf16[8,32,1024]{2,1,0:T(8,128)(2,1)S(1)}, u32[]{:S(2)}, u32[]{:S(2)}) async-start(bf16[8,32,1024]{2,1,0:T(8,128)(2,1)} %broadcast_in_dim.14), calls=%async_computation.3 | async-start | bytes 1048576 | tf_op jit(solution)/shard_map/all_to_all | solution.py:18
  85.3 4.0 %collective-permute-start.14 = (bf16[16,1024]{1,0:T(8,128)(2,1)S(1)}, bf16[16,1024]{1,0:T(8,128)(2,1)S(1)}, u32[]{:S(2)}, u32[]{:S(2)}) collective-permute-start(bf16[16,1024]{1,0:T(8,128)(2,1)S(1)} %broadcast_select_fusion.3), channel_id=1, source_target_pairs={{0,16},{16,0},{1,17},{17,1},{2,18},{18,2},{3,19},{19,3},{4,20},{20... | collective-permute-start | bytes 98312 | tf_op jit(solution)/shard_map/ppermute | solution.py:35
  89.4 0.7 collective-permute-done.14
  90.8 1.9 %all-to-all-done.3 = bf16[8,32,1024]{2,1,0:T(8,128)(2,1)S(1)} async-done(((bf16[8,32,1024]{2,1,0:T(8,128)(2,1)}), bf16[8,32,1024]{2,1,0:T(8,128)(2,1)S(1)}, u32[]{:S(2)}, u32[]{:S(2)}) %all-to-all-start.3) | async-done | bytes 524320 | tf_op jit(solution)/shard_map/all_to_all | solution.py:18
  92.7 5.1 %collective-permute-start.16 = (bf16[256,1024]{1,0:T(8,128)(2,1)S(1)}, bf16[256,1024]{1,0:T(8,128)(2,1)S(1)}, u32[]{:S(2)}, u32[]{:S(2)}) collective-permute-start(bf16[256,1024]{1,0:T(8,128)(2,1)S(1)} %bitcast.38), channel_id=1, source_target_pairs={{0,16},{16,0},{1,17},{17,1},{2,18},{18,2},{3,19},{19,3},{4,20},{20... | collective-permute-start | bytes 1572872 | tf_op jit(solution)/shard_map/ppermute | solution.py:35
  97.8 0.7 fusion.1
  98.6 0.8 collective-permute-done.16
  99.3 2.1 %add_convert_fusion = bf16[1024,1024]{1,0:T(8,128)(2,1)} fusion(f32[1024,1024]{1,0:T(8,128)S(1)} %fusion.1, bf16[256,1024]{1,0:T(8,128)(2,1)S(1)} %collective-permute-done.15, bf16[256,1024]{1,0:T(8,128)(2,1)S(1)} %collective-permute-done.16), kind=kOutput, calls=%fused_computation | convolution fusion | flops 538968064 | bytes 7340032 | tf_op jit(solution)/shard_map/dot_general | solution.py:342
  (56 shorter events, 5.2 us)
Async XLA Ops:
  0.6 19.3 %collective-permute-start = (bf16[8,8,256,128]{3,2,1,0:T(8,128)(2,1)}, bf16[8,8,256,128]{3,2,1,0:T(8,128)(2,1)}, u32[]{:S(2)}, u32[]{:S(2)}) collective-permute-start(bf16[8,8,256,128]{3,2,1,0:T(8,128)(2,1)} %ko.1), channel_id=1, source_target_pairs={{0,16},{16,0},{1,17},{17,1},{2,18},{18,2},{3,19},{19,3},{4,20},{20... | collective-permute-start | bytes 12582920 | tf_op jit(solution)/shard_map/ppermute | solution.py:35
  4.0 16.0 %collective-permute-start.1 = (bf16[8,8,256,128]{3,2,1,0:T(8,128)(2,1)}, bf16[8,8,256,128]{3,2,1,0:T(8,128)(2,1)}, u32[]{:S(2)}, u32[]{:S(2)}) collective-permute-start(bf16[8,8,256,128]{3,2,1,0:T(8,128)(2,1)} %vo.1), channel_id=1, source_target_pairs={{0,16},{16,0},{1,17},{17,1},{2,18},{18,2},{3,19},{19,3},{4,20},{20... | collective-permute-start | bytes 12582920 | tf_op jit(solution)/shard_map/ppermute | solution.py:35
  5.8 14.1 %all-to-all-start = ((bf16[16,4,32,128]{3,2,1,0:T(8,128)(2,1)}), bf16[16,4,32,128]{3,2,1,0:T(8,128)(2,1)S(1)}, u32[]{:S(2)}, u32[]{:S(2)}) async-start(bf16[16,4,32,128]{3,2,1,0:T(8,128)(2,1)} %bitcast.8), calls=%async_computation | async-start | bytes 1048576 | tf_op jit(solution)/shard_map/all_to_all | solution.py:283
  19.9 10.5 %copy-start = (bf16[1024,1024]{1,0:T(8,128)(2,1)S(1)}, bf16[1024,1024]{1,0:T(8,128)(2,1)}, u32[]{:S(2)}) copy-start(bf16[1024,1024]{1,0:T(8,128)(2,1)} %refs_10_.1) | copy-start | bytes 6291460
  19.9 11.8 %copy-start.1 = (f32[1024]{0:T(1024)S(1)}, f32[1024]{0:T(1024)}, u32[]{:S(2)}) copy-start(f32[1024]{0:T(1024)} %param.15) | copy-start | bytes 12292
  26.9 12.8 %all-to-all-start.1 = ((bf16[8,272,128]{2,1,0:T(8,128)(2,1)}), bf16[8,272,128]{2,1,0:T(8,128)(2,1)S(1)}, u32[]{:S(2)}, u32[]{:S(2)}) async-start(bf16[8,272,128]{2,1,0:T(8,128)(2,1)} %attend.1), calls=%async_computation.1 | async-start | bytes 1114112 | tf_op jit(solution)/shard_map/all_to_all | solution.py:295
  30.5 26.0 %collective-permute-start.12 = (bf16[1024,1024]{1,0:T(8,128)(2,1)S(1)}, bf16[1024,1024]{1,0:T(8,128)(2,1)}, u32[]{:S(2)}, u32[]{:S(2)}) collective-permute-start(bf16[1024,1024]{1,0:T(8,128)(2,1)S(1)} %copy-done), channel_id=1, source_target_pairs={{0,16},{16,0},{1,17},{17,1},{2,18},{18,2},{3,19},{19,3},{4,20},{20... | collective-permute-start | bytes 6291464 | tf_op jit(solution)/shard_map/ppermute | solution.py:35
  31.7 8.9 %collective-permute-start.2 = (f32[1024]{0:T(1024)S(1)}, f32[1024]{0:T(1024)S(1)}, u32[]{:S(2)}, u32[]{:S(2)}) collective-permute-start(f32[1024]{0:T(1024)S(1)} %copy-done.1), channel_id=1, source_target_pairs={{0,16},{16,0},{1,17},{17,1},{2,18},{18,2},{3,19},{19,3},{4,20},{20... | collective-permute-start | bytes 12296 | tf_op jit(solution)/shard_map/ppermute | solution.py:35
  40.5 32.1 %copy-start.3 = (bf16[32,1024]{1,0:T(8,128)(2,1)S(1)}, bf16[32,1024]{1,0:T(8,128)(2,1)}, u32[]{:S(2)}) copy-start(bf16[32,1024]{1,0:T(8,128)(2,1)} %param.17) | copy-start | bytes 196612
  40.7 9.6 %collective-permute-start.5 = (bf16[2,16,1024]{2,1,0:T(8,128)(2,1)S(1)}, bf16[2,16,1024]{2,1,0:T(8,128)(2,1)S(1)}, u32[]{:S(2)}, u32[]{:S(2)}) collective-permute-start(bf16[2,16,1024]{2,1,0:T(8,128)(2,1)S(1)} %pad_maximum_fusion.2), channel_id=1, source_target_pairs={{0,8},{4,12},{8,0},{12,4},{1,9},{5,13},{9,1},{13,5},{2,10},{6,14},... | collective-permute-start | bytes 196616 | tf_op jit(solution)/shard_map/ppermute | solution.py:31
  46.7 7.0 %collective-permute-start.3 = (bf16[2,16,1024]{2,1,0:T(8,128)(2,1)S(1)}, bf16[2,16,1024]{2,1,0:T(8,128)(2,1)S(1)}, u32[]{:S(2)}, u32[]{:S(2)}) collective-permute-start(bf16[2,16,1024]{2,1,0:T(8,128)(2,1)S(1)} %pad_maximum_fusion.2), channel_id=1, source_target_pairs={{0,4},{4,8},{8,12},{12,0},{1,5},{5,9},{9,13},{13,1},{2,6},{6,10},{... | collective-permute-start | bytes 196616 | tf_op jit(solution)/shard_map/ppermute | solution.py:31
  48.3 7.6 %collective-permute-start.4 = (bf16[2,16,1024]{2,1,0:T(8,128)(2,1)S(1)}, bf16[2,16,1024]{2,1,0:T(8,128)(2,1)S(1)}, u32[]{:S(2)}, u32[]{:S(2)}) collective-permute-start(bf16[2,16,1024]{2,1,0:T(8,128)(2,1)S(1)} %pad_maximum_fusion.2), channel_id=1, source_target_pairs={{0,12},{4,0},{8,4},{12,8},{1,13},{5,1},{9,5},{13,9},{2,14},{6,2},{... | collective-permute-start | bytes 196616 | tf_op jit(solution)/shard_map/ppermute | solution.py:31
  50.3 6.9 %collective-permute-start.11 = (bf16[2,2,16,1024]{3,2,1,0:T(8,128)(2,1)S(1)}, bf16[2,2,16,1024]{3,2,1,0:T(8,128)(2,1)S(1)}, u32[]{:S(2)}, u32[]{:S(2)}) collective-permute-start(bf16[2,2,16,1024]{3,2,1,0:T(8,128)(2,1)S(1)} %pad_maximum_fusion.1.refs_1_), channel_id=1, source_target_pairs={{0,2},{1,3},{2,0},{3,1},{4,6},{5,7},{6,4},{7,5},{8,10},{9,11},{10,... | collective-permute-start | bytes 393224 | tf_op jit(solution)/shard_map/ppermute | solution.py:31
  53.2 6.4 %collective-permute-start.7 = (bf16[2,2,16,1024]{3,2,1,0:T(8,128)(2,1)S(1)}, bf16[2,2,16,1024]{3,2,1,0:T(8,128)(2,1)S(1)}, u32[]{:S(2)}, u32[]{:S(2)}) collective-permute-start(bf16[2,2,16,1024]{3,2,1,0:T(8,128)(2,1)S(1)} %pad_maximum_fusion.1.refs_1_), channel_id=1, source_target_pairs={{0,1},{1,2},{2,3},{3,0},{4,5},{5,6},{6,7},{7,4},{8,9},{9,10},{10,1... | collective-permute-start | bytes 393224 | tf_op jit(solution)/shard_map/ppermute | solution.py:31
  53.7 6.9 %collective-permute-start.9 = (bf16[2,2,16,1024]{3,2,1,0:T(8,128)(2,1)S(1)}, bf16[2,2,16,1024]{3,2,1,0:T(8,128)(2,1)S(1)}, u32[]{:S(2)}, u32[]{:S(2)}) collective-permute-start(bf16[2,2,16,1024]{3,2,1,0:T(8,128)(2,1)S(1)} %pad_maximum_fusion.1.refs_1_), channel_id=1, source_target_pairs={{0,3},{1,0},{2,1},{3,2},{4,7},{5,4},{6,5},{7,6},{8,11},{9,8},{10,9... | collective-permute-start | bytes 393224 | tf_op jit(solution)/shard_map/ppermute | solution.py:31
  55.9 6.5 %collective-permute-start.10 = (bf16[2,2,16,1024]{3,2,1,0:T(8,128)(2,1)S(1)}, bf16[2,2,16,1024]{3,2,1,0:T(8,128)(2,1)S(1)}, u32[]{:S(2)}, u32[]{:S(2)}) collective-permute-start(bf16[2,2,16,1024]{3,2,1,0:T(8,128)(2,1)S(1)} %pad_maximum_fusion.refs_0_), channel_id=1, source_target_pairs={{0,2},{1,3},{2,0},{3,1},{4,6},{5,7},{6,4},{7,5},{8,10},{9,11},{10,... | collective-permute-start | bytes 393224 | tf_op jit(solution)/shard_map/ppermute | solution.py:31
  56.5 7.6 %collective-permute-start.6 = (bf16[2,2,16,1024]{3,2,1,0:T(8,128)(2,1)S(1)}, bf16[2,2,16,1024]{3,2,1,0:T(8,128)(2,1)S(1)}, u32[]{:S(2)}, u32[]{:S(2)}) collective-permute-start(bf16[2,2,16,1024]{3,2,1,0:T(8,128)(2,1)S(1)} %pad_maximum_fusion.refs_0_), channel_id=1, source_target_pairs={{0,1},{1,2},{2,3},{3,0},{4,5},{5,6},{6,7},{7,4},{8,9},{9,10},{10,1... | collective-permute-start | bytes 393224 | tf_op jit(solution)/shard_map/ppermute | solution.py:31
  57.2 6.9 %collective-permute-start.8 = (bf16[2,2,16,1024]{3,2,1,0:T(8,128)(2,1)S(1)}, bf16[2,2,16,1024]{3,2,1,0:T(8,128)(2,1)S(1)}, u32[]{:S(2)}, u32[]{:S(2)}) collective-permute-start(bf16[2,2,16,1024]{3,2,1,0:T(8,128)(2,1)S(1)} %pad_maximum_fusion.refs_0_), channel_id=1, source_target_pairs={{0,3},{1,0},{2,1},{3,2},{4,7},{5,4},{6,5},{7,6},{8,11},{9,8},{10,9... | collective-permute-start | bytes 393224 | tf_op jit(solution)/shard_map/ppermute | solution.py:31
  67.9 21.4 %copy-start.4 = (bf16[256,1024]{1,0:T(8,128)(2,1)S(1)}, bf16[256,1024]{1,0:T(8,128)(2,1)}, u32[]{:S(2)}) copy-start(bf16[256,1024]{1,0:T(8,128)(2,1)} %get-tuple-element.9) | copy-start | bytes 1572868
  67.9 29.9 %copy-start.2 = (bf16[256,1024]{1,0:T(8,128)(2,1)S(1)}, bf16[256,1024]{1,0:T(8,128)(2,1)}, u32[]{:S(2)}) copy-start(bf16[256,1024]{1,0:T(8,128)(2,1)} %get-tuple-element.11) | copy-start | bytes 1572868
  67.9 12.7 %all-to-all-start.2 = ((bf16[8,32,1152]{2,1,0:T(8,128)(2,1)}), bf16[8,32,1152]{2,1,0:T(8,128)(2,1)S(1)}, u32[]{:S(2)}, u32[]{:S(2)}) async-start(bf16[8,32,1152]{2,1,0:T(8,128)(2,1)} %bitcast.40), calls=%async_computation.2 | async-start | bytes 1179648 | tf_op jit(solution)/shard_map/all_to_all | solution.py:322
  72.6 3.7 %collective-permute-start.13 = (bf16[16,1024]{1,0:T(8,128)(2,1)S(1)}, bf16[16,1024]{1,0:T(8,128)(2,1)S(1)}, u32[]{:S(2)}, u32[]{:S(2)}) collective-permute-start(bf16[16,1024]{1,0:T(8,128)(2,1)S(1)} %constant_dynamic-slice_fusion), channel_id=1, source_target_pairs={{0,16},{16,0},{1,17},{17,1},{2,18},{18,2},{3,19},{19,3},{4,20},{20... | collective-permute-start | bytes 98312 | tf_op jit(solution)/shard_map/ppermute | solution.py:35
  81.8 11.0 %all-to-all-start.3 = ((bf16[8,32,1024]{2,1,0:T(8,128)(2,1)}), bf16[8,32,1024]{2,1,0:T(8,128)(2,1)S(1)}, u32[]{:S(2)}, u32[]{:S(2)}) async-start(bf16[8,32,1024]{2,1,0:T(8,128)(2,1)} %broadcast_in_dim.14), calls=%async_computation.3 | async-start | bytes 1048576 | tf_op jit(solution)/shard_map/all_to_all | solution.py:18
  85.3 4.9 %collective-permute-start.14 = (bf16[16,1024]{1,0:T(8,128)(2,1)S(1)}, bf16[16,1024]{1,0:T(8,128)(2,1)S(1)}, u32[]{:S(2)}, u32[]{:S(2)}) collective-permute-start(bf16[16,1024]{1,0:T(8,128)(2,1)S(1)} %broadcast_select_fusion.3), channel_id=1, source_target_pairs={{0,16},{16,0},{1,17},{17,1},{2,18},{18,2},{3,19},{19,3},{4,20},{20... | collective-permute-start | bytes 98312 | tf_op jit(solution)/shard_map/ppermute | solution.py:35
  89.3 9.3 %collective-permute-start.15 = (bf16[256,1024]{1,0:T(8,128)(2,1)S(1)}, bf16[256,1024]{1,0:T(8,128)(2,1)S(1)}, u32[]{:S(2)}, u32[]{:S(2)}) collective-permute-start(bf16[256,1024]{1,0:T(8,128)(2,1)S(1)} %copy-done.4), channel_id=1, source_target_pairs={{0,16},{16,0},{1,17},{17,1},{2,18},{18,2},{3,19},{19,3},{4,20},{20... | collective-permute-start | bytes 1572872 | tf_op jit(solution)/shard_map/ppermute | solution.py:35
  92.7 6.6 %collective-permute-start.16 = (bf16[256,1024]{1,0:T(8,128)(2,1)S(1)}, bf16[256,1024]{1,0:T(8,128)(2,1)S(1)}, u32[]{:S(2)}, u32[]{:S(2)}) collective-permute-start(bf16[256,1024]{1,0:T(8,128)(2,1)S(1)} %bitcast.38), channel_id=1, source_target_pairs={{0,16},{16,0},{1,17},{17,1},{2,18},{18,2},{3,19},{19,3},{4,20},{20... | collective-permute-start | bytes 1572872 | tf_op jit(solution)/shard_map/ppermute | solution.py:35

commit v7 on v6

--- a/solution.py
+++ b/solution.py
@@ -306,8 +306,10 @@
     raw = jnp.stack([flat_own * norm_gain[None, :], flat_sib * sib_gain[None, :]])
     raw = raw.astype(jnp.bfloat16)
 
-    near = jnp.stack([shift(raw, "zh", 1), shift(raw, "zh", 3)])
-    far = jnp.stack([raw, shift(raw, "zh", 2)])
+    z_1, z_3 = shift(raw, "zh", 1), shift(raw, "zh", 3)
+    near = jnp.stack([z_1, z_3])
+    later, _ = lax.optimization_barrier((raw, z_1))
+    far = jnp.stack([raw, shift(later, "zh", 2)])
     blocks = [near, far]
     for k in (1, 3, 2):
         blocks += [shift(near, "y", k), shift(far, "y", k)]

time: 102 us -> 104 us (1.020)
  waiting for transfers between devices: 29.4 us -> 33.6 us
  starting transfers between devices: 51.3 us -> 49.3 us
    ppermute x8, starting transfers between devices: 16.9 us -> 14.5 us  [swap(): return lax.ppermute(x, 'c', [(0, 1), (1, 0)])]
    ppermute x9, waiting for transfers between devices: 4.86 us -> 6.64 us  [shift(): return lax.ppermute(x, axis, [(j, (j + k) % n) for j in range(n)])]
    all_to_all x1, waiting for transfers between devices: 4.22 us -> 5.37 us  [per_device(): parts = lax.all_to_all(payload, 'ch', 0, 0)]
where the time goes in v7:
time: 104 us
  starting transfers between devices  49.3 us (47%)
  waiting for transfers between devices  33.6 us (32%)
  Pallas kernels  11 us (11%)
  other arithmetic  3.33 us (3%)
  local copies, waits for them, and re-layouts  2.94 us (3%)
  matrix products  2.82 us (3%)
    ppermute x9, starting transfers between devices, shift(): return lax.ppermute(x, axis, [(j, (j + k) % n) for j in range(n)])  17.9 us
    ppermute x8, starting transfers between devices, swap(): return lax.ppermute(x, 'c', [(0, 1), (1, 0)])  14.5 us
    all_to_all x1, waiting for transfers between devices, per_device(): got = lax.all_to_all(sent, 'ch', 0, 0)  8.37 us
    all_to_all x1, waiting for transfers between devices, per_device(): lax.all_to_all(spread, TP, 0, 0)  8.11 us
    pallas_call x1, Pallas kernels, attend(): pl.pallas_call(functools.partial(attend_kernel, steps), in_specs=[pl.Bloc...  7.21 us
    ppermute x9, waiting for transfers between devices, shift(): return lax.ppermute(x, axis, [(j, (j + k) % n) for j in range(n)])  6.64 us
    all_to_all x1, starting transfers between devices, per_device(): parts = lax.all_to_all(payload, 'ch', 0, 0)  5.55 us
    all_to_all x1, waiting for transfers between devices, per_device(): parts = lax.all_to_all(payload, 'ch', 0, 0)  5.37 us
  transfers between devices with their start and end apart: 21, of which 11 were waited for; matrix products, arithmetic and copies ran while one was open for 6% of the time, Pallas kernels for 0%

profile of v7, /device:TPU:1, one launch (start us, length us, event | category | flops | bytes accessed | tf_op | source)
XLA Modules:
  0.0 103.9 jit_solution(15092344044466423308)
XLA Ops:
  0.6 3.3 %collective-permute-start = (bf16[8,8,256,128]{3,2,1,0:T(8,128)(2,1)}, bf16[8,8,256,128]{3,2,1,0:T(8,128)(2,1)}, u32[]{:S(2)}, u32[]{:S(2)}) collective-permute-start(bf16[8,8,256,128]{3,2,1,0:T(8,128)(2,1)} %ko.1), channel_id=1, source_target_pairs={{0,16},{16,0},{1,17},{17,1},{2,18},{18,2},{3,19},{19,3},{4,20},{20... | collective-permute-start | bytes 12582920 | tf_op jit(solution)/shard_map/ppermute | solution.py:35
  4.1 1.7 %broadcast_in_dim.11 = bf16[8,2,4,32,128]{4,3,2,1,0:T(8,128)(2,1)} broadcast(bf16[2,4,32,128]{3,2,1,0:T(8,128)(2,1)} %bitcast.45), dimensions={1,2,3,4} | broadcast | bytes 589824 | tf_op jit(solution)/shard_map/broadcast_in_dim | solution.py:273
  5.8 4.3 %all-to-all-start = ((bf16[16,4,32,128]{3,2,1,0:T(8,128)(2,1)}), bf16[16,4,32,128]{3,2,1,0:T(8,128)(2,1)S(1)}, u32[]{:S(2)}, u32[]{:S(2)}) async-start(bf16[16,4,32,128]{3,2,1,0:T(8,128)(2,1)} %bitcast.8), calls=%async_computation | async-start | bytes 1048576 | tf_op jit(solution)/shard_map/all_to_all | solution.py:283
  10.9 1.0 convert_bitcast_fusion.new_ref
  11.8 8.1 %all-to-all-done = bf16[16,4,32,128]{3,2,1,0:T(8,128)(2,1)S(1)} async-done(((bf16[16,4,32,128]{3,2,1,0:T(8,128)(2,1)}), bf16[16,4,32,128]{3,2,1,0:T(8,128)(2,1)S(1)}, u32[]{:S(2)}, u32[]{:S(2)}) %all-to-all-start) | async-done | bytes 524320 | tf_op jit(solution)/shard_map/all_to_all | solution.py:283
  20.0 7.2 %attend.1 = bf16[8,272,128]{2,1,0:T(8,128)(2,1)} custom-call(s32[11]{0:T(128)S(1)} %pad_add_fusion.1.meta, bf16[8,2,4,32,128]{4,3,2,1,0:T(8,128)(2,1)S(1)} %bitcast.35, bf16[8,8,256,128]{3,2,1,0:T(8,128)(2,1)} %ko.1, bf16[8,8,256,128]{3,2,1,0:T(8,128)(2,1)} %vo.1, bf16[8,8,256,128]{3,2,1,0:T(8,128)(2,1)} %collective-permute-done.ks, ...), custom_call_target="tpu_custom_call" | custom-call | flops 536870912 | bytes 8388608 | tf_op jit(solution)/shard_map/attend/pallas_call | solution.py:146
  27.2 3.5 %all-to-all-start.1 = ((bf16[8,272,128]{2,1,0:T(8,128)(2,1)}), bf16[8,272,128]{2,1,0:T(8,128)(2,1)S(1)}, u32[]{:S(2)}, u32[]{:S(2)}) async-start(bf16[8,272,128]{2,1,0:T(8,128)(2,1)} %attend.1), calls=%async_computation.1 | async-start | bytes 1114112 | tf_op jit(solution)/shard_map/all_to_all | solution.py:295
  30.7 1.0 collective-permute-start.12
  31.9 8.4 %all-to-all-done.1 = bf16[8,272,128]{2,1,0:T(8,128)(2,1)S(1)} async-done(((bf16[8,272,128]{2,1,0:T(8,128)(2,1)}), bf16[8,272,128]{2,1,0:T(8,128)(2,1)S(1)}, u32[]{:S(2)}, u32[]{:S(2)}) %all-to-all-start.1) | async-done | bytes 557088 | tf_op jit(solution)/shard_map/all_to_all | solution.py:295
  41.2 3.2 %collective-permute-start.3 = (bf16[2,16,1024]{2,1,0:T(8,128)(2,1)S(1)}, bf16[2,16,1024]{2,1,0:T(8,128)(2,1)S(1)}, u32[]{:S(2)}, u32[]{:S(2)}) collective-permute-start(bf16[2,16,1024]{2,1,0:T(8,128)(2,1)S(1)} %pad_maximum_fusion.2), channel_id=1, source_target_pairs={{0,4},{4,8},{8,12},{12,0},{1,5},{5,9},{9,13},{13,1},{2,6},{6,10},{... | collective-permute-start | bytes 196616 | tf_op jit(solution)/shard_map/ppermute | solution.py:31
  44.4 1.6 %collective-permute-start.4 = (bf16[2,16,1024]{2,1,0:T(8,128)(2,1)S(1)}, bf16[2,16,1024]{2,1,0:T(8,128)(2,1)S(1)}, u32[]{:S(2)}, u32[]{:S(2)}) collective-permute-start(bf16[2,16,1024]{2,1,0:T(8,128)(2,1)S(1)} %pad_maximum_fusion.2), channel_id=1, source_target_pairs={{0,12},{4,0},{8,4},{12,8},{1,13},{5,1},{9,5},{13,9},{2,14},{6,2},{... | collective-permute-start | bytes 196616 | tf_op jit(solution)/shard_map/ppermute | solution.py:31
  46.0 1.6 %collective-permute-done.3 = bf16[2,16,1024]{2,1,0:T(8,128)(2,1)S(1)} collective-permute-done((bf16[2,16,1024]{2,1,0:T(8,128)(2,1)S(1)}, bf16[2,16,1024]{2,1,0:T(8,128)(2,1)S(1)}, u32[]{:S(2)}, u32[]{:S(2)}) %collective-permute-start.3) | collective-permute-done | bytes 65568 | tf_op jit(solution)/shard_map/ppermute | solution.py:31
  47.6 4.6 %collective-permute-start.5 = (bf16[2,16,1024]{2,1,0:T(8,128)(2,1)S(1)}, bf16[2,16,1024]{2,1,0:T(8,128)(2,1)S(1)}, u32[]{:S(2)}, u32[]{:S(2)}) collective-permute-start(bf16[2,16,1024]{2,1,0:T(8,128)(2,1)S(1)} %pad_maximum_fusion.2), channel_id=1, source_target_pairs={{0,8},{4,12},{8,0},{12,4},{1,9},{5,13},{9,1},{13,5},{2,10},{6,14},... | collective-permute-start | bytes 196616 | tf_op jit(solution)/shard_map/ppermute | solution.py:31
  52.2 2.6 %collective-permute-start.10 = (bf16[2,2,16,1024]{3,2,1,0:T(8,128)(2,1)S(1)}, bf16[2,2,16,1024]{3,2,1,0:T(8,128)(2,1)S(1)}, u32[]{:S(2)}, u32[]{:S(2)}) collective-permute-start(bf16[2,2,16,1024]{3,2,1,0:T(8,128)(2,1)S(1)} %pad_maximum_fusion.refs_0_), channel_id=1, source_target_pairs={{0,2},{1,3},{2,0},{3,1},{4,6},{5,7},{6,4},{7,5},{8,10},{9,11},{10,... | collective-permute-start | bytes 393224 | tf_op jit(solution)/shard_map/ppermute | solution.py:31
  55.3 2.2 %collective-permute-start.8 = (bf16[2,2,16,1024]{3,2,1,0:T(8,128)(2,1)S(1)}, bf16[2,2,16,1024]{3,2,1,0:T(8,128)(2,1)S(1)}, u32[]{:S(2)}, u32[]{:S(2)}) collective-permute-start(bf16[2,2,16,1024]{3,2,1,0:T(8,128)(2,1)S(1)} %pad_maximum_fusion.refs_0_), channel_id=1, source_target_pairs={{0,3},{1,0},{2,1},{3,2},{4,7},{5,4},{6,5},{7,6},{8,11},{9,8},{10,9... | collective-permute-start | bytes 393224 | tf_op jit(solution)/shard_map/ppermute | solution.py:31
  58.0 0.9 collective-permute-start.7
  58.9 1.8 %collective-permute-start.9 = (bf16[2,2,16,1024]{3,2,1,0:T(8,128)(2,1)S(1)}, bf16[2,2,16,1024]{3,2,1,0:T(8,128)(2,1)S(1)}, u32[]{:S(2)}, u32[]{:S(2)}) collective-permute-start(bf16[2,2,16,1024]{3,2,1,0:T(8,128)(2,1)S(1)} %pad_maximum_fusion.1.refs_1_), channel_id=1, source_target_pairs={{0,3},{1,0},{2,1},{3,2},{4,7},{5,4},{6,5},{7,6},{8,11},{9,8},{10,9... | collective-permute-start | bytes 393224 | tf_op jit(solution)/shard_map/ppermute | solution.py:31
  60.8 1.0 collective-permute-done.8.refs_4_
  61.8 1.9 %collective-permute-done.11.refs_7_ = bf16[2,2,16,1024]{3,2,1,0:T(8,128)(2,1)S(1)} collective-permute-done((bf16[2,2,16,1024]{3,2,1,0:T(8,128)(2,1)S(1)}, bf16[2,2,16,1024]{3,2,1,0:T(8,128)(2,1)S(1)}, u32[]{:S(2)}, u32[]{:S(2)}) %collective-permute-start.11) | collective-permute-done | bytes 131104 | tf_op jit(solution)/shard_map/ppermute | solution.py:31
  63.8 2.1 %collective-permute-done.7.refs_3_ = bf16[2,2,16,1024]{3,2,1,0:T(8,128)(2,1)S(1)} collective-permute-done((bf16[2,2,16,1024]{3,2,1,0:T(8,128)(2,1)S(1)}, bf16[2,2,16,1024]{3,2,1,0:T(8,128)(2,1)S(1)}, u32[]{:S(2)}, u32[]{:S(2)}) %collective-permute-start.7) | collective-permute-done | bytes 131104 | tf_op jit(solution)/shard_map/ppermute | solution.py:31
  65.9 3.8 %project.1 = (bf16[256,1152]{1,0:T(8,128)(2,1)}, bf16[256,1024]{1,0:T(8,128)(2,1)}, bf16[256,1024]{1,0:T(8,128)(2,1)}) custom-call(s32[2]{0:T(128)S(1)} %pad_add_fusion.place, bf16[2,2,16,1024]{3,2,1,0:T(8,128)(2,1)S(1)} %pad_maximum_fusion.refs_0_, bf16[2,2,16,1024]{3,2,1,0:T(8,128)(2,1)S(1)} %pad_maximum_fusion.1.refs_1_, ...), custom_call_target="tpu_custom_call" | custom-call | flops 1073741824 | bytes 4194304 | tf_op jit(solution)/shard_map/project/pallas_call | solution.py:229
  69.7 5.5 %all-to-all-start.2 = ((bf16[8,32,1152]{2,1,0:T(8,128)(2,1)}), bf16[8,32,1152]{2,1,0:T(8,128)(2,1)S(1)}, u32[]{:S(2)}, u32[]{:S(2)}) async-start(bf16[8,32,1152]{2,1,0:T(8,128)(2,1)} %bitcast.40), calls=%async_computation.2 | async-start | bytes 1179648 | tf_op jit(solution)/shard_map/all_to_all | solution.py:324
  75.2 2.4 %collective-permute-start.13 = (bf16[16,1024]{1,0:T(8,128)(2,1)S(1)}, bf16[16,1024]{1,0:T(8,128)(2,1)S(1)}, u32[]{:S(2)}, u32[]{:S(2)}) collective-permute-start(bf16[16,1024]{1,0:T(8,128)(2,1)S(1)} %constant_dynamic-slice_fusion), channel_id=1, source_target_pairs={{0,16},{16,0},{1,17},{17,1},{2,18},{18,2},{3,19},{19,3},{4,20},{20... | collective-permute-start | bytes 98312 | tf_op jit(solution)/shard_map/ppermute | solution.py:35
  77.6 0.9 collective-permute-done.13
  78.5 5.4 %all-to-all-done.2 = bf16[8,32,1152]{2,1,0:T(8,128)(2,1)S(1)} async-done(((bf16[8,32,1152]{2,1,0:T(8,128)(2,1)}), bf16[8,32,1152]{2,1,0:T(8,128)(2,1)S(1)}, u32[]{:S(2)}, u32[]{:S(2)}) %all-to-all-start.2) | async-done | bytes 589856 | tf_op jit(solution)/shard_map/all_to_all | solution.py:324
  84.1 0.9 broadcast_in_dim.14
  85.0 3.5 %all-to-all-start.3 = ((bf16[8,32,1024]{2,1,0:T(8,128)(2,1)}), bf16[8,32,1024]{2,1,0:T(8,128)(2,1)S(1)}, u32[]{:S(2)}, u32[]{:S(2)}) async-start(bf16[8,32,1024]{2,1,0:T(8,128)(2,1)} %broadcast_in_dim.14), calls=%async_computation.3 | async-start | bytes 1048576 | tf_op jit(solution)/shard_map/all_to_all | solution.py:18
  88.5 3.2 %collective-permute-start.14 = (bf16[16,1024]{1,0:T(8,128)(2,1)S(1)}, bf16[16,1024]{1,0:T(8,128)(2,1)S(1)}, u32[]{:S(2)}, u32[]{:S(2)}) collective-permute-start(bf16[16,1024]{1,0:T(8,128)(2,1)S(1)} %broadcast_select_fusion.3), channel_id=1, source_target_pairs={{0,16},{16,0},{1,17},{17,1},{2,18},{18,2},{3,19},{19,3},{4,20},{20... | collective-permute-start | bytes 98312 | tf_op jit(solution)/shard_map/ppermute | solution.py:35
  93.2 2.8 %all-to-all-done.3 = bf16[8,32,1024]{2,1,0:T(8,128)(2,1)S(1)} async-done(((bf16[8,32,1024]{2,1,0:T(8,128)(2,1)}), bf16[8,32,1024]{2,1,0:T(8,128)(2,1)S(1)}, u32[]{:S(2)}, u32[]{:S(2)}) %all-to-all-start.3) | async-done | bytes 524320 | tf_op jit(solution)/shard_map/all_to_all | solution.py:18
  96.0 4.3 %collective-permute-start.16 = (bf16[256,1024]{1,0:T(8,128)(2,1)S(1)}, bf16[256,1024]{1,0:T(8,128)(2,1)S(1)}, u32[]{:S(2)}, u32[]{:S(2)}) collective-permute-start(bf16[256,1024]{1,0:T(8,128)(2,1)S(1)} %bitcast.38), channel_id=1, source_target_pairs={{0,16},{16,0},{1,17},{17,1},{2,18},{18,2},{3,19},{19,3},{4,20},{20... | collective-permute-start | bytes 1572872 | tf_op jit(solution)/shard_map/ppermute | solution.py:35
  101.0 0.8 collective-permute-done.16
  101.8 2.1 %add_convert_fusion = bf16[1024,1024]{1,0:T(8,128)(2,1)} fusion(f32[1024,1024]{1,0:T(8,128)S(1)} %fusion.1, bf16[256,1024]{1,0:T(8,128)(2,1)S(1)} %collective-permute-done.15, bf16[256,1024]{1,0:T(8,128)(2,1)S(1)} %collective-permute-done.16), kind=kOutput, calls=%fused_computation | convolution fusion | flops 538968064 | bytes 7340032 | tf_op jit(solution)/shard_map/dot_general | solution.py:344
  (56 shorter events, 5.5 us)
Async XLA Ops:
  0.6 19.3 %collective-permute-start = (bf16[8,8,256,128]{3,2,1,0:T(8,128)(2,1)}, bf16[8,8,256,128]{3,2,1,0:T(8,128)(2,1)}, u32[]{:S(2)}, u32[]{:S(2)}) collective-permute-start(bf16[8,8,256,128]{3,2,1,0:T(8,128)(2,1)} %ko.1), channel_id=1, source_target_pairs={{0,16},{16,0},{1,17},{17,1},{2,18},{18,2},{3,19},{19,3},{4,20},{20... | collective-permute-start | bytes 12582920 | tf_op jit(solution)/shard_map/ppermute | solution.py:35
  4.0 16.0 %collective-permute-start.1 = (bf16[8,8,256,128]{3,2,1,0:T(8,128)(2,1)}, bf16[8,8,256,128]{3,2,1,0:T(8,128)(2,1)}, u32[]{:S(2)}, u32[]{:S(2)}) collective-permute-start(bf16[8,8,256,128]{3,2,1,0:T(8,128)(2,1)} %vo.1), channel_id=1, source_target_pairs={{0,16},{16,0},{1,17},{17,1},{2,18},{18,2},{3,19},{19,3},{4,20},{20... | collective-permute-start | bytes 12582920 | tf_op jit(solution)/shard_map/ppermute | solution.py:35
  5.8 14.1 %all-to-all-start = ((bf16[16,4,32,128]{3,2,1,0:T(8,128)(2,1)}), bf16[16,4,32,128]{3,2,1,0:T(8,128)(2,1)S(1)}, u32[]{:S(2)}, u32[]{:S(2)}) async-start(bf16[16,4,32,128]{3,2,1,0:T(8,128)(2,1)} %bitcast.8), calls=%async_computation | async-start | bytes 1048576 | tf_op jit(solution)/shard_map/all_to_all | solution.py:283
  19.9 10.8 %copy-start = (bf16[1024,1024]{1,0:T(8,128)(2,1)S(1)}, bf16[1024,1024]{1,0:T(8,128)(2,1)}, u32[]{:S(2)}) copy-start(bf16[1024,1024]{1,0:T(8,128)(2,1)} %refs_10_.1) | copy-start | bytes 6291460
  19.9 11.8 %copy-start.1 = (f32[1024]{0:T(1024)S(1)}, f32[1024]{0:T(1024)}, u32[]{:S(2)}) copy-start(f32[1024]{0:T(1024)} %param.15) | copy-start | bytes 12292
  27.2 13.1 %all-to-all-start.1 = ((bf16[8,272,128]{2,1,0:T(8,128)(2,1)}), bf16[8,272,128]{2,1,0:T(8,128)(2,1)S(1)}, u32[]{:S(2)}, u32[]{:S(2)}) async-start(bf16[8,272,128]{2,1,0:T(8,128)(2,1)} %attend.1), calls=%async_computation.1 | async-start | bytes 1114112 | tf_op jit(solution)/shard_map/all_to_all | solution.py:295
  30.7 27.3 %collective-permute-start.12 = (bf16[1024,1024]{1,0:T(8,128)(2,1)S(1)}, bf16[1024,1024]{1,0:T(8,128)(2,1)}, u32[]{:S(2)}, u32[]{:S(2)}) collective-permute-start(bf16[1024,1024]{1,0:T(8,128)(2,1)S(1)} %copy-done), channel_id=1, source_target_pairs={{0,16},{16,0},{1,17},{17,1},{2,18},{18,2},{3,19},{19,3},{4,20},{20... | collective-permute-start | bytes 6291464 | tf_op jit(solution)/shard_map/ppermute | solution.py:35
  31.7 9.4 %collective-permute-start.2 = (f32[1024]{0:T(1024)S(1)}, f32[1024]{0:T(1024)S(1)}, u32[]{:S(2)}, u32[]{:S(2)}) collective-permute-start(f32[1024]{0:T(1024)S(1)} %copy-done.1), channel_id=1, source_target_pairs={{0,16},{16,0},{1,17},{17,1},{2,18},{18,2},{3,19},{19,3},{4,20},{20... | collective-permute-start | bytes 12296 | tf_op jit(solution)/shard_map/ppermute | solution.py:35
  41.0 34.3 %copy-start.3 = (bf16[32,1024]{1,0:T(8,128)(2,1)S(1)}, bf16[32,1024]{1,0:T(8,128)(2,1)}, u32[]{:S(2)}) copy-start(bf16[32,1024]{1,0:T(8,128)(2,1)} %param.17) | copy-start | bytes 196612
  41.2 6.4 %collective-permute-start.3 = (bf16[2,16,1024]{2,1,0:T(8,128)(2,1)S(1)}, bf16[2,16,1024]{2,1,0:T(8,128)(2,1)S(1)}, u32[]{:S(2)}, u32[]{:S(2)}) collective-permute-start(bf16[2,16,1024]{2,1,0:T(8,128)(2,1)S(1)} %pad_maximum_fusion.2), channel_id=1, source_target_pairs={{0,4},{4,8},{8,12},{12,0},{1,5},{5,9},{9,13},{13,1},{2,6},{6,10},{... | collective-permute-start | bytes 196616 | tf_op jit(solution)/shard_map/ppermute | solution.py:31
  44.4 7.8 %collective-permute-start.4 = (bf16[2,16,1024]{2,1,0:T(8,128)(2,1)S(1)}, bf16[2,16,1024]{2,1,0:T(8,128)(2,1)S(1)}, u32[]{:S(2)}, u32[]{:S(2)}) collective-permute-start(bf16[2,16,1024]{2,1,0:T(8,128)(2,1)S(1)} %pad_maximum_fusion.2), channel_id=1, source_target_pairs={{0,12},{4,0},{8,4},{12,8},{1,13},{5,1},{9,5},{13,9},{2,14},{6,2},{... | collective-permute-start | bytes 196616 | tf_op jit(solution)/shard_map/ppermute | solution.py:31
  47.6 9.9 %collective-permute-start.5 = (bf16[2,16,1024]{2,1,0:T(8,128)(2,1)S(1)}, bf16[2,16,1024]{2,1,0:T(8,128)(2,1)S(1)}, u32[]{:S(2)}, u32[]{:S(2)}) collective-permute-start(bf16[2,16,1024]{2,1,0:T(8,128)(2,1)S(1)} %pad_maximum_fusion.2), channel_id=1, source_target_pairs={{0,8},{4,12},{8,0},{12,4},{1,9},{5,13},{9,1},{13,5},{2,10},{6,14},... | collective-permute-start | bytes 196616 | tf_op jit(solution)/shard_map/ppermute | solution.py:31
  52.2 6.6 %collective-permute-start.10 = (bf16[2,2,16,1024]{3,2,1,0:T(8,128)(2,1)S(1)}, bf16[2,2,16,1024]{3,2,1,0:T(8,128)(2,1)S(1)}, u32[]{:S(2)}, u32[]{:S(2)}) collective-permute-start(bf16[2,2,16,1024]{3,2,1,0:T(8,128)(2,1)S(1)} %pad_maximum_fusion.refs_0_), channel_id=1, source_target_pairs={{0,2},{1,3},{2,0},{3,1},{4,6},{5,7},{6,4},{7,5},{8,10},{9,11},{10,... | collective-permute-start | bytes 393224 | tf_op jit(solution)/shard_map/ppermute | solution.py:31
  54.9 5.9 %collective-permute-start.6 = (bf16[2,2,16,1024]{3,2,1,0:T(8,128)(2,1)S(1)}, bf16[2,2,16,1024]{3,2,1,0:T(8,128)(2,1)S(1)}, u32[]{:S(2)}, u32[]{:S(2)}) collective-permute-start(bf16[2,2,16,1024]{3,2,1,0:T(8,128)(2,1)S(1)} %pad_maximum_fusion.refs_0_), channel_id=1, source_target_pairs={{0,1},{1,2},{2,3},{3,0},{4,5},{5,6},{6,7},{7,4},{8,9},{9,10},{10,1... | collective-permute-start | bytes 393224 | tf_op jit(solution)/shard_map/ppermute | solution.py:31
  55.3 6.5 %collective-permute-start.8 = (bf16[2,2,16,1024]{3,2,1,0:T(8,128)(2,1)S(1)}, bf16[2,2,16,1024]{3,2,1,0:T(8,128)(2,1)S(1)}, u32[]{:S(2)}, u32[]{:S(2)}) collective-permute-start(bf16[2,2,16,1024]{3,2,1,0:T(8,128)(2,1)S(1)} %pad_maximum_fusion.refs_0_), channel_id=1, source_target_pairs={{0,3},{1,0},{2,1},{3,2},{4,7},{5,4},{6,5},{7,6},{8,11},{9,8},{10,9... | collective-permute-start | bytes 393224 | tf_op jit(solution)/shard_map/ppermute | solution.py:31
  57.6 6.2 %collective-permute-start.11 = (bf16[2,2,16,1024]{3,2,1,0:T(8,128)(2,1)S(1)}, bf16[2,2,16,1024]{3,2,1,0:T(8,128)(2,1)S(1)}, u32[]{:S(2)}, u32[]{:S(2)}) collective-permute-start(bf16[2,2,16,1024]{3,2,1,0:T(8,128)(2,1)S(1)} %pad_maximum_fusion.1.refs_1_), channel_id=1, source_target_pairs={{0,2},{1,3},{2,0},{3,1},{4,6},{5,7},{6,4},{7,5},{8,10},{9,11},{10,... | collective-permute-start | bytes 393224 | tf_op jit(solution)/shard_map/ppermute | solution.py:31
  58.0 7.8 %collective-permute-start.7 = (bf16[2,2,16,1024]{3,2,1,0:T(8,128)(2,1)S(1)}, bf16[2,2,16,1024]{3,2,1,0:T(8,128)(2,1)S(1)}, u32[]{:S(2)}, u32[]{:S(2)}) collective-permute-start(bf16[2,2,16,1024]{3,2,1,0:T(8,128)(2,1)S(1)} %pad_maximum_fusion.1.refs_1_), channel_id=1, source_target_pairs={{0,1},{1,2},{2,3},{3,0},{4,5},{5,6},{6,7},{7,4},{8,9},{9,10},{10,1... | collective-permute-start | bytes 393224 | tf_op jit(solution)/shard_map/ppermute | solution.py:31
  58.9 7.0 %collective-permute-start.9 = (bf16[2,2,16,1024]{3,2,1,0:T(8,128)(2,1)S(1)}, bf16[2,2,16,1024]{3,2,1,0:T(8,128)(2,1)S(1)}, u32[]{:S(2)}, u32[]{:S(2)}) collective-permute-start(bf16[2,2,16,1024]{3,2,1,0:T(8,128)(2,1)S(1)} %pad_maximum_fusion.1.refs_1_), channel_id=1, source_target_pairs={{0,3},{1,0},{2,1},{3,2},{4,7},{5,4},{6,5},{7,6},{8,11},{9,8},{10,9... | collective-permute-start | bytes 393224 | tf_op jit(solution)/shard_map/ppermute | solution.py:31
  69.6 22.1 %copy-start.4 = (bf16[256,1024]{1,0:T(8,128)(2,1)S(1)}, bf16[256,1024]{1,0:T(8,128)(2,1)}, u32[]{:S(2)}) copy-start(bf16[256,1024]{1,0:T(8,128)(2,1)} %get-tuple-element.11) | copy-start | bytes 1572868
  69.7 30.6 %copy-start.2 = (bf16[256,1024]{1,0:T(8,128)(2,1)S(1)}, bf16[256,1024]{1,0:T(8,128)(2,1)}, u32[]{:S(2)}) copy-start(bf16[256,1024]{1,0:T(8,128)(2,1)} %get-tuple-element.13) | copy-start | bytes 1572868
  69.7 14.2 %all-to-all-start.2 = ((bf16[8,32,1152]{2,1,0:T(8,128)(2,1)}), bf16[8,32,1152]{2,1,0:T(8,128)(2,1)S(1)}, u32[]{:S(2)}, u32[]{:S(2)}) async-start(bf16[8,32,1152]{2,1,0:T(8,128)(2,1)} %bitcast.40), calls=%async_computation.2 | async-start | bytes 1179648 | tf_op jit(solution)/shard_map/all_to_all | solution.py:324
  75.2 3.2 %collective-permute-start.13 = (bf16[16,1024]{1,0:T(8,128)(2,1)S(1)}, bf16[16,1024]{1,0:T(8,128)(2,1)S(1)}, u32[]{:S(2)}, u32[]{:S(2)}) collective-permute-start(bf16[16,1024]{1,0:T(8,128)(2,1)S(1)} %constant_dynamic-slice_fusion), channel_id=1, source_target_pairs={{0,16},{16,0},{1,17},{17,1},{2,18},{18,2},{3,19},{19,3},{4,20},{20... | collective-permute-start | bytes 98312 | tf_op jit(solution)/shard_map/ppermute | solution.py:35
  85.0 11.0 %all-to-all-start.3 = ((bf16[8,32,1024]{2,1,0:T(8,128)(2,1)}), bf16[8,32,1024]{2,1,0:T(8,128)(2,1)S(1)}, u32[]{:S(2)}, u32[]{:S(2)}) async-start(bf16[8,32,1024]{2,1,0:T(8,128)(2,1)} %broadcast_in_dim.14), calls=%async_computation.3 | async-start | bytes 1048576 | tf_op jit(solution)/shard_map/all_to_all | solution.py:18
  88.5 4.1 %collective-permute-start.14 = (bf16[16,1024]{1,0:T(8,128)(2,1)S(1)}, bf16[16,1024]{1,0:T(8,128)(2,1)S(1)}, u32[]{:S(2)}, u32[]{:S(2)}) collective-permute-start(bf16[16,1024]{1,0:T(8,128)(2,1)S(1)} %broadcast_select_fusion.3), channel_id=1, source_target_pairs={{0,16},{16,0},{1,17},{17,1},{2,18},{18,2},{3,19},{19,3},{4,20},{20... | collective-permute-start | bytes 98312 | tf_op jit(solution)/shard_map/ppermute | solution.py:35
  91.7 9.3 %collective-permute-start.15 = (bf16[256,1024]{1,0:T(8,128)(2,1)S(1)}, bf16[256,1024]{1,0:T(8,128)(2,1)S(1)}, u32[]{:S(2)}, u32[]{:S(2)}) collective-permute-start(bf16[256,1024]{1,0:T(8,128)(2,1)S(1)} %copy-done.4), channel_id=1, source_target_pairs={{0,16},{16,0},{1,17},{17,1},{2,18},{18,2},{3,19},{19,3},{4,20},{20... | collective-permute-start | bytes 1572872 | tf_op jit(solution)/shard_map/ppermute | solution.py:35
  96.0 5.8 %collective-permute-start.16 = (bf16[256,1024]{1,0:T(8,128)(2,1)S(1)}, bf16[256,1024]{1,0:T(8,128)(2,1)S(1)}, u32[]{:S(2)}, u32[]{:S(2)}) collective-permute-start(bf16[256,1024]{1,0:T(8,128)(2,1)S(1)} %bitcast.38), channel_id=1, source_target_pairs={{0,16},{16,0},{1,17},{17,1},{2,18},{18,2},{3,19},{19,3},{4,20},{20... | collective-permute-start | bytes 1572872 | tf_op jit(solution)/shard_map/ppermute | solution.py:35
